TPU v7x, 32 devices: a whole 2x2x4 slice. The times are simulated.
32 devices in a mesh: groups: 2 (over x), rows: 16 (over z, y, core).
Axes of the slice: x: 2, y: 2, z: 4, core: 2. Of those that a mesh axis runs over, the one named last changes fastest.
Arguments:
- queries: bfloat16 [64, 4096], P(('groups', 'rows')), parts along dimension 0, may hold values from -128 to 128
- new_keys: bfloat16 [64, 4096], P(('groups', 'rows')), parts along dimension 0, may hold values from -4 to 4
- new_values: bfloat16 [64, 4096], P(('groups', 'rows')), parts along dimension 0, may hold values from -5 to 5
- cache_keys: bfloat16 [64, 64, 4096], P(('groups', 'rows')), parts along dimension 0, may hold values from -4 to 4
- cache_values: bfloat16 [64, 64, 4096], P(('groups', 'rows')), parts along dimension 0, may hold values from -5 to 5
- cache_lengths: int32 [64], P(('groups', 'rows')), parts along dimension 0, may hold values from 1 to 64, as said below
- out_weight: bfloat16 [4096, 4096], P('rows'), may hold values from -0.09375 to 0.09375
- codes: int32 [64, 768], P(('groups', 'rows')), parts along dimension 0, may hold values from 0 to 1073741823
- tile_slot: int32 [64], P(('groups', 'rows')), parts along dimension 0, may hold values from -1 to 3, as said below
- code_weight: float32 [5, 512], replicated, may hold values from -2.5 to 2.5
- conv_one: bfloat16 [3, 3, 512, 512], replicated, may hold values from -0.09375 to 0.09375
- conv_two: bfloat16 [3, 3, 512, 512], replicated, may hold values from -0.09375 to 0.09375
Outputs:
- mixed: bfloat16 [64, 4096], P(('groups', 'rows')), parts along dimension 0
- decoded: bfloat16 [256, 48, 512], P(('groups', 'rows')), parts along dimension 0
There are 2 independent parts, one for each index of `groups`. A program takes and returns all parts, laid end to end along the dimension named above; an argument that names none is the same for every part. Nothing has to cross between parts.
Inputs may be any that keep to these rules, and one draw needn't show every extreme that they name: `cache_lengths`: some row's length is exactly 64. `tile_slot`: each slot 0 to 3 belongs to exactly one row; all other rows hold -1.
All inputs are finite; a program needn't handle non-finite values.
Results may differ from a plain program's by a relative error of at most 0.0075.
Values may be sent and summed in bfloat16 or wider, within the bound.
No kernel may reach another device: no remote copies, remote signals or barrier semaphores. Data moves between devices by JAX's collectives and lax.ppermute only.
A program may use at most 64 MiB of HBM per device.

v0:
```python
import functools
import math

import jax
import jax.numpy as jnp
from jax import lax
from jax.experimental import pallas as pl
from jax.experimental.pallas import tpu as pltpu
from jax.sharding import PartitionSpec as P

HEAD_DIM = 128
FSQ_DIMS = 5
IMG_SPLIT = 4
TILE_H = 8
IMG_W = 48
LANES = 128
HALO = 2
ROW_WORDS = IMG_W // 2
TILE_ROWS = TILE_H + 2 * HALO
WINDOW = 3
PIECES = 2
CODE_ROWS = WINDOW * PIECES
TAP_ROWS = 24
FOLD_ROWS = 256
VMEM_LIMIT = 24 * 1024 * 1024


def window_start(section):
    return (TILE_H * ROW_WORDS * section - HALO * ROW_WORDS) // LANES


def member(at, tiles):
    return (at + tiles // 4 * 2) % tiles


def message_rows(features):
    return -(-(features + CODE_ROWS) // 16) * 16


def encode(code):
    fraction = (code & 127).astype(jnp.float32) * (1.0 / 128.0) + 1.0
    for bit in range(7):
        up = ((code >> (7 + bit)) & 1) == 1
        fraction = jnp.where(up, fraction * 2.0 ** (1 << bit), fraction)
        if bit == 5:
            fraction = fraction * 2.0**-64
    return jnp.where(((code >> 14) & 1) == 1, -fraction, fraction)


def decode_number(value):
    size = jnp.abs(value)
    code = jnp.where(value < 0.0, 1 << 14, 0)
    for bit in range(6, -1, -1):
        step = 1 << bit
        up = size >= 2.0 ** (step - 64)
        code = code + jnp.where(up, step << 7, 0)
        size = jnp.where(up, size * 2.0**-step, size)
    return code + ((size * 2.0**64 - 1.0) * 128.0).astype(jnp.int32)


def attend_kernel(
    lengths,
    slots,
    parity_ref,
    q_any,
    nk_any,
    nv_any,
    k_any,
    v_any,
    codes_any,
    weight_any,
    out_ref,
    give_ref,
    q_ref,
    nk_ref,
    nv_ref,
    k_ref,
    v_ref,
    codes_ref,
    msg,
    sems,
    *,
    tiles,
    per,
    feature_rows,
):
    rows, width = q_ref.shape
    give_columns = give_ref.shape[1]
    small = [
        pltpu.make_async_copy(source, target, sems.at[at])
        for at, (source, target) in enumerate(
            ((q_any, q_ref), (nk_any, nk_ref), (nv_any, nv_ref), (codes_any, codes_ref))
        )
    ]
    keys = [pltpu.make_async_copy(k_any.at[r], k_ref.at[r], sems.at[4 + r]) for r in range(rows)]
    values = [
        pltpu.make_async_copy(v_any.at[r], v_ref.at[r], sems.at[4 + rows + r]) for r in range(rows)
    ]
    begin = pl.multiple_of((1 - parity_ref[0]) * give_columns, LANES)
    give = pltpu.make_async_copy(
        weight_any.at[:, pl.ds(begin, give_columns)], give_ref, sems.at[4 + 2 * rows]
    )
    for copy in small:
        copy.start()
    for r in range(rows):
        keys[r].start()
        values[r].start()
    give.start()

    heads = width // HEAD_DIM
    factor = 1.0 / math.sqrt(HEAD_DIM)
    same = (
        lax.broadcasted_iota(jnp.int32, (heads, width), 1) // HEAD_DIM
        == lax.broadcasted_iota(jnp.int32, (heads, width), 0)
    )
    msg[...] = jnp.zeros_like(msg)
    for copy in small:
        copy.wait()

    words = codes_ref[...]
    blocks = words.shape[1] // LANES
    pieces = [encode(words & 32767), encode(words >> 15)]
    for tile in range(tiles):
        number = (member(tile, tiles) + IMG_SPLIT // 2) % tiles
        start = window_start(number % IMG_SPLIT)
        gains = [
            jnp.where(slots[r] == number // IMG_SPLIT, 1.0, 0.0).astype(jnp.float32)
            for r in range(rows)
        ]
        for at, piece in enumerate(pieces):
            for step in range(WINDOW):
                block = start + step
                if block < 0 or block >= blocks:
                    continue
                part = piece[:, block * LANES : (block + 1) * LANES]
                total = part[0:1] * gains[0]
                for r in range(1, rows):
                    total = total + part[r : r + 1] * gains[r]
                place = feature_rows + at * WINDOW + step
                msg[tile, place : place + 1, :] = total

    queries = q_ref[...].astype(jnp.float32)
    new_keys = nk_ref[...].astype(jnp.float32)
    new_values = nv_ref[...].astype(jnp.float32)
    for r in range(rows):
        query, new_key, new_value = (x[r : r + 1] for x in (queries, new_keys, new_values))
        spread = jnp.where(same, query, 0.0).astype(jnp.bfloat16)
        own_score = jnp.sum(jnp.where(same, query * new_key, 0.0), 1, keepdims=True) * factor
        keys[r].wait()
        scores = (
            lax.dot_general(
                spread, k_ref[r], (((1,), (1,)), ((), ())), preferred_element_type=jnp.float32
            )
            * factor
        )
        live = lax.broadcasted_iota(jnp.int32, scores.shape, 1) < lengths[r]
        scores = jnp.where(live, scores, jnp.float32(-1e30))
        highest = jnp.maximum(jnp.max(scores, 1, keepdims=True), own_score)
        cache_exp = jnp.where(live, jnp.exp(scores - highest), 0.0)
        own_exp = jnp.exp(own_score - highest)
        denom = jnp.sum(cache_exp, 1, keepdims=True) + own_exp
        cache_weight = (cache_exp / denom).astype(jnp.bfloat16)
        own_weight = (own_exp / denom).astype(jnp.bfloat16).astype(jnp.float32)
        values[r].wait()
        mixed_in = jnp.dot(cache_weight, v_ref[r], preferred_element_type=jnp.float32)
        attended = jnp.sum(
            jnp.where(same, mixed_in + own_weight * new_value, 0.0), 0, keepdims=True
        )
        for tile in range(tiles):
            for step in range(per):
                begin = (member(tile, tiles) // 2 * per + step) * LANES
                place = r * per + step
                msg[tile, place : place + 1, :] = attended[:, begin : begin + LANES]
    out_ref[...] = msg[...].astype(jnp.bfloat16)
    give.wait()


def project_kernel(parity_ref, in_ref, own_ref, other_ref, out_ref, held, total, *, rows, per):
    tiles, depth = in_ref.shape[:2]
    held[...] = in_ref[...].astype(jnp.float32).reshape(held.shape)
    groups = total.shape[0]
    lines = out_ref.shape[2] // rows
    share = own_ref.shape[0]
    lhs = []
    for row in range(rows):
        parts = [held[pl.ds(row * per + j, tiles, stride=depth), :] for j in range(per)]
        lhs.append(jnp.concatenate(parts, 1))
    lhs = jnp.concatenate(lhs, 0)
    even = parity_ref[0] == 0
    first, second = lhs[:, :share], lhs[:, share:]
    own = jnp.where(even, first, second).astype(jnp.bfloat16)
    other = jnp.where(even, second, first).astype(jnp.bfloat16)
    product = jnp.dot(own, own_ref[...], preferred_element_type=jnp.float32) + jnp.dot(
        other, other_ref[...], preferred_element_type=jnp.float32
    )
    for row in range(rows):
        for group in range(groups):
            for line in range(lines):
                begin = (group * lines + line) * LANES
                total[group, pl.ds(row * lines + line, tiles, stride=rows * lines), :] = product[
                    row * tiles : (row + 1) * tiles, begin : begin + LANES
                ]
    for group in range(groups):
        out_ref[:, group] = (
            total[group].astype(jnp.bfloat16).reshape(tiles, rows * lines, LANES)
        )


def total_kernel(in_ref, out_ref, held, *, rows):
    tiles, groups, depth, _ = in_ref.shape
    lines = depth // rows
    parts = in_ref[...].astype(jnp.float32).reshape(tiles // 2, 2 * groups, depth, LANES)
    held[...] = jnp.sum(parts, 0)
    for group in range(2 * groups):
        for line in range(lines):
            begin = (group * lines + line) * LANES
            out_ref[:, begin : begin + LANES] = held[
                group, pl.ds(line, rows, stride=lines), :
            ].astype(jnp.bfloat16)


def split_three(whole):
    high = whole.astype(jnp.bfloat16).astype(jnp.float32)
    middle = (whole - high).astype(jnp.bfloat16).astype(jnp.float32)
    return jnp.concatenate([high, middle, whole - high - middle], 0)


def fold_kernel(
    parity_ref, cw_ref, conv_ref, weight_ref, after_ref, out_ref, near_ref, levels_w, folded, held, sems, near_sem
):
    del after_ref
    taps = [(dr, dc) for dr in range(3) for dc in range(3)]
    copies = [
        pltpu.make_async_copy(conv_ref.at[dr, dc], held.at[at], sems.at[at])
        for at, (dr, dc) in enumerate(taps)
    ]
    for copy in copies:
        copy.start()
    begin = pl.multiple_of(parity_ref[0] * near_ref.shape[1], LANES)
    bring = pltpu.make_async_copy(
        weight_ref.at[:, pl.ds(begin, near_ref.shape[1])], near_ref, near_sem
    )
    bring.start()
    levels_w[...] = jnp.zeros_like(levels_w)
    levels_w[0:FSQ_DIMS, :] = cw_ref[...]
    left = split_three(levels_w[...]).astype(jnp.bfloat16)
    folded[...] = jnp.zeros_like(folded)
    for at, copy in enumerate(copies):
        copy.wait()
        parts = jnp.dot(left, held[at], preferred_element_type=jnp.float32)
        total = parts[0:8] + parts[8:16] + parts[16:24]
        folded[at * TAP_ROWS : (at + 1) * TAP_ROWS, :] = split_three(total)
    out_ref[...] = folded[...].astype(jnp.bfloat16)
    bring.wait()


def decode_kernel(section_ref, in_ref, fold_ref, two_ref, after_ref, out_ref, *, feature_rows):
    del after_ref
    section = section_ref[0]
    got = jnp.sum(in_ref[...].astype(jnp.float32), 0)
    pieces = []
    for at in range(PIECES):
        lines = [
            got[feature_rows + at * WINDOW + step : feature_rows + at * WINDOW + step + 1]
            for step in range(WINDOW)
        ]
        pieces.append(jnp.concatenate(lines, 1))
    codes = decode_number(jnp.concatenate(pieces, 1))
    span = codes.shape[1]
    depth = fold_ref.shape[0]
    level = lax.broadcasted_iota(jnp.int32, (8, span), 0)
    taken = level < FSQ_DIMS
    shift = jnp.where(taken, level * 3, 0)
    value = (2 * ((jnp.broadcast_to(codes, (8, span)) >> shift) & 7) - 7).astype(
        jnp.float32
    ) * 0.125
    value = jnp.where(taken, value, 0.0)
    value = jnp.concatenate([value] * (depth // 8), 0).astype(jnp.bfloat16)

    count = TILE_ROWS * IMG_W
    begin = TILE_H * ROW_WORDS * section - HALO * ROW_WORDS
    offset = begin & (LANES - 1)
    spot = lax.broadcasted_iota(jnp.int32, (count, 1), 0)
    line = spot // IMG_W + TILE_H * section - HALO
    inside = (line >= 0) & (line < IMG_SPLIT * TILE_H)
    target = jnp.where(inside, (spot >> 1) + offset + (span // 2) * (spot & 1), -1)
    chooser = jnp.where(
        lax.broadcasted_iota(jnp.int32, (count, span), 1) == target, 1.0, 0.0
    ).astype(jnp.bfloat16)
    placed = lax.dot_general(
        chooser, value, (((1,), (1,)), ((), ())), preferred_element_type=jnp.float32
    )
    column = spot % IMG_W
    moved = [
        jnp.where(column == 0, 0.0, pltpu.roll(placed, 1, 0)),
        placed,
        jnp.where(column == IMG_W - 1, 0.0, pltpu.roll(placed, count - 1, 0)),
    ]
    count = count - 2 * IMG_W
    tap_of = lax.broadcasted_iota(jnp.int32, (1, depth), 1) // TAP_ROWS
    taps = jnp.zeros((count, depth), jnp.float32)
    for dr in range(3):
        for dc in range(3):
            taps = jnp.where(
                tap_of == 3 * dr + dc, moved[dc][dr * IMG_W : dr * IMG_W + count], taps
            )
    hidden = jnp.dot(taps.astype(jnp.bfloat16), fold_ref[...], preferred_element_type=jnp.float32)

    line = lax.broadcasted_iota(jnp.int32, (count, 1), 0) // IMG_W + TILE_H * section - 1
    inside = (line >= 0) & (line < IMG_SPLIT * TILE_H)
    activated = jnp.where(inside, hidden * jax.nn.sigmoid(hidden), 0.0).astype(jnp.bfloat16)

    count = count - 2 * IMG_W
    column = lax.broadcasted_iota(jnp.int32, (count, 1), 0) % IMG_W
    summed = None
    for dc in (1, 0, 2):
        part = None
        for dr in range(3):
            term = jnp.dot(
                activated[dr * IMG_W : dr * IMG_W + count],
                two_ref[dr, dc],
                preferred_element_type=jnp.float32,
            )
            part = term if part is None else part + term
        if dc == 0:
            part = jnp.where(column == 0, 0.0, pltpu.roll(part, 1, 0))
        if dc == 2:
            part = jnp.where(column == IMG_W - 1, 0.0, pltpu.roll(part, count - 1, 0))
        summed = part if summed is None else summed + part
    out_ref[...] = summed.astype(jnp.bfloat16)


def near(array):
    return pltpu.with_memory_space_constraint(array, pltpu.VMEM)


def far(array):
    return pltpu.with_memory_space_constraint(array, pltpu.HBM)


def on_device(
    queries,
    new_keys,
    new_values,
    cache_keys,
    cache_values,
    cache_lengths,
    out_weight,
    codes,
    tile_slot,
    code_weight,
    conv_one,
    conv_two,
):
    tiles = lax.axis_size("rows")
    place = lax.axis_index("rows")
    rows, width = queries.shape
    channels = code_weight.shape[1]
    share = width // tiles
    per = 2 * share // LANES
    feature_rows = rows * per
    depth = message_rows(feature_rows)
    half = width // 2
    lines = 8
    groups = half // (lines * LANES)
    params = pltpu.CompilerParams(vmem_limit_bytes=VMEM_LIMIT)
    smem = pl.BlockSpec(memory_space=pltpu.SMEM)
    vmem = pl.BlockSpec(memory_space=pltpu.VMEM)
    anywhere = pl.BlockSpec(memory_space=pl.ANY)
    parity = (place % 2).reshape(1).astype(jnp.int32)

    outgoing, give = pl.pallas_call(
        functools.partial(attend_kernel, tiles=tiles, per=per, feature_rows=feature_rows),
        in_specs=[smem] * 3 + [anywhere] * 7,
        out_specs=[vmem, vmem],
        out_shape=[
            pltpu.VMEM((tiles, depth, LANES), jnp.bfloat16),
            pltpu.VMEM((share, half), out_weight.dtype),
        ],
        scratch_shapes=[
            pltpu.VMEM(queries.shape, queries.dtype),
            pltpu.VMEM(new_keys.shape, new_keys.dtype),
            pltpu.VMEM(new_values.shape, new_values.dtype),
            pltpu.VMEM(cache_keys.shape, cache_keys.dtype),
            pltpu.VMEM(cache_values.shape, cache_values.dtype),
            pltpu.VMEM(codes.shape, codes.dtype),
            pltpu.VMEM((tiles, depth, LANES), jnp.float32),
            pltpu.SemaphoreType.DMA((5 + 2 * rows,)),
        ],
        compiler_params=pltpu.CompilerParams(vmem_limit_bytes=56 * 1024 * 1024),
    )(
        cache_lengths,
        tile_slot,
        parity,
        far(queries),
        far(new_keys),
        far(new_values),
        far(cache_keys),
        far(cache_values),
        far(codes),
        far(out_weight),
    )
    order = [[member(at, tiles) for at in range(tiles)]]
    incoming = lax.all_to_all(
        outgoing, "rows", split_axis=0, concat_axis=0, axis_index_groups=order, tiled=True
    )
    other = lax.ppermute(give, "rows", [(i, i ^ 1) for i in range(tiles)])

    folded, own = pl.pallas_call(
        fold_kernel,
        in_specs=[smem, vmem, anywhere, anywhere, anywhere],
        out_specs=[vmem, vmem],
        out_shape=[
            jax.ShapeDtypeStruct((FOLD_ROWS, channels), jnp.bfloat16),
            pltpu.VMEM((share, half), out_weight.dtype),
        ],
        scratch_shapes=[
            pltpu.VMEM((8, channels), jnp.float32),
            pltpu.VMEM((FOLD_ROWS, channels), jnp.float32),
            pltpu.VMEM((9,) + conv_one.shape[2:], conv_one.dtype),
            pltpu.SemaphoreType.DMA((9,)),
            pltpu.SemaphoreType.DMA,
        ],
        compiler_params=params,
    )(parity, far(code_weight), far(conv_one), far(out_weight), near(outgoing))

    partials = pl.pallas_call(
        functools.partial(project_kernel, rows=rows, per=per),
        in_specs=[smem, vmem, vmem, vmem],
        out_shape=pltpu.VMEM((tiles, groups, rows * lines, LANES), jnp.bfloat16),
        scratch_shapes=[
            pltpu.VMEM((tiles * depth, LANES), jnp.float32),
            pltpu.VMEM((groups, tiles * rows * lines, LANES), jnp.float32),
        ],
        compiler_params=params,
    )(parity, near(incoming), near(own), near(other))
    gathered = lax.all_to_all(
        partials, "rows", split_axis=0, concat_axis=0, axis_index_groups=order, tiled=True
    )

    section = (place + IMG_SPLIT // 2) % tiles % IMG_SPLIT
    decoded = pl.pallas_call(
        functools.partial(decode_kernel, feature_rows=feature_rows),
        in_specs=[smem, vmem, vmem, vmem, anywhere],
        out_specs=vmem,
        out_shape=jax.ShapeDtypeStruct((TILE_H * IMG_W, channels), jnp.bfloat16),
        compiler_params=params,
    )(section.reshape(1).astype(jnp.int32), near(incoming), near(folded), near(conv_two), near(partials))

    mixed = pl.pallas_call(
        functools.partial(total_kernel, rows=rows),
        in_specs=[vmem],
        out_shape=jax.ShapeDtypeStruct((rows, width), jnp.bfloat16),
        scratch_shapes=[pltpu.VMEM((2 * groups, rows * lines, LANES), jnp.float32)],
        compiler_params=params,
    )(near(gathered))
    return (mixed, decoded.reshape(TILE_H, IMG_W, channels))


def solution(mesh):
    in_specs = (
        P(("groups", "rows"), None),
        P(("groups", "rows"), None),
        P(("groups", "rows"), None),
        P(("groups", "rows"), None, None),
        P(("groups", "rows"), None, None),
        P(("groups", "rows")),
        P("rows", None),
        P(("groups", "rows"), None),
        P(("groups", "rows")),
        P(),
        P(),
        P(),
    )
    out_specs = (P(("groups", "rows"), None), P(("groups", "rows"), None, None))
    return jax.shard_map(
        on_device, mesh=mesh, in_specs=in_specs, out_specs=out_specs, check_vma=False
    )
```

profile of v0, /device:TPU:0, one launch (start us, length us, event | category | flops | bytes accessed | tf_op | source)
XLA Modules:
  0.0 30.2 jit_solution(10011969206147204625)
XLA Ops:
  0.6 4.2 %shard_map.131 = (bf16[16,16,128]{2,1,0:T(8,128)(2,1)}, bf16[256,2048]{1,0:T(8,128)(2,1)S(1)}) custom-call(s32[2]{0:T(128)} %lengths.1, s32[2]{0:T(128)} %slots.1, s32[1]{0:T(128)} %bitcast.parity_ref, bf16[2,4096]{1,0:T(2,128)(2,1)} %q_any.1, bf16[2,4096]{1,0:T(2,128)(2,1)} %nk_any.1, bf16[2,4096]{1,0:T(2,128)(2,1)} %nv_any.1, bf16[2,64,4096]{2,1,0:T(8,128)(2,1)} %k_any.1, ...), custom_call_target="tpu_custom_call" | custom-call | tf_op jit(solution)/shard_map/pallas_call | solution.py:372
  4.8 0.5 %collective-permute-start = (bf16[256,2048]{1,0:T(8,128)(2,1)S(1)}, bf16[256,2048]{1,0:T(8,128)(2,1)S(1)}, u32[]{:S(2)}, u32[]{:S(2)}) collective-permute-start(bf16[256,2048]{1,0:T(8,128)(2,1)S(1)} %get-tuple-element.8), channel_id=1, source_target_pairs={{0,1},{1,0},{2,3},{3,2},{4,5},{5,4},{6,7},{7,6},{8,9},{9,8},{10,11... | collective-permute-start | bytes 3145736 | tf_op jit(solution)/shard_map/ppermute | solution.py:407
  5.3 7.5 %all-to-all-start = ((bf16[16,16,128]{2,1,0:T(8,128)(2,1)}), bf16[16,16,128]{2,1,0:T(8,128)(2,1)S(1)}, u32[]{:S(2)}, u32[]{:S(2)}) async-start(bf16[16,16,128]{2,1,0:T(8,128)(2,1)} %get-tuple-element.6.after_ref), calls=%async_computation | async-start | bytes 131072 | tf_op jit(solution)/shard_map/all_to_all | solution.py:404
  12.9 3.7 %shard_map.132 = (bf16[256,512]{1,0:T(8,128)(2,1)S(1)}, bf16[256,2048]{1,0:T(8,128)(2,1)S(1)}) custom-call(s32[1]{0:T(128)} %bitcast.parity_ref, f32[5,512]{1,0:T(8,128)} %cw_ref.1, bf16[3,3,512,512]{3,2,1,0:T(8,128)(2,1)} %conv_ref.1, bf16[256,4096]{1,0:T(8,128)(2,1)} %weight_ref.1, bf16[16,16,128]{2,1,0:T(8,128)(2,1)} %get-tuple-element.6.after_ref), custom_call_target="tpu_custom_call" | custom-call | tf_op jit(solution)/shard_map/pallas_call | solution.py:409
  16.6 0.9 %all-to-all-done.in_ref = bf16[16,16,128]{2,1,0:T(8,128)(2,1)S(1)} async-done(((bf16[16,16,128]{2,1,0:T(8,128)(2,1)}), bf16[16,16,128]{2,1,0:T(8,128)(2,1)S(1)}, u32[]{:S(2)}, u32[]{:S(2)}) %all-to-all-start) | async-done | bytes 65568 | tf_op jit(solution)/shard_map/all_to_all | solution.py:404
  17.5 0.0 collective-permute-done.other_ref
  17.5 1.1 %shard_map.133.after_ref = bf16[16,2,16,128]{3,2,1,0:T(8,128)(2,1)} custom-call(s32[1]{0:T(128)} %bitcast.parity_ref, bf16[16,16,128]{2,1,0:T(8,128)(2,1)S(1)} %all-to-all-done.in_ref, bf16[256,2048]{1,0:T(8,128)(2,1)S(1)} %get-tuple-element.7.own_ref, bf16[256,2048]{1,0:T(8,128)(2,1)S(1)} %collective-permute-done.other_ref), custom_call_target="tpu_custom_call" | custom-call | tf_op jit(solution)/shard_map/pallas_call | solution.py:427
  18.6 4.4 %all-to-all-start.1 = ((bf16[16,2,16,128]{3,2,1,0:T(8,128)(2,1)}), bf16[16,2,16,128]{3,2,1,0:T(8,128)(2,1)S(1)}, u32[]{:S(2)}, u32[]{:S(2)}) async-start(bf16[16,2,16,128]{3,2,1,0:T(8,128)(2,1)} %shard_map.133.after_ref), calls=%async_computation.1 | async-start | bytes 262144 | tf_op jit(solution)/shard_map/all_to_all | solution.py:437
  23.0 0.0 copy-start
  23.0 2.3 %copy-done = bf16[3,3,512,512]{3,2,1,0:T(8,128)(2,1)S(1)} copy-done((bf16[3,3,512,512]{3,2,1,0:T(8,128)(2,1)S(1)}, bf16[3,3,512,512]{3,2,1,0:T(8,128)(2,1)}, u32[]{:S(2)}) %copy-start) | copy-done | bytes 4718616
  25.3 4.3 %shard_map.135 = bf16[384,512]{1,0:T(8,128)(2,1)} custom-call(s32[1]{0:T(128)} %bitcast.1.section_ref, bf16[16,16,128]{2,1,0:T(8,128)(2,1)S(1)} %all-to-all-done.in_ref, bf16[256,512]{1,0:T(8,128)(2,1)S(1)} %get-tuple-element.9.fold_ref, bf16[3,3,512,512]{3,2,1,0:T(8,128)(2,1)S(1)} %copy-done, bf16[16,2,16,128]{3,2,1,0:T(8,128)(2,1)} %shard_map.133.after_ref), custom_call_target="tpu_custom_call" | custom-call | tf_op jit(solution)/shard_map/pallas_call | solution.py:442
  29.6 0.0 all-to-all-done.1.in_ref
  29.6 0.6 %shard_map.134 = bf16[2,4096]{1,0:T(2,128)(2,1)} custom-call(bf16[16,2,16,128]{3,2,1,0:T(8,128)(2,1)S(1)} %all-to-all-done.1.in_ref), custom_call_target="tpu_custom_call" | custom-call | tf_op jit(solution)/shard_map/pallas_call | solution.py:450
Async XLA Ops:
  4.8 12.7 %collective-permute-start = (bf16[256,2048]{1,0:T(8,128)(2,1)S(1)}, bf16[256,2048]{1,0:T(8,128)(2,1)S(1)}, u32[]{:S(2)}, u32[]{:S(2)}) collective-permute-start(bf16[256,2048]{1,0:T(8,128)(2,1)S(1)} %get-tuple-element.8), channel_id=1, source_target_pairs={{0,1},{1,0},{2,3},{3,2},{4,5},{5,4},{6,7},{7,6},{8,9},{9,8},{10,11... | collective-permute-start | bytes 3145736 | tf_op jit(solution)/shard_map/ppermute | solution.py:407
  5.3 12.1 %all-to-all-start = ((bf16[16,16,128]{2,1,0:T(8,128)(2,1)}), bf16[16,16,128]{2,1,0:T(8,128)(2,1)S(1)}, u32[]{:S(2)}, u32[]{:S(2)}) async-start(bf16[16,16,128]{2,1,0:T(8,128)(2,1)} %get-tuple-element.6.after_ref), calls=%async_computation | async-start | bytes 131072 | tf_op jit(solution)/shard_map/all_to_all | solution.py:404
  18.6 11.0 %all-to-all-start.1 = ((bf16[16,2,16,128]{3,2,1,0:T(8,128)(2,1)}), bf16[16,2,16,128]{3,2,1,0:T(8,128)(2,1)S(1)}, u32[]{:S(2)}, u32[]{:S(2)}) async-start(bf16[16,2,16,128]{3,2,1,0:T(8,128)(2,1)} %shard_map.133.after_ref), calls=%async_computation.1 | async-start | bytes 262144 | tf_op jit(solution)/shard_map/all_to_all | solution.py:437
  23.0 2.3 %copy-start = (bf16[3,3,512,512]{3,2,1,0:T(8,128)(2,1)S(1)}, bf16[3,3,512,512]{3,2,1,0:T(8,128)(2,1)}, u32[]{:S(2)}) copy-start(bf16[3,3,512,512]{3,2,1,0:T(8,128)(2,1)} %two_ref.1) | copy-start | bytes 14155780
where the time goes:
time: 30.7 us; the launch traced here: 30.2 us
  Pallas kernels  13.9 us (45%)
  starting transfers between devices  12.4 us (40%)
  local copies, waits for them, and re-layouts  2.33 us (8%)
  waiting for transfers between devices  0.92 us (3%)
  between operations  0.67 us (2%)
    all_to_all x1, starting transfers between devices, on_device(): lax.all_to_all(outgoing, 'rows', split_axis=0, concat_axis=0, axis_index_...  7.52 us
    all_to_all x1, starting transfers between devices, on_device(): lax.all_to_all(partials, 'rows', split_axis=0, concat_axis=0, axis_index_...  4.37 us
    pallas_call x1, Pallas kernels, on_device(): pl.pallas_call(functools.partial(decode_kernel, feature_rows=feature_rows...  4.25 us
    pallas_call x1, Pallas kernels, on_device(): pl.pallas_call(functools.partial(attend_kernel, tiles=tiles, per=per, fea...  4.17 us
    pallas_call x1, Pallas kernels, on_device(): pl.pallas_call(fold_kernel, in_specs=[smem, vmem, anywhere, anywhere, any...  3.71 us
    unnamed x2, local copies, waits for them, and re-layouts  2.33 us
    pallas_call x1, Pallas kernels, on_device(): pl.pallas_call(functools.partial(project_kernel, rows=rows, per=per), in_...  1.14 us
    all_to_all x1, waiting for transfers between devices, on_device(): lax.all_to_all(outgoing, 'rows', split_axis=0, concat_axis=0, axis_index_...  0.91 us
  transfers between devices with their start and end apart: 3, of which 1 were waited for; matrix products, arithmetic and copies ran while one was open for 0% of the time, Pallas kernels for 26%

commit v1 on v0

--- a/solution.py
+++ b/solution.py
@@ -92,20 +92,24 @@
             ((q_any, q_ref), (nk_any, nk_ref), (nv_any, nv_ref), (codes_any, codes_ref))
         )
     ]
-    keys = [pltpu.make_async_copy(k_any.at[r], k_ref.at[r], sems.at[4 + r]) for r in range(rows)]
-    values = [
-        pltpu.make_async_copy(v_any.at[r], v_ref.at[r], sems.at[4 + rows + r]) for r in range(rows)
-    ]
+    cached = k_any.shape[1]
+    keys, values = (
+        [
+            pltpu.make_async_copy(
+                source.at[r], target.at[pl.ds(r * cached, cached)], sems.at[base + r]
+            )
+            for r in range(rows)
+        ]
+        for source, target, base in ((k_any, k_ref, 4), (v_any, v_ref, 4 + rows))
+    )
     begin = pl.multiple_of((1 - parity_ref[0]) * give_columns, LANES)
     give = pltpu.make_async_copy(
         weight_any.at[:, pl.ds(begin, give_columns)], give_ref, sems.at[4 + 2 * rows]
     )
     for copy in small:
         copy.start()
-    for r in range(rows):
-        keys[r].start()
-        values[r].start()
-    give.start()
+    for copy in keys + values:
+        copy.start()
 
     heads = width // HEAD_DIM
     factor = 1.0 / math.sqrt(HEAD_DIM)
@@ -139,38 +143,59 @@
                 place = feature_rows + at * WINDOW + step
                 msg[tile, place : place + 1, :] = total
 
+    padding = jnp.zeros((16 - rows, width), jnp.float32)
+    new_keys = jnp.concatenate([nk_ref[...].astype(jnp.float32), padding], 0).astype(jnp.bfloat16)
+    new_values = jnp.concatenate([nv_ref[...].astype(jnp.float32), padding], 0).astype(jnp.bfloat16)
     queries = q_ref[...].astype(jnp.float32)
-    new_keys = nk_ref[...].astype(jnp.float32)
-    new_values = nv_ref[...].astype(jnp.float32)
-    for r in range(rows):
-        query, new_key, new_value = (x[r : r + 1] for x in (queries, new_keys, new_values))
-        spread = jnp.where(same, query, 0.0).astype(jnp.bfloat16)
-        own_score = jnp.sum(jnp.where(same, query * new_key, 0.0), 1, keepdims=True) * factor
-        keys[r].wait()
-        scores = (
+    spread = jnp.concatenate(
+        [jnp.where(same, queries[r : r + 1], 0.0) for r in range(rows)], 0
+    ).astype(jnp.bfloat16)
+
+    def products(cached):
+        return (
             lax.dot_general(
-                spread, k_ref[r], (((1,), (1,)), ((), ())), preferred_element_type=jnp.float32
+                spread, cached, (((1,), (1,)), ((), ())), preferred_element_type=jnp.float32
             )
             * factor
         )
-        live = lax.broadcasted_iota(jnp.int32, scores.shape, 1) < lengths[r]
-        scores = jnp.where(live, scores, jnp.float32(-1e30))
-        highest = jnp.maximum(jnp.max(scores, 1, keepdims=True), own_score)
-        cache_exp = jnp.where(live, jnp.exp(scores - highest), 0.0)
-        own_exp = jnp.exp(own_score - highest)
-        denom = jnp.sum(cache_exp, 1, keepdims=True) + own_exp
-        cache_weight = (cache_exp / denom).astype(jnp.bfloat16)
-        own_weight = (own_exp / denom).astype(jnp.bfloat16).astype(jnp.float32)
-        values[r].wait()
-        mixed_in = jnp.dot(cache_weight, v_ref[r], preferred_element_type=jnp.float32)
-        attended = jnp.sum(
-            jnp.where(same, mixed_in + own_weight * new_value, 0.0), 0, keepdims=True
-        )
-        for tile in range(tiles):
+
+    def owner(shape):
+        return lax.broadcasted_iota(jnp.int32, shape, 0) // heads
+
+    own_scores = products(new_keys)
+    own_at = owner(own_scores.shape) == lax.broadcasted_iota(jnp.int32, own_scores.shape, 1)
+    own_score = jnp.sum(jnp.where(own_at, own_scores, 0.0), 1, keepdims=True)
+    for copy in keys:
+        copy.wait()
+    scores = products(k_ref[...])
+    cache = scores.shape[1] // rows
+    row = owner(scores.shape)
+    position = lax.broadcasted_iota(jnp.int32, scores.shape, 1) - row * cache
+    limit = jnp.zeros(scores.shape, jnp.int32)
+    for r in range(rows):
+        limit = jnp.where(row == r, lengths[r], limit)
+    live = (position >= 0) & (position < limit)
+    scores = jnp.where(live, scores, jnp.float32(-1e30))
+    highest = jnp.maximum(jnp.max(scores, 1, keepdims=True), own_score)
+    cache_exp = jnp.where(live, jnp.exp(scores - highest), 0.0)
+    own_exp = jnp.exp(own_score - highest)
+    denom = jnp.sum(cache_exp, 1, keepdims=True) + own_exp
+    cache_weight = (cache_exp / denom).astype(jnp.bfloat16)
+    own_weight = jnp.where(own_at, own_exp / denom, 0.0).astype(jnp.bfloat16)
+    for copy in values:
+        copy.wait()
+    give.start()
+    attended = jnp.dot(cache_weight, v_ref[...], preferred_element_type=jnp.float32) + jnp.dot(
+        own_weight, new_values, preferred_element_type=jnp.float32
+    )
+    for tile in range(tiles):
+        for r in range(rows):
             for step in range(per):
-                begin = (member(tile, tiles) // 2 * per + step) * LANES
+                head = member(tile, tiles) // 2 * per + step
                 place = r * per + step
-                msg[tile, place : place + 1, :] = attended[:, begin : begin + LANES]
+                msg[tile, place : place + 1, :] = attended[
+                    r * heads + head : r * heads + head + 1, head * LANES : (head + 1) * LANES
+                ]
     out_ref[...] = msg[...].astype(jnp.bfloat16)
     give.wait()
 
@@ -381,8 +406,8 @@
             pltpu.VMEM(queries.shape, queries.dtype),
             pltpu.VMEM(new_keys.shape, new_keys.dtype),
             pltpu.VMEM(new_values.shape, new_values.dtype),
-            pltpu.VMEM(cache_keys.shape, cache_keys.dtype),
-            pltpu.VMEM(cache_values.shape, cache_values.dtype),
+            pltpu.VMEM((rows * cache_keys.shape[1], width), cache_keys.dtype),
+            pltpu.VMEM((rows * cache_values.shape[1], width), cache_values.dtype),
             pltpu.VMEM(codes.shape, codes.dtype),
             pltpu.VMEM((tiles, depth, LANES), jnp.float32),
             pltpu.SemaphoreType.DMA((5 + 2 * rows,)),
@@ -432,6 +457,11 @@
             pltpu.VMEM((tiles * depth, LANES), jnp.float32),
             pltpu.VMEM((groups, tiles * rows * lines, LANES), jnp.float32),
         ],
+        cost_estimate=pl.CostEstimate(
+            flops=4 * tiles * rows * share * half,
+            transcendentals=0,
+            bytes_accessed=3 * conv_two.size,
+        ),
         compiler_params=params,
     )(parity, near(incoming), near(own), near(other))
     gathered = lax.all_to_all(

time: 30.7 us -> 31.3 us (1.020)
  Pallas kernels: 13.9 us -> 14.5 us
    pallas_call x1, Pallas kernels: 4.17 us -> 4.72 us  [on_device(): pl.pallas_call(functools.partial(attend_kernel, tiles=tiles, per=per, fea...]
where the time goes in v1:
time: 31.3 us; the launch traced here: 30.8 us
  Pallas kernels  14.5 us (46%)
  starting transfers between devices  12.4 us (40%)
  local copies, waits for them, and re-layouts  2.33 us (7%)
  waiting for transfers between devices  0.92 us (3%)
  between operations  0.67 us (2%)
    all_to_all x1, starting transfers between devices, on_device(): lax.all_to_all(outgoing, 'rows', split_axis=0, concat_axis=0, axis_index_...  7.52 us
    pallas_call x1, Pallas kernels, on_device(): pl.pallas_call(functools.partial(attend_kernel, tiles=tiles, per=per, fea...  4.72 us
    all_to_all x1, starting transfers between devices, on_device(): lax.all_to_all(partials, 'rows', split_axis=0, concat_axis=0, axis_index_...  4.37 us
    pallas_call x1, Pallas kernels, on_device(): pl.pallas_call(functools.partial(decode_kernel, feature_rows=feature_rows...  4.25 us
    pallas_call x1, Pallas kernels, on_device(): pl.pallas_call(fold_kernel, in_specs=[smem, vmem, anywhere, anywhere, any...  3.71 us
    unnamed x2, local copies, waits for them, and re-layouts  2.33 us
    pallas_call x1, Pallas kernels, on_device(): pl.pallas_call(functools.partial(project_kernel, rows=rows, per=per), in_...  1.14 us
    all_to_all x1, waiting for transfers between devices, on_device(): lax.all_to_all(outgoing, 'rows', split_axis=0, concat_axis=0, axis_index_...  0.91 us
  transfers between devices with their start and end apart: 3, of which 1 were waited for; matrix products, arithmetic and copies ran while one was open for 0% of the time, Pallas kernels for 26%

profile of v1, /device:TPU:0, one launch (start us, length us, event | category | flops | bytes accessed | tf_op | source)
XLA Modules:
  0.0 30.8 jit_solution(17805612345325097677)
XLA Ops:
  0.6 4.7 %shard_map.131 = (bf16[16,16,128]{2,1,0:T(8,128)(2,1)}, bf16[256,2048]{1,0:T(8,128)(2,1)S(1)}) custom-call(s32[2]{0:T(128)} %lengths.1, s32[2]{0:T(128)} %slots.1, s32[1]{0:T(128)} %bitcast.parity_ref, bf16[2,4096]{1,0:T(2,128)(2,1)} %q_any.1, bf16[2,4096]{1,0:T(2,128)(2,1)} %nk_any.1, bf16[2,4096]{1,0:T(2,128)(2,1)} %nv_any.1, bf16[2,64,4096]{2,1,0:T(8,128)(2,1)} %k_any.1, ...), custom_call_target="tpu_custom_call" | custom-call | tf_op jit(solution)/shard_map/pallas_call | solution.py:397
  5.4 0.5 %collective-permute-start = (bf16[256,2048]{1,0:T(8,128)(2,1)S(1)}, bf16[256,2048]{1,0:T(8,128)(2,1)S(1)}, u32[]{:S(2)}, u32[]{:S(2)}) collective-permute-start(bf16[256,2048]{1,0:T(8,128)(2,1)S(1)} %get-tuple-element.8), channel_id=1, source_target_pairs={{0,1},{1,0},{2,3},{3,2},{4,5},{5,4},{6,7},{7,6},{8,9},{9,8},{10,11... | collective-permute-start | bytes 3145736 | tf_op jit(solution)/shard_map/ppermute | solution.py:432
  5.9 7.5 %all-to-all-start = ((bf16[16,16,128]{2,1,0:T(8,128)(2,1)}), bf16[16,16,128]{2,1,0:T(8,128)(2,1)S(1)}, u32[]{:S(2)}, u32[]{:S(2)}) async-start(bf16[16,16,128]{2,1,0:T(8,128)(2,1)} %get-tuple-element.6.after_ref), calls=%async_computation | async-start | bytes 131072 | tf_op jit(solution)/shard_map/all_to_all | solution.py:429
  13.4 3.7 %shard_map.132 = (bf16[256,512]{1,0:T(8,128)(2,1)S(1)}, bf16[256,2048]{1,0:T(8,128)(2,1)S(1)}) custom-call(s32[1]{0:T(128)} %bitcast.parity_ref, f32[5,512]{1,0:T(8,128)} %cw_ref.1, bf16[3,3,512,512]{3,2,1,0:T(8,128)(2,1)} %conv_ref.1, bf16[256,4096]{1,0:T(8,128)(2,1)} %weight_ref.1, bf16[16,16,128]{2,1,0:T(8,128)(2,1)} %get-tuple-element.6.after_ref), custom_call_target="tpu_custom_call" | custom-call | tf_op jit(solution)/shard_map/pallas_call | solution.py:434
  17.1 0.9 %all-to-all-done.in_ref = bf16[16,16,128]{2,1,0:T(8,128)(2,1)S(1)} async-done(((bf16[16,16,128]{2,1,0:T(8,128)(2,1)}), bf16[16,16,128]{2,1,0:T(8,128)(2,1)S(1)}, u32[]{:S(2)}, u32[]{:S(2)}) %all-to-all-start) | async-done | bytes 65568 | tf_op jit(solution)/shard_map/all_to_all | solution.py:429
  18.0 0.0 collective-permute-done.other_ref
  18.0 1.1 %shard_map.133.after_ref = bf16[16,2,16,128]{3,2,1,0:T(8,128)(2,1)} custom-call(s32[1]{0:T(128)} %bitcast.parity_ref, bf16[16,16,128]{2,1,0:T(8,128)(2,1)S(1)} %all-to-all-done.in_ref, bf16[256,2048]{1,0:T(8,128)(2,1)S(1)} %get-tuple-element.7.own_ref, bf16[256,2048]{1,0:T(8,128)(2,1)S(1)} %collective-permute-done.other_ref), custom_call_target="tpu_custom_call" | custom-call | flops 67108864 | bytes 7077888 | tf_op jit(solution)/shard_map/pallas_call | solution.py:452
  19.2 4.4 %all-to-all-start.1 = ((bf16[16,2,16,128]{3,2,1,0:T(8,128)(2,1)}), bf16[16,2,16,128]{3,2,1,0:T(8,128)(2,1)S(1)}, u32[]{:S(2)}, u32[]{:S(2)}) async-start(bf16[16,2,16,128]{3,2,1,0:T(8,128)(2,1)} %shard_map.133.after_ref), calls=%async_computation.1 | async-start | bytes 262144 | tf_op jit(solution)/shard_map/all_to_all | solution.py:467
  23.6 0.0 copy-start
  23.6 2.3 %copy-done = bf16[3,3,512,512]{3,2,1,0:T(8,128)(2,1)S(1)} copy-done((bf16[3,3,512,512]{3,2,1,0:T(8,128)(2,1)S(1)}, bf16[3,3,512,512]{3,2,1,0:T(8,128)(2,1)}, u32[]{:S(2)}) %copy-start) | copy-done | bytes 4718616
  25.9 4.3 %shard_map.135 = bf16[384,512]{1,0:T(8,128)(2,1)} custom-call(s32[1]{0:T(128)} %bitcast.1.section_ref, bf16[16,16,128]{2,1,0:T(8,128)(2,1)S(1)} %all-to-all-done.in_ref, bf16[256,512]{1,0:T(8,128)(2,1)S(1)} %get-tuple-element.9.fold_ref, bf16[3,3,512,512]{3,2,1,0:T(8,128)(2,1)S(1)} %copy-done, bf16[16,2,16,128]{3,2,1,0:T(8,128)(2,1)} %shard_map.133.after_ref), custom_call_target="tpu_custom_call" | custom-call | tf_op jit(solution)/shard_map/pallas_call | solution.py:472
  30.1 0.0 all-to-all-done.1.in_ref
  30.1 0.6 %shard_map.134 = bf16[2,4096]{1,0:T(2,128)(2,1)} custom-call(bf16[16,2,16,128]{3,2,1,0:T(8,128)(2,1)S(1)} %all-to-all-done.1.in_ref), custom_call_target="tpu_custom_call" | custom-call | tf_op jit(solution)/shard_map/pallas_call | solution.py:480
Async XLA Ops:
  5.4 12.7 %collective-permute-start = (bf16[256,2048]{1,0:T(8,128)(2,1)S(1)}, bf16[256,2048]{1,0:T(8,128)(2,1)S(1)}, u32[]{:S(2)}, u32[]{:S(2)}) collective-permute-start(bf16[256,2048]{1,0:T(8,128)(2,1)S(1)} %get-tuple-element.8), channel_id=1, source_target_pairs={{0,1},{1,0},{2,3},{3,2},{4,5},{5,4},{6,7},{7,6},{8,9},{9,8},{10,11... | collective-permute-start | bytes 3145736 | tf_op jit(solution)/shard_map/ppermute | solution.py:432
  5.9 12.1 %all-to-all-start = ((bf16[16,16,128]{2,1,0:T(8,128)(2,1)}), bf16[16,16,128]{2,1,0:T(8,128)(2,1)S(1)}, u32[]{:S(2)}, u32[]{:S(2)}) async-start(bf16[16,16,128]{2,1,0:T(8,128)(2,1)} %get-tuple-element.6.after_ref), calls=%async_computation | async-start | bytes 131072 | tf_op jit(solution)/shard_map/all_to_all | solution.py:429
  19.2 11.0 %all-to-all-start.1 = ((bf16[16,2,16,128]{3,2,1,0:T(8,128)(2,1)}), bf16[16,2,16,128]{3,2,1,0:T(8,128)(2,1)S(1)}, u32[]{:S(2)}, u32[]{:S(2)}) async-start(bf16[16,2,16,128]{3,2,1,0:T(8,128)(2,1)} %shard_map.133.after_ref), calls=%async_computation.1 | async-start | bytes 262144 | tf_op jit(solution)/shard_map/all_to_all | solution.py:467
  23.6 2.3 %copy-start = (bf16[3,3,512,512]{3,2,1,0:T(8,128)(2,1)S(1)}, bf16[3,3,512,512]{3,2,1,0:T(8,128)(2,1)}, u32[]{:S(2)}) copy-start(bf16[3,3,512,512]{3,2,1,0:T(8,128)(2,1)} %two_ref.1) | copy-start | bytes 14155780

commit v2 on v1

--- a/solution.py
+++ b/solution.py
@@ -78,6 +78,8 @@
     v_ref,
     codes_ref,
     msg,
+    by_head,
+    spread,
     sems,
     *,
     tiles,
@@ -113,10 +115,6 @@
 
     heads = width // HEAD_DIM
     factor = 1.0 / math.sqrt(HEAD_DIM)
-    same = (
-        lax.broadcasted_iota(jnp.int32, (heads, width), 1) // HEAD_DIM
-        == lax.broadcasted_iota(jnp.int32, (heads, width), 0)
-    )
     msg[...] = jnp.zeros_like(msg)
     for copy in small:
         copy.wait()
@@ -124,67 +122,70 @@
     words = codes_ref[...]
     blocks = words.shape[1] // LANES
     pieces = [encode(words & 32767), encode(words >> 15)]
-    for tile in range(tiles):
-        number = (member(tile, tiles) + IMG_SPLIT // 2) % tiles
-        start = window_start(number % IMG_SPLIT)
+    for slot in range(tiles // IMG_SPLIT):
         gains = [
-            jnp.where(slots[r] == number // IMG_SPLIT, 1.0, 0.0).astype(jnp.float32)
-            for r in range(rows)
+            jnp.where(slots[r] == slot, 1.0, 0.0).astype(jnp.float32) for r in range(rows)
         ]
         for at, piece in enumerate(pieces):
-            for step in range(WINDOW):
-                block = start + step
-                if block < 0 or block >= blocks:
+            total = piece[0:1] * gains[0]
+            for r in range(1, rows):
+                total = total + piece[r : r + 1] * gains[r]
+            for tile in range(tiles):
+                number = (member(tile, tiles) + IMG_SPLIT // 2) % tiles
+                if number // IMG_SPLIT != slot:
                     continue
-                part = piece[:, block * LANES : (block + 1) * LANES]
-                total = part[0:1] * gains[0]
-                for r in range(1, rows):
-                    total = total + part[r : r + 1] * gains[r]
-                place = feature_rows + at * WINDOW + step
-                msg[tile, place : place + 1, :] = total
-
+                for step in range(WINDOW):
+                    block = window_start(number % IMG_SPLIT) + step
+                    if block < 0 or block >= blocks:
+                        continue
+                    place = feature_rows + at * WINDOW + step
+                    msg[tile, place : place + 1, :] = total[:, block * LANES : (block + 1) * LANES]
+
+    queries = q_ref[...].astype(jnp.float32)
+    by_head[...] = jnp.zeros_like(by_head)
+    for r in range(rows):
+        for head in range(heads):
+            by_head[r * heads + head : r * heads + head + 1, :] = queries[
+                r : r + 1, head * LANES : (head + 1) * LANES
+            ]
+    turned = by_head[...].T
+    column = lax.broadcasted_iota(jnp.int32, (1, LANES), 1)
+    for head in range(heads):
+        spread[head * LANES : (head + 1) * LANES, :] = jnp.where(
+            column % heads == head, turned, 0.0
+        ).astype(jnp.bfloat16)
     padding = jnp.zeros((16 - rows, width), jnp.float32)
-    new_keys = jnp.concatenate([nk_ref[...].astype(jnp.float32), padding], 0).astype(jnp.bfloat16)
+    known = rows * cached
+    k_ref[known:, :] = jnp.concatenate([nk_ref[...].astype(jnp.float32), padding], 0).astype(
+        jnp.bfloat16
+    )
     new_values = jnp.concatenate([nv_ref[...].astype(jnp.float32), padding], 0).astype(jnp.bfloat16)
-    queries = q_ref[...].astype(jnp.float32)
-    spread = jnp.concatenate(
-        [jnp.where(same, queries[r : r + 1], 0.0) for r in range(rows)], 0
-    ).astype(jnp.bfloat16)
-
-    def products(cached):
-        return (
-            lax.dot_general(
-                spread, cached, (((1,), (1,)), ((), ())), preferred_element_type=jnp.float32
-            )
-            * factor
-        )
-
-    def owner(shape):
-        return lax.broadcasted_iota(jnp.int32, shape, 0) // heads
-
-    own_scores = products(new_keys)
-    own_at = owner(own_scores.shape) == lax.broadcasted_iota(jnp.int32, own_scores.shape, 1)
-    own_score = jnp.sum(jnp.where(own_at, own_scores, 0.0), 1, keepdims=True)
     for copy in keys:
         copy.wait()
-    scores = products(k_ref[...])
-    cache = scores.shape[1] // rows
-    row = owner(scores.shape)
-    position = lax.broadcasted_iota(jnp.int32, scores.shape, 1) - row * cache
-    limit = jnp.zeros(scores.shape, jnp.int32)
+    products = jnp.dot(k_ref[...], spread[...], preferred_element_type=jnp.float32) * factor
+    give.start()
+    own_scores = products[known:]
+    scores = products[:known]
+    owner = column // heads
+    own_at = lax.broadcasted_iota(jnp.int32, own_scores.shape, 0) == owner
+    own_score = jnp.sum(jnp.where(own_at, own_scores, 0.0), 0, keepdims=True)
+    limit = jnp.zeros(column.shape, jnp.int32)
     for r in range(rows):
-        limit = jnp.where(row == r, lengths[r], limit)
+        limit = jnp.where(owner == r, lengths[r], limit)
+    position = lax.broadcasted_iota(jnp.int32, scores.shape, 0) - owner * cached
     live = (position >= 0) & (position < limit)
     scores = jnp.where(live, scores, jnp.float32(-1e30))
-    highest = jnp.maximum(jnp.max(scores, 1, keepdims=True), own_score)
+    highest = jnp.maximum(jnp.max(scores, 0, keepdims=True), own_score)
     cache_exp = jnp.where(live, jnp.exp(scores - highest), 0.0)
     own_exp = jnp.exp(own_score - highest)
-    denom = jnp.sum(cache_exp, 1, keepdims=True) + own_exp
-    cache_weight = (cache_exp / denom).astype(jnp.bfloat16)
-    own_weight = jnp.where(own_at, own_exp / denom, 0.0).astype(jnp.bfloat16)
+    denom = jnp.sum(cache_exp, 0, keepdims=True) + own_exp
+    cache_weight = (cache_exp / denom).T[: rows * heads].astype(jnp.bfloat16)
+    own_weight = jnp.where(own_at, own_exp / denom, 0.0)
+    own_weight = jnp.concatenate(
+        [own_weight, jnp.zeros((LANES - own_weight.shape[0], LANES), jnp.float32)], 0
+    ).T[: rows * heads, :16].astype(jnp.bfloat16)
     for copy in values:
         copy.wait()
-    give.start()
     attended = jnp.dot(cache_weight, v_ref[...], preferred_element_type=jnp.float32) + jnp.dot(
         own_weight, new_values, preferred_element_type=jnp.float32
     )
@@ -279,8 +280,17 @@
     bring.wait()
 
 
-def decode_kernel(section_ref, in_ref, fold_ref, two_ref, after_ref, out_ref, *, feature_rows):
+def decode_kernel(
+    section_ref, in_ref, fold_ref, two_any, after_ref, out_ref, two_ref, sems, *, feature_rows
+):
     del after_ref
+    copies = {}
+    for dc in (1, 0, 2):
+        for dr in range(3):
+            copies[dr, dc] = pltpu.make_async_copy(
+                two_any.at[dr, dc], two_ref.at[dr, dc], sems.at[dr, dc]
+            )
+            copies[dr, dc].start()
     section = section_ref[0]
     got = jnp.sum(in_ref[...].astype(jnp.float32), 0)
     pieces = []
@@ -341,6 +351,7 @@
     for dc in (1, 0, 2):
         part = None
         for dr in range(3):
+            copies[dr, dc].wait()
             term = jnp.dot(
                 activated[dr * IMG_W : dr * IMG_W + count],
                 two_ref[dr, dc],
@@ -406,10 +417,12 @@
             pltpu.VMEM(queries.shape, queries.dtype),
             pltpu.VMEM(new_keys.shape, new_keys.dtype),
             pltpu.VMEM(new_values.shape, new_values.dtype),
-            pltpu.VMEM((rows * cache_keys.shape[1], width), cache_keys.dtype),
+            pltpu.VMEM((rows * cache_keys.shape[1] + 16, width), cache_keys.dtype),
             pltpu.VMEM((rows * cache_values.shape[1], width), cache_values.dtype),
             pltpu.VMEM(codes.shape, codes.dtype),
             pltpu.VMEM((tiles, depth, LANES), jnp.float32),
+            pltpu.VMEM((LANES, LANES), jnp.float32),
+            pltpu.VMEM((width, LANES), jnp.bfloat16),
             pltpu.SemaphoreType.DMA((5 + 2 * rows,)),
         ],
         compiler_params=pltpu.CompilerParams(vmem_limit_bytes=56 * 1024 * 1024),
@@ -457,11 +470,6 @@
             pltpu.VMEM((tiles * depth, LANES), jnp.float32),
             pltpu.VMEM((groups, tiles * rows * lines, LANES), jnp.float32),
         ],
-        cost_estimate=pl.CostEstimate(
-            flops=4 * tiles * rows * share * half,
-            transcendentals=0,
-            bytes_accessed=3 * conv_two.size,
-        ),
         compiler_params=params,
     )(parity, near(incoming), near(own), near(other))
     gathered = lax.all_to_all(
@@ -471,11 +479,15 @@
     section = (place + IMG_SPLIT // 2) % tiles % IMG_SPLIT
     decoded = pl.pallas_call(
         functools.partial(decode_kernel, feature_rows=feature_rows),
-        in_specs=[smem, vmem, vmem, vmem, anywhere],
+        in_specs=[smem, vmem, vmem, anywhere, anywhere],
         out_specs=vmem,
         out_shape=jax.ShapeDtypeStruct((TILE_H * IMG_W, channels), jnp.bfloat16),
+        scratch_shapes=[
+            pltpu.VMEM(conv_two.shape, conv_two.dtype),
+            pltpu.SemaphoreType.DMA((3, 3)),
+        ],
         compiler_params=params,
-    )(section.reshape(1).astype(jnp.int32), near(incoming), near(folded), near(conv_two), near(partials))
+    )(section.reshape(1).astype(jnp.int32), near(incoming), near(folded), far(conv_two), near(partials))
 
     mixed = pl.pallas_call(
         functools.partial(total_kernel, rows=rows),

time: 31.3 us -> 30.2 us (0.965)
  local copies, waits for them, and re-layouts: 2.33 us -> 0 us
  Pallas kernels: 14.5 us -> 15.7 us
    unnamed x2 -> x0, local copies, waits for them, and re-layouts: 2.33 us -> none
    pallas_call x1, Pallas kernels: 4.25 us -> 6.23 us  [on_device(): pl.pallas_call(functools.partial(decode_kernel, feature_rows=feature_rows...]
    pallas_call x1, Pallas kernels: 4.72 us -> 3.95 us  [on_device(): pl.pallas_call(functools.partial(attend_kernel, tiles=tiles, per=per, fea...]
  transfers between devices with their start and end apart: 3 -> 3, of which waited for: 1 -> 1; matrix products, arithmetic and copies ran while one was open for 0% -> 0% of each run, Pallas kernels for 26% -> 33%
where the time goes in v2:
time: 30.2 us; the launch traced here: 29.7 us
  Pallas kernels  15.7 us (52%)
  starting transfers between devices  12.4 us (41%)
  waiting for transfers between devices  0.92 us (3%)
  between operations  0.68 us (2%)
    all_to_all x1, starting transfers between devices, on_device(): lax.all_to_all(outgoing, 'rows', split_axis=0, concat_axis=0, axis_index_...  7.52 us
    pallas_call x1, Pallas kernels, on_device(): pl.pallas_call(functools.partial(decode_kernel, feature_rows=feature_rows...  6.23 us
    all_to_all x1, starting transfers between devices, on_device(): lax.all_to_all(partials, 'rows', split_axis=0, concat_axis=0, axis_index_...  4.37 us
    pallas_call x1, Pallas kernels, on_device(): pl.pallas_call(functools.partial(attend_kernel, tiles=tiles, per=per, fea...  3.95 us
    pallas_call x1, Pallas kernels, on_device(): pl.pallas_call(fold_kernel, in_specs=[smem, vmem, anywhere, anywhere, any...  3.71 us
    pallas_call x1, Pallas kernels, on_device(): pl.pallas_call(functools.partial(project_kernel, rows=rows, per=per), in_...  1.14 us
    all_to_all x1, waiting for transfers between devices, on_device(): lax.all_to_all(outgoing, 'rows', split_axis=0, concat_axis=0, axis_index_...  0.91 us
    pallas_call x1, Pallas kernels, on_device(): pl.pallas_call(functools.partial(total_kernel, rows=rows), in_specs=[vmem...  0.64 us
  transfers between devices with their start and end apart: 3, of which 1 were waited for; matrix products, arithmetic and copies ran while one was open for 0% of the time, Pallas kernels for 33%

profile of v2, /device:TPU:0, one launch (start us, length us, event | category | flops | bytes accessed | tf_op | source)
XLA Modules:
  0.0 29.7 jit_solution(10140855717388325691)
XLA Ops:
  0.6 4.0 %shard_map.131 = (bf16[16,16,128]{2,1,0:T(8,128)(2,1)}, bf16[256,2048]{1,0:T(8,128)(2,1)S(1)}) custom-call(s32[2]{0:T(128)} %lengths.1, s32[2]{0:T(128)} %slots.1, s32[1]{0:T(128)} %bitcast.parity_ref, bf16[2,4096]{1,0:T(2,128)(2,1)} %q_any.1, bf16[2,4096]{1,0:T(2,128)(2,1)} %nk_any.1, bf16[2,4096]{1,0:T(2,128)(2,1)} %nv_any.1, bf16[2,64,4096]{2,1,0:T(8,128)(2,1)} %k_any.1, ...), custom_call_target="tpu_custom_call" | custom-call | tf_op jit(solution)/shard_map/pallas_call | solution.py:408
  4.6 0.5 %collective-permute-start = (bf16[256,2048]{1,0:T(8,128)(2,1)S(1)}, bf16[256,2048]{1,0:T(8,128)(2,1)S(1)}, u32[]{:S(2)}, u32[]{:S(2)}) collective-permute-start(bf16[256,2048]{1,0:T(8,128)(2,1)S(1)} %get-tuple-element.8), channel_id=1, source_target_pairs={{0,1},{1,0},{2,3},{3,2},{4,5},{5,4},{6,7},{7,6},{8,9},{9,8},{10,11... | collective-permute-start | bytes 3145736 | tf_op jit(solution)/shard_map/ppermute | solution.py:445
  5.1 7.5 %all-to-all-start = ((bf16[16,16,128]{2,1,0:T(8,128)(2,1)}), bf16[16,16,128]{2,1,0:T(8,128)(2,1)S(1)}, u32[]{:S(2)}, u32[]{:S(2)}) async-start(bf16[16,16,128]{2,1,0:T(8,128)(2,1)} %get-tuple-element.6.after_ref), calls=%async_computation | async-start | bytes 131072 | tf_op jit(solution)/shard_map/all_to_all | solution.py:442
  12.6 3.7 %shard_map.132 = (bf16[256,512]{1,0:T(8,128)(2,1)S(1)}, bf16[256,2048]{1,0:T(8,128)(2,1)S(1)}) custom-call(s32[1]{0:T(128)} %bitcast.parity_ref, f32[5,512]{1,0:T(8,128)} %cw_ref.1, bf16[3,3,512,512]{3,2,1,0:T(8,128)(2,1)} %conv_ref.1, bf16[256,4096]{1,0:T(8,128)(2,1)} %weight_ref.1, bf16[16,16,128]{2,1,0:T(8,128)(2,1)} %get-tuple-element.6.after_ref), custom_call_target="tpu_custom_call" | custom-call | tf_op jit(solution)/shard_map/pallas_call | solution.py:447
  16.4 0.9 %all-to-all-done.in_ref = bf16[16,16,128]{2,1,0:T(8,128)(2,1)S(1)} async-done(((bf16[16,16,128]{2,1,0:T(8,128)(2,1)}), bf16[16,16,128]{2,1,0:T(8,128)(2,1)S(1)}, u32[]{:S(2)}, u32[]{:S(2)}) %all-to-all-start) | async-done | bytes 65568 | tf_op jit(solution)/shard_map/all_to_all | solution.py:442
  17.3 0.0 collective-permute-done.other_ref
  17.3 1.1 %shard_map.133.after_ref = bf16[16,2,16,128]{3,2,1,0:T(8,128)(2,1)} custom-call(s32[1]{0:T(128)} %bitcast.parity_ref, bf16[16,16,128]{2,1,0:T(8,128)(2,1)S(1)} %all-to-all-done.in_ref, bf16[256,2048]{1,0:T(8,128)(2,1)S(1)} %get-tuple-element.7.own_ref, bf16[256,2048]{1,0:T(8,128)(2,1)S(1)} %collective-permute-done.other_ref), custom_call_target="tpu_custom_call" | custom-call | tf_op jit(solution)/shard_map/pallas_call | solution.py:465
  18.4 4.4 %all-to-all-start.1 = ((bf16[16,2,16,128]{3,2,1,0:T(8,128)(2,1)}), bf16[16,2,16,128]{3,2,1,0:T(8,128)(2,1)S(1)}, u32[]{:S(2)}, u32[]{:S(2)}) async-start(bf16[16,2,16,128]{3,2,1,0:T(8,128)(2,1)} %shard_map.133.after_ref), calls=%async_computation.1 | async-start | bytes 262144 | tf_op jit(solution)/shard_map/all_to_all | solution.py:475
  22.8 6.2 %shard_map.135 = bf16[384,512]{1,0:T(8,128)(2,1)} custom-call(s32[1]{0:T(128)} %bitcast.1.section_ref, bf16[16,16,128]{2,1,0:T(8,128)(2,1)S(1)} %all-to-all-done.in_ref, bf16[256,512]{1,0:T(8,128)(2,1)S(1)} %get-tuple-element.9.fold_ref, bf16[3,3,512,512]{3,2,1,0:T(8,128)(2,1)} %two_any.1, bf16[16,2,16,128]{3,2,1,0:T(8,128)(2,1)} %shard_map.133.after_ref), custom_call_target="tpu_custom_call" | custom-call | tf_op jit(solution)/shard_map/pallas_call | solution.py:480
  29.0 0.0 all-to-all-done.1.in_ref
  29.0 0.6 %shard_map.134 = bf16[2,4096]{1,0:T(2,128)(2,1)} custom-call(bf16[16,2,16,128]{3,2,1,0:T(8,128)(2,1)S(1)} %all-to-all-done.1.in_ref), custom_call_target="tpu_custom_call" | custom-call | tf_op jit(solution)/shard_map/pallas_call | solution.py:492
Async XLA Ops:
  4.6 12.7 %collective-permute-start = (bf16[256,2048]{1,0:T(8,128)(2,1)S(1)}, bf16[256,2048]{1,0:T(8,128)(2,1)S(1)}, u32[]{:S(2)}, u32[]{:S(2)}) collective-permute-start(bf16[256,2048]{1,0:T(8,128)(2,1)S(1)} %get-tuple-element.8), channel_id=1, source_target_pairs={{0,1},{1,0},{2,3},{3,2},{4,5},{5,4},{6,7},{7,6},{8,9},{9,8},{10,11... | collective-permute-start | bytes 3145736 | tf_op jit(solution)/shard_map/ppermute | solution.py:445
  5.1 12.1 %all-to-all-start = ((bf16[16,16,128]{2,1,0:T(8,128)(2,1)}), bf16[16,16,128]{2,1,0:T(8,128)(2,1)S(1)}, u32[]{:S(2)}, u32[]{:S(2)}) async-start(bf16[16,16,128]{2,1,0:T(8,128)(2,1)} %get-tuple-element.6.after_ref), calls=%async_computation | async-start | bytes 131072 | tf_op jit(solution)/shard_map/all_to_all | solution.py:442
  18.4 10.6 %all-to-all-start.1 = ((bf16[16,2,16,128]{3,2,1,0:T(8,128)(2,1)}), bf16[16,2,16,128]{3,2,1,0:T(8,128)(2,1)S(1)}, u32[]{:S(2)}, u32[]{:S(2)}) async-start(bf16[16,2,16,128]{3,2,1,0:T(8,128)(2,1)} %shard_map.133.after_ref), calls=%async_computation.1 | async-start | bytes 262144 | tf_op jit(solution)/shard_map/all_to_all | solution.py:475

commit v3 on v2

--- a/solution.py
+++ b/solution.py
@@ -22,6 +22,8 @@
 CODE_ROWS = WINDOW * PIECES
 TAP_ROWS = 24
 FOLD_ROWS = 256
+TAPS = [(dr, dc) for dc in (1, 0, 2) for dr in range(3)]
+EARLY = 4
 VMEM_LIMIT = 24 * 1024 * 1024
 
 
@@ -61,16 +63,13 @@
 def attend_kernel(
     lengths,
     slots,
-    parity_ref,
     q_any,
     nk_any,
     nv_any,
     k_any,
     v_any,
     codes_any,
-    weight_any,
     out_ref,
-    give_ref,
     q_ref,
     nk_ref,
     nv_ref,
@@ -87,7 +86,6 @@
     feature_rows,
 ):
     rows, width = q_ref.shape
-    give_columns = give_ref.shape[1]
     small = [
         pltpu.make_async_copy(source, target, sems.at[at])
         for at, (source, target) in enumerate(
@@ -104,13 +102,9 @@
         ]
         for source, target, base in ((k_any, k_ref, 4), (v_any, v_ref, 4 + rows))
     )
-    begin = pl.multiple_of((1 - parity_ref[0]) * give_columns, LANES)
-    give = pltpu.make_async_copy(
-        weight_any.at[:, pl.ds(begin, give_columns)], give_ref, sems.at[4 + 2 * rows]
-    )
     for copy in small:
         copy.start()
-    for copy in keys + values:
+    for copy in keys:
         copy.start()
 
     heads = width // HEAD_DIM
@@ -160,10 +154,11 @@
         jnp.bfloat16
     )
     new_values = jnp.concatenate([nv_ref[...].astype(jnp.float32), padding], 0).astype(jnp.bfloat16)
+    for copy in values:
+        copy.start()
     for copy in keys:
         copy.wait()
     products = jnp.dot(k_ref[...], spread[...], preferred_element_type=jnp.float32) * factor
-    give.start()
     own_scores = products[known:]
     scores = products[:known]
     owner = column // heads
@@ -198,10 +193,29 @@
                     r * heads + head : r * heads + head + 1, head * LANES : (head + 1) * LANES
                 ]
     out_ref[...] = msg[...].astype(jnp.bfloat16)
-    give.wait()
-
-
-def project_kernel(parity_ref, in_ref, own_ref, other_ref, out_ref, held, total, *, rows, per):
+
+
+def project_kernel(
+    parity_ref,
+    in_ref,
+    own_ref,
+    other_ref,
+    two_any,
+    out_ref,
+    early_ref,
+    held,
+    total,
+    sems,
+    *,
+    rows,
+    per,
+):
+    copies = [
+        pltpu.make_async_copy(two_any.at[dr, dc], early_ref.at[at], sems.at[at])
+        for at, (dr, dc) in enumerate(TAPS[:EARLY])
+    ]
+    for copy in copies:
+        copy.start()
     tiles, depth = in_ref.shape[:2]
     held[...] = in_ref[...].astype(jnp.float32).reshape(held.shape)
     groups = total.shape[0]
@@ -216,8 +230,10 @@
     first, second = lhs[:, :share], lhs[:, share:]
     own = jnp.where(even, first, second).astype(jnp.bfloat16)
     other = jnp.where(even, second, first).astype(jnp.bfloat16)
+    half = own_ref.shape[1]
+    begin = pl.multiple_of(parity_ref[0] * half, LANES)
     product = jnp.dot(own, own_ref[...], preferred_element_type=jnp.float32) + jnp.dot(
-        other, other_ref[...], preferred_element_type=jnp.float32
+        other, other_ref[:, pl.ds(begin, half)], preferred_element_type=jnp.float32
     )
     for row in range(rows):
         for group in range(groups):
@@ -230,6 +246,8 @@
         out_ref[:, group] = (
             total[group].astype(jnp.bfloat16).reshape(tiles, rows * lines, LANES)
         )
+    for copy in copies:
+        copy.wait()
 
 
 def total_kernel(in_ref, out_ref, held, *, rows):
@@ -281,16 +299,14 @@
 
 
 def decode_kernel(
-    section_ref, in_ref, fold_ref, two_any, after_ref, out_ref, two_ref, sems, *, feature_rows
+    section_ref, in_ref, fold_ref, early_ref, two_any, out_ref, late_ref, sems, *, feature_rows
 ):
-    del after_ref
-    copies = {}
-    for dc in (1, 0, 2):
-        for dr in range(3):
-            copies[dr, dc] = pltpu.make_async_copy(
-                two_any.at[dr, dc], two_ref.at[dr, dc], sems.at[dr, dc]
-            )
-            copies[dr, dc].start()
+    copies = [
+        pltpu.make_async_copy(two_any.at[dr, dc], late_ref.at[at], sems.at[at])
+        for at, (dr, dc) in enumerate(TAPS[EARLY:])
+    ]
+    for copy in copies:
+        copy.start()
     section = section_ref[0]
     got = jnp.sum(in_ref[...].astype(jnp.float32), 0)
     pieces = []
@@ -347,22 +363,23 @@
 
     count = count - 2 * IMG_W
     column = lax.broadcasted_iota(jnp.int32, (count, 1), 0) % IMG_W
-    summed = None
-    for dc in (1, 0, 2):
-        part = None
-        for dr in range(3):
-            copies[dr, dc].wait()
-            term = jnp.dot(
-                activated[dr * IMG_W : dr * IMG_W + count],
-                two_ref[dr, dc],
-                preferred_element_type=jnp.float32,
-            )
-            part = term if part is None else part + term
+    summed = part = None
+    for at, (dr, dc) in enumerate(TAPS):
+        if at >= EARLY:
+            copies[at - EARLY].wait()
+        weight = early_ref[at] if at < EARLY else late_ref[at - EARLY]
+        term = jnp.dot(
+            activated[dr * IMG_W : dr * IMG_W + count], weight, preferred_element_type=jnp.float32
+        )
+        part = term if part is None else part + term
+        if dr < 2:
+            continue
         if dc == 0:
             part = jnp.where(column == 0, 0.0, pltpu.roll(part, 1, 0))
         if dc == 2:
             part = jnp.where(column == IMG_W - 1, 0.0, pltpu.roll(part, count - 1, 0))
         summed = part if summed is None else summed + part
+        part = None
     out_ref[...] = summed.astype(jnp.bfloat16)
 
 
@@ -405,14 +422,11 @@
     anywhere = pl.BlockSpec(memory_space=pl.ANY)
     parity = (place % 2).reshape(1).astype(jnp.int32)
 
-    outgoing, give = pl.pallas_call(
+    outgoing = pl.pallas_call(
         functools.partial(attend_kernel, tiles=tiles, per=per, feature_rows=feature_rows),
-        in_specs=[smem] * 3 + [anywhere] * 7,
-        out_specs=[vmem, vmem],
-        out_shape=[
-            pltpu.VMEM((tiles, depth, LANES), jnp.bfloat16),
-            pltpu.VMEM((share, half), out_weight.dtype),
-        ],
+        in_specs=[smem] * 2 + [anywhere] * 6,
+        out_specs=vmem,
+        out_shape=jax.ShapeDtypeStruct((tiles, depth, LANES), jnp.bfloat16),
         scratch_shapes=[
             pltpu.VMEM(queries.shape, queries.dtype),
             pltpu.VMEM(new_keys.shape, new_keys.dtype),
@@ -423,26 +437,24 @@
             pltpu.VMEM((tiles, depth, LANES), jnp.float32),
             pltpu.VMEM((LANES, LANES), jnp.float32),
             pltpu.VMEM((width, LANES), jnp.bfloat16),
-            pltpu.SemaphoreType.DMA((5 + 2 * rows,)),
+            pltpu.SemaphoreType.DMA((4 + 2 * rows,)),
         ],
         compiler_params=pltpu.CompilerParams(vmem_limit_bytes=56 * 1024 * 1024),
     )(
         cache_lengths,
         tile_slot,
-        parity,
         far(queries),
         far(new_keys),
         far(new_values),
         far(cache_keys),
         far(cache_values),
         far(codes),
-        far(out_weight),
     )
     order = [[member(at, tiles) for at in range(tiles)]]
     incoming = lax.all_to_all(
         outgoing, "rows", split_axis=0, concat_axis=0, axis_index_groups=order, tiled=True
     )
-    other = lax.ppermute(give, "rows", [(i, i ^ 1) for i in range(tiles)])
+    other = lax.ppermute(out_weight, "rows", [(i, i ^ 1) for i in range(tiles)])
 
     folded, own = pl.pallas_call(
         fold_kernel,
@@ -462,16 +474,21 @@
         compiler_params=params,
     )(parity, far(code_weight), far(conv_one), far(out_weight), near(outgoing))
 
-    partials = pl.pallas_call(
+    partials, early = pl.pallas_call(
         functools.partial(project_kernel, rows=rows, per=per),
-        in_specs=[smem, vmem, vmem, vmem],
-        out_shape=pltpu.VMEM((tiles, groups, rows * lines, LANES), jnp.bfloat16),
+        in_specs=[smem, vmem, vmem, vmem, anywhere],
+        out_specs=[vmem, vmem],
+        out_shape=[
+            jax.ShapeDtypeStruct((tiles, groups, rows * lines, LANES), jnp.bfloat16),
+            pltpu.VMEM((EARLY,) + conv_two.shape[2:], conv_two.dtype),
+        ],
         scratch_shapes=[
             pltpu.VMEM((tiles * depth, LANES), jnp.float32),
             pltpu.VMEM((groups, tiles * rows * lines, LANES), jnp.float32),
+            pltpu.SemaphoreType.DMA((EARLY,)),
         ],
         compiler_params=params,
-    )(parity, near(incoming), near(own), near(other))
+    )(parity, near(incoming), near(own), near(other), far(conv_two))
     gathered = lax.all_to_all(
         partials, "rows", split_axis=0, concat_axis=0, axis_index_groups=order, tiled=True
     )
@@ -479,15 +496,15 @@
     section = (place + IMG_SPLIT // 2) % tiles % IMG_SPLIT
     decoded = pl.pallas_call(
         functools.partial(decode_kernel, feature_rows=feature_rows),
-        in_specs=[smem, vmem, vmem, anywhere, anywhere],
+        in_specs=[smem, vmem, vmem, vmem, anywhere],
         out_specs=vmem,
         out_shape=jax.ShapeDtypeStruct((TILE_H * IMG_W, channels), jnp.bfloat16),
         scratch_shapes=[
-            pltpu.VMEM(conv_two.shape, conv_two.dtype),
-            pltpu.SemaphoreType.DMA((3, 3)),
+            pltpu.VMEM((len(TAPS) - EARLY,) + conv_two.shape[2:], conv_two.dtype),
+            pltpu.SemaphoreType.DMA((len(TAPS) - EARLY,)),
         ],
         compiler_params=params,
-    )(section.reshape(1).astype(jnp.int32), near(incoming), near(folded), far(conv_two), near(partials))
+    )(section.reshape(1).astype(jnp.int32), near(incoming), near(folded), near(early), far(conv_two))
 
     mixed = pl.pallas_call(
         functools.partial(total_kernel, rows=rows),

time: 30.2 us -> 34.4 us (1.14)
  local copies, waits for them, and re-layouts: 0 us -> 4.43 us
  waiting for transfers between devices: 0.92 us -> 0.04 us
  starting transfers between devices: 12.4 us -> 13.1 us
    unnamed x0 -> x8, local copies, waits for them, and re-layouts: none -> 4.43 us
    all_to_all x1, waiting for transfers between devices: 0.91 us -> 0.04 us  [on_device(): lax.all_to_all(outgoing, 'rows', split_axis=0, concat_axis=0, axis_index_...]
    all_to_all x1, starting transfers between devices: 4.37 us -> 5.09 us  [on_device(): lax.all_to_all(partials, 'rows', split_axis=0, concat_axis=0, axis_index_...]
    pallas_call x1, Pallas kernels: 1.14 us -> 1.59 us  [on_device(): pl.pallas_call(functools.partial(project_kernel, rows=rows, per=per), in_...]
    pallas_call x1, Pallas kernels: 6.23 us -> 5.83 us  [on_device(): pl.pallas_call(functools.partial(decode_kernel, feature_rows=feature_rows...]
  transfers between devices with their start and end apart: 3 -> 3, of which waited for: 1 -> 0; matrix products, arithmetic and copies ran while one was open for 0% -> 0% of each run, Pallas kernels for 33% -> 39%
where the time goes in v3:
time: 34.4 us; the launch traced here: 33.9 us
  Pallas kernels  15.6 us (45%)
  starting transfers between devices  13.1 us (38%)
  local copies, waits for them, and re-layouts  4.43 us (13%)
  between operations  0.69 us (2%)
    all_to_all x1, starting transfers between devices, on_device(): lax.all_to_all(outgoing, 'rows', split_axis=0, concat_axis=0, axis_index_...  7.53 us
    pallas_call x1, Pallas kernels, on_device(): pl.pallas_call(functools.partial(decode_kernel, feature_rows=feature_rows...  5.83 us
    all_to_all x1, starting transfers between devices, on_device(): lax.all_to_all(partials, 'rows', split_axis=0, concat_axis=0, axis_index_...  5.09 us
    unnamed x8, local copies, waits for them, and re-layouts  4.43 us
    pallas_call x1, Pallas kernels, on_device(): pl.pallas_call(functools.partial(attend_kernel, tiles=tiles, per=per, fea...  3.82 us
    pallas_call x1, Pallas kernels, on_device(): pl.pallas_call(fold_kernel, in_specs=[smem, vmem, anywhere, anywhere, any...  3.71 us
    pallas_call x1, Pallas kernels, on_device(): pl.pallas_call(functools.partial(project_kernel, rows=rows, per=per), in_...  1.59 us
  transfers between devices with their start and end apart: 3, of which 0 were waited for; matrix products, arithmetic and copies ran while one was open for 0% of the time, Pallas kernels for 39%

profile of v3, /device:TPU:0, one launch (start us, length us, event | category | flops | bytes accessed | tf_op | source)
XLA Modules:
  0.0 33.9 jit_solution(6628563324733476444)
XLA Ops:
  0.6 0.5 %collective-permute-start = (bf16[256,4096]{1,0:T(8,128)(2,1)}, bf16[256,4096]{1,0:T(8,128)(2,1)S(1)}, u32[]{:S(2)}, u32[]{:S(2)}) collective-permute-start(bf16[256,4096]{1,0:T(8,128)(2,1)} %weight_ref.1), channel_id=1, source_target_pairs={{0,1},{1,0},{2,3},{3,2},{4,5},{5,4},{6,7},{7,6},{8,9},{9,8},{10,11... | collective-permute-start | bytes 6291464 | tf_op jit(solution)/shard_map/ppermute | solution.py:457
  1.2 3.8 %shard_map.131.after_ref = bf16[16,16,128]{2,1,0:T(8,128)(2,1)} custom-call(s32[2]{0:T(128)} %lengths.1, s32[2]{0:T(128)} %slots.1, bf16[2,4096]{1,0:T(2,128)(2,1)} %q_any.1, bf16[2,4096]{1,0:T(2,128)(2,1)} %nk_any.1, bf16[2,4096]{1,0:T(2,128)(2,1)} %nv_any.1, bf16[2,64,4096]{2,1,0:T(8,128)(2,1)} %k_any.1, bf16[2,64,4096]{2,1,0:T(8,128)(2,1)} %v_any.1, ...), custom_call_target="tpu_custom_call" | custom-call | tf_op jit(solution)/shard_map/pallas_call | solution.py:425
  5.0 7.5 %all-to-all-start = ((bf16[16,16,128]{2,1,0:T(8,128)(2,1)}), bf16[16,16,128]{2,1,0:T(8,128)(2,1)S(1)}, u32[]{:S(2)}, u32[]{:S(2)}) async-start(bf16[16,16,128]{2,1,0:T(8,128)(2,1)} %shard_map.131.after_ref), calls=%async_computation | async-start | bytes 131072 | tf_op jit(solution)/shard_map/all_to_all | solution.py:454
  12.5 0.0 copy-start.2
  12.5 0.9 %copy-done.2 = bf16[16,16,128]{2,1,0:T(8,128)(2,1)S(1)} copy-done((bf16[16,16,128]{2,1,0:T(8,128)(2,1)S(1)}, bf16[16,16,128]{2,1,0:T(8,128)(2,1)}, u32[]{:S(2)}) %copy-start.2) | copy-done | bytes 65560
  13.4 3.7 %shard_map.132 = (bf16[256,512]{1,0:T(8,128)(2,1)S(1)}, bf16[256,2048]{1,0:T(8,128)(2,1)S(1)}) custom-call(s32[1]{0:T(128)} %bitcast.parity_ref, f32[5,512]{1,0:T(8,128)} %cw_ref.1, bf16[3,3,512,512]{3,2,1,0:T(8,128)(2,1)} %conv_ref.1, bf16[256,4096]{1,0:T(8,128)(2,1)} %weight_ref.1, bf16[16,16,128]{2,1,0:T(8,128)(2,1)S(1)} %copy-done.2), custom_call_target="tpu_custom_call" | custom-call | tf_op jit(solution)/shard_map/pallas_call | solution.py:459
  17.1 0.0 all-to-all-done.in_ref
  17.1 0.0 collective-permute-done.other_ref
  17.1 0.0 copy-start
  17.1 1.3 %copy-done = bf16[256,4096]{1,0:T(8,128)(2,1)} copy-done((bf16[256,4096]{1,0:T(8,128)(2,1)}, bf16[256,4096]{1,0:T(8,128)(2,1)S(1)}, u32[]{:S(2)}) %copy-start) | copy-done | bytes 2097176
  18.5 0.0 copy-start.1
  18.5 1.6 %copy-done.1 = bf16[256,4096]{1,0:T(8,128)(2,1)S(1)} copy-done((bf16[256,4096]{1,0:T(8,128)(2,1)S(1)}, bf16[256,4096]{1,0:T(8,128)(2,1)}, u32[]{:S(2)}) %copy-start.1) | copy-done | bytes 2097176
  20.1 1.6 %shard_map.133 = (bf16[16,2,16,128]{3,2,1,0:T(8,128)(2,1)S(1)}, bf16[4,512,512]{2,1,0:T(8,128)(2,1)S(1)}) custom-call(s32[1]{0:T(128)} %bitcast.parity_ref, bf16[16,16,128]{2,1,0:T(8,128)(2,1)S(1)} %all-to-all-done.in_ref, bf16[256,2048]{1,0:T(8,128)(2,1)S(1)} %get-tuple-element.6.own_ref, bf16[256,4096]{1,0:T(8,128)(2,1)S(1)} %copy-done.1, ...), custom_call_target="tpu_custom_call" | custom-call | tf_op jit(solution)/shard_map/pallas_call | solution.py:477
  21.7 0.0 copy-start.3
  21.7 0.6 %copy-done.3 = bf16[16,2,16,128]{3,2,1,0:T(8,128)(2,1)} copy-done((bf16[16,2,16,128]{3,2,1,0:T(8,128)(2,1)}, bf16[16,2,16,128]{3,2,1,0:T(8,128)(2,1)S(1)}, u32[]{:S(2)}) %copy-start.3) | copy-done | bytes 131096
  22.3 5.1 %all-to-all-start.1 = ((bf16[16,2,16,128]{3,2,1,0:T(8,128)(2,1)}), bf16[16,2,16,128]{3,2,1,0:T(8,128)(2,1)S(1)}, u32[]{:S(2)}, u32[]{:S(2)}) async-start(bf16[16,2,16,128]{3,2,1,0:T(8,128)(2,1)} %copy-done.3), calls=%async_computation.1 | async-start | bytes 262144 | tf_op jit(solution)/shard_map/all_to_all | solution.py:492
  27.4 5.8 %shard_map.135 = bf16[384,512]{1,0:T(8,128)(2,1)} custom-call(s32[1]{0:T(128)} %bitcast.1.section_ref, bf16[16,16,128]{2,1,0:T(8,128)(2,1)S(1)} %all-to-all-done.in_ref, bf16[256,512]{1,0:T(8,128)(2,1)S(1)} %get-tuple-element.8.fold_ref, bf16[4,512,512]{2,1,0:T(8,128)(2,1)S(1)} %get-tuple-element.9.early_ref, bf16[3,3,512,512]{3,2,1,0:T(8,128)(2,1)} %two_any.3), custom_call_target="tpu_custom_call" | custom-call | tf_op jit(solution)/shard_map/pallas_call | solution.py:497
  33.2 0.0 all-to-all-done.1.in_ref
  33.3 0.6 %shard_map.134 = bf16[2,4096]{1,0:T(2,128)(2,1)} custom-call(bf16[16,2,16,128]{3,2,1,0:T(8,128)(2,1)S(1)} %all-to-all-done.1.in_ref), custom_call_target="tpu_custom_call" | custom-call | tf_op jit(solution)/shard_map/pallas_call | solution.py:509
Async XLA Ops:
  0.6 16.5 %collective-permute-start = (bf16[256,4096]{1,0:T(8,128)(2,1)}, bf16[256,4096]{1,0:T(8,128)(2,1)S(1)}, u32[]{:S(2)}, u32[]{:S(2)}) collective-permute-start(bf16[256,4096]{1,0:T(8,128)(2,1)} %weight_ref.1), channel_id=1, source_target_pairs={{0,1},{1,0},{2,3},{3,2},{4,5},{5,4},{6,7},{7,6},{8,9},{9,8},{10,11... | collective-permute-start | bytes 6291464 | tf_op jit(solution)/shard_map/ppermute | solution.py:457
  5.0 12.2 %all-to-all-start = ((bf16[16,16,128]{2,1,0:T(8,128)(2,1)}), bf16[16,16,128]{2,1,0:T(8,128)(2,1)S(1)}, u32[]{:S(2)}, u32[]{:S(2)}) async-start(bf16[16,16,128]{2,1,0:T(8,128)(2,1)} %shard_map.131.after_ref), calls=%async_computation | async-start | bytes 131072 | tf_op jit(solution)/shard_map/all_to_all | solution.py:454
  12.5 0.9 %copy-start.2 = (bf16[16,16,128]{2,1,0:T(8,128)(2,1)S(1)}, bf16[16,16,128]{2,1,0:T(8,128)(2,1)}, u32[]{:S(2)}) copy-start(bf16[16,16,128]{2,1,0:T(8,128)(2,1)} %shard_map.131.after_ref) | copy-start | bytes 196612
  17.1 1.3 %copy-start = (bf16[256,4096]{1,0:T(8,128)(2,1)}, bf16[256,4096]{1,0:T(8,128)(2,1)S(1)}, u32[]{:S(2)}) copy-start(bf16[256,4096]{1,0:T(8,128)(2,1)S(1)} %collective-permute-done.other_ref) | copy-start | bytes 6291460
  18.5 1.6 %copy-start.1 = (bf16[256,4096]{1,0:T(8,128)(2,1)S(1)}, bf16[256,4096]{1,0:T(8,128)(2,1)}, u32[]{:S(2)}) copy-start(bf16[256,4096]{1,0:T(8,128)(2,1)} %copy-done) | copy-start | bytes 6291460
  21.7 0.6 %copy-start.3 = (bf16[16,2,16,128]{3,2,1,0:T(8,128)(2,1)}, bf16[16,2,16,128]{3,2,1,0:T(8,128)(2,1)S(1)}, u32[]{:S(2)}) copy-start(bf16[16,2,16,128]{3,2,1,0:T(8,128)(2,1)S(1)} %get-tuple-element.7) | copy-start | bytes 393220
  22.3 10.9 %all-to-all-start.1 = ((bf16[16,2,16,128]{3,2,1,0:T(8,128)(2,1)}), bf16[16,2,16,128]{3,2,1,0:T(8,128)(2,1)S(1)}, u32[]{:S(2)}, u32[]{:S(2)}) async-start(bf16[16,2,16,128]{3,2,1,0:T(8,128)(2,1)} %copy-done.3), calls=%async_computation.1 | async-start | bytes 262144 | tf_op jit(solution)/shard_map/all_to_all | solution.py:492

commit v4 on v3

--- a/solution.py
+++ b/solution.py
@@ -23,7 +23,7 @@
 TAP_ROWS = 24
 FOLD_ROWS = 256
 TAPS = [(dr, dc) for dc in (1, 0, 2) for dr in range(3)]
-EARLY = 4
+EARLY = 3
 VMEM_LIMIT = 24 * 1024 * 1024
 
 
@@ -63,13 +63,16 @@
 def attend_kernel(
     lengths,
     slots,
+    parity_ref,
     q_any,
     nk_any,
     nv_any,
     k_any,
     v_any,
     codes_any,
+    weight_any,
     out_ref,
+    give_ref,
     q_ref,
     nk_ref,
     nv_ref,
@@ -86,6 +89,7 @@
     feature_rows,
 ):
     rows, width = q_ref.shape
+    give_columns = give_ref.shape[1]
     small = [
         pltpu.make_async_copy(source, target, sems.at[at])
         for at, (source, target) in enumerate(
@@ -101,6 +105,10 @@
             for r in range(rows)
         ]
         for source, target, base in ((k_any, k_ref, 4), (v_any, v_ref, 4 + rows))
+    )
+    begin = pl.multiple_of((1 - parity_ref[0]) * give_columns, LANES)
+    give = pltpu.make_async_copy(
+        weight_any.at[:, pl.ds(begin, give_columns)], give_ref, sems.at[4 + 2 * rows]
     )
     for copy in small:
         copy.start()
@@ -159,6 +167,7 @@
     for copy in keys:
         copy.wait()
     products = jnp.dot(k_ref[...], spread[...], preferred_element_type=jnp.float32) * factor
+    give.start()
     own_scores = products[known:]
     scores = products[:known]
     owner = column // heads
@@ -193,6 +202,7 @@
                     r * heads + head : r * heads + head + 1, head * LANES : (head + 1) * LANES
                 ]
     out_ref[...] = msg[...].astype(jnp.bfloat16)
+    give.wait()
 
 
 def project_kernel(
@@ -230,10 +240,8 @@
     first, second = lhs[:, :share], lhs[:, share:]
     own = jnp.where(even, first, second).astype(jnp.bfloat16)
     other = jnp.where(even, second, first).astype(jnp.bfloat16)
-    half = own_ref.shape[1]
-    begin = pl.multiple_of(parity_ref[0] * half, LANES)
     product = jnp.dot(own, own_ref[...], preferred_element_type=jnp.float32) + jnp.dot(
-        other, other_ref[:, pl.ds(begin, half)], preferred_element_type=jnp.float32
+        other, other_ref[...], preferred_element_type=jnp.float32
     )
     for row in range(rows):
         for group in range(groups):
@@ -299,8 +307,19 @@
 
 
 def decode_kernel(
-    section_ref, in_ref, fold_ref, early_ref, two_any, out_ref, late_ref, sems, *, feature_rows
+    section_ref,
+    in_ref,
+    fold_ref,
+    early_ref,
+    two_any,
+    after_ref,
+    out_ref,
+    late_ref,
+    sems,
+    *,
+    feature_rows,
 ):
+    del after_ref
     copies = [
         pltpu.make_async_copy(two_any.at[dr, dc], late_ref.at[at], sems.at[at])
         for at, (dr, dc) in enumerate(TAPS[EARLY:])
@@ -365,8 +384,9 @@
     column = lax.broadcasted_iota(jnp.int32, (count, 1), 0) % IMG_W
     summed = part = None
     for at, (dr, dc) in enumerate(TAPS):
-        if at >= EARLY:
-            copies[at - EARLY].wait()
+        if at == EARLY:
+            for copy in copies:
+                copy.wait()
         weight = early_ref[at] if at < EARLY else late_ref[at - EARLY]
         term = jnp.dot(
             activated[dr * IMG_W : dr * IMG_W + count], weight, preferred_element_type=jnp.float32
@@ -422,11 +442,14 @@
     anywhere = pl.BlockSpec(memory_space=pl.ANY)
     parity = (place % 2).reshape(1).astype(jnp.int32)
 
-    outgoing = pl.pallas_call(
+    outgoing, give = pl.pallas_call(
         functools.partial(attend_kernel, tiles=tiles, per=per, feature_rows=feature_rows),
-        in_specs=[smem] * 2 + [anywhere] * 6,
-        out_specs=vmem,
-        out_shape=jax.ShapeDtypeStruct((tiles, depth, LANES), jnp.bfloat16),
+        in_specs=[smem] * 3 + [anywhere] * 7,
+        out_specs=[vmem, vmem],
+        out_shape=[
+            pltpu.VMEM((tiles, depth, LANES), jnp.bfloat16),
+            pltpu.VMEM((share, half), out_weight.dtype),
+        ],
         scratch_shapes=[
             pltpu.VMEM(queries.shape, queries.dtype),
             pltpu.VMEM(new_keys.shape, new_keys.dtype),
@@ -437,24 +460,26 @@
             pltpu.VMEM((tiles, depth, LANES), jnp.float32),
             pltpu.VMEM((LANES, LANES), jnp.float32),
             pltpu.VMEM((width, LANES), jnp.bfloat16),
-            pltpu.SemaphoreType.DMA((4 + 2 * rows,)),
+            pltpu.SemaphoreType.DMA((5 + 2 * rows,)),
         ],
         compiler_params=pltpu.CompilerParams(vmem_limit_bytes=56 * 1024 * 1024),
     )(
         cache_lengths,
         tile_slot,
+        parity,
         far(queries),
         far(new_keys),
         far(new_values),
         far(cache_keys),
         far(cache_values),
         far(codes),
+        far(out_weight),
     )
     order = [[member(at, tiles) for at in range(tiles)]]
     incoming = lax.all_to_all(
         outgoing, "rows", split_axis=0, concat_axis=0, axis_index_groups=order, tiled=True
     )
-    other = lax.ppermute(out_weight, "rows", [(i, i ^ 1) for i in range(tiles)])
+    other = lax.ppermute(give, "rows", [(i, i ^ 1) for i in range(tiles)])
 
     folded, own = pl.pallas_call(
         fold_kernel,
@@ -479,7 +504,7 @@
         in_specs=[smem, vmem, vmem, vmem, anywhere],
         out_specs=[vmem, vmem],
         out_shape=[
-            jax.ShapeDtypeStruct((tiles, groups, rows * lines, LANES), jnp.bfloat16),
+            pltpu.VMEM((tiles, groups, rows * lines, LANES), jnp.bfloat16),
             pltpu.VMEM((EARLY,) + conv_two.shape[2:], conv_two.dtype),
         ],
         scratch_shapes=[
@@ -496,7 +521,7 @@
     section = (place + IMG_SPLIT // 2) % tiles % IMG_SPLIT
     decoded = pl.pallas_call(
         functools.partial(decode_kernel, feature_rows=feature_rows),
-        in_specs=[smem, vmem, vmem, vmem, anywhere],
+        in_specs=[smem, vmem, vmem, vmem, anywhere, anywhere],
         out_specs=vmem,
         out_shape=jax.ShapeDtypeStruct((TILE_H * IMG_W, channels), jnp.bfloat16),
         scratch_shapes=[
@@ -504,7 +529,7 @@
             pltpu.SemaphoreType.DMA((len(TAPS) - EARLY,)),
         ],
         compiler_params=params,
-    )(section.reshape(1).astype(jnp.int32), near(incoming), near(folded), near(early), far(conv_two))
+    )(section.reshape(1).astype(jnp.int32), near(incoming), near(folded), near(early), far(conv_two), near(partials))
 
     mixed = pl.pallas_call(
         functools.partial(total_kernel, rows=rows),

time: 34.4 us -> 32.7 us (0.951)
  local copies, waits for them, and re-layouts: 4.43 us -> 2.18 us
  waiting for transfers between devices: 0.04 us -> 1.22 us
  Pallas kernels: 15.6 us -> 14.9 us
    unnamed x8 -> x4, local copies, waits for them, and re-layouts: 4.43 us -> 2.18 us
    pallas_call x1, Pallas kernels: 5.83 us -> 4.44 us  [on_device(): pl.pallas_call(functools.partial(decode_kernel, feature_rows=feature_rows...]
    all_to_all x1, waiting for transfers between devices: 0.01 us -> 1.21 us  [on_device(): lax.all_to_all(partials, 'rows', split_axis=0, concat_axis=0, axis_index_...]
    pallas_call x1, Pallas kernels: 1.59 us -> 2.18 us  [on_device(): pl.pallas_call(functools.partial(project_kernel, rows=rows, per=per), in_...]
  transfers between devices with their start and end apart: 3 -> 3, of which waited for: 0 -> 1; matrix products, arithmetic and copies ran while one was open for 0% -> 0% of each run, Pallas kernels for 39% -> 25%
where the time goes in v4:
time: 32.7 us; the launch traced here: 32.2 us
  Pallas kernels  14.9 us (46%)
  starting transfers between devices  13.2 us (40%)
  local copies, waits for them, and re-layouts  2.18 us (7%)
  waiting for transfers between devices  1.22 us (4%)
  between operations  0.69 us (2%)
    all_to_all x1, starting transfers between devices, on_device(): lax.all_to_all(outgoing, 'rows', split_axis=0, concat_axis=0, axis_index_...  7.52 us
    all_to_all x1, starting transfers between devices, on_device(): lax.all_to_all(partials, 'rows', split_axis=0, concat_axis=0, axis_index_...  5.13 us
    pallas_call x1, Pallas kernels, on_device(): pl.pallas_call(functools.partial(decode_kernel, feature_rows=feature_rows...  4.44 us
    pallas_call x1, Pallas kernels, on_device(): pl.pallas_call(functools.partial(attend_kernel, tiles=tiles, per=per, fea...  3.95 us
    pallas_call x1, Pallas kernels, on_device(): pl.pallas_call(fold_kernel, in_specs=[smem, vmem, anywhere, anywhere, any...  3.71 us
    pallas_call x1, Pallas kernels, on_device(): pl.pallas_call(functools.partial(project_kernel, rows=rows, per=per), in_...  2.18 us
    unnamed x4, local copies, waits for them, and re-layouts  2.18 us
    all_to_all x1, waiting for transfers between devices, on_device(): lax.all_to_all(partials, 'rows', split_axis=0, concat_axis=0, axis_index_...  1.21 us
  transfers between devices with their start and end apart: 3, of which 1 were waited for; matrix products, arithmetic and copies ran while one was open for 0% of the time, Pallas kernels for 25%

profile of v4, /device:TPU:0, one launch (start us, length us, event | category | flops | bytes accessed | tf_op | source)
XLA Modules:
  0.0 32.2 jit_solution(16484119786293219011)
XLA Ops:
  0.6 4.0 %shard_map.131 = (bf16[16,16,128]{2,1,0:T(8,128)(2,1)}, bf16[256,2048]{1,0:T(8,128)(2,1)S(1)}) custom-call(s32[2]{0:T(128)} %lengths.1, s32[2]{0:T(128)} %slots.1, s32[1]{0:T(128)} %bitcast.parity_ref, bf16[2,4096]{1,0:T(2,128)(2,1)} %q_any.1, bf16[2,4096]{1,0:T(2,128)(2,1)} %nk_any.1, bf16[2,4096]{1,0:T(2,128)(2,1)} %nv_any.1, bf16[2,64,4096]{2,1,0:T(8,128)(2,1)} %k_any.1, ...), custom_call_target="tpu_custom_call" | custom-call | tf_op jit(solution)/shard_map/pallas_call | solution.py:445
  4.6 0.5 %collective-permute-start = (bf16[256,2048]{1,0:T(8,128)(2,1)S(1)}, bf16[256,2048]{1,0:T(8,128)(2,1)S(1)}, u32[]{:S(2)}, u32[]{:S(2)}) collective-permute-start(bf16[256,2048]{1,0:T(8,128)(2,1)S(1)} %get-tuple-element.10), channel_id=1, source_target_pairs={{0,1},{1,0},{2,3},{3,2},{4,5},{5,4},{6,7},{7,6},{8,9},{9,8},{10,11... | collective-permute-start | bytes 3145736 | tf_op jit(solution)/shard_map/ppermute | solution.py:482
  5.1 7.5 %all-to-all-start = ((bf16[16,16,128]{2,1,0:T(8,128)(2,1)}), bf16[16,16,128]{2,1,0:T(8,128)(2,1)S(1)}, u32[]{:S(2)}, u32[]{:S(2)}) async-start(bf16[16,16,128]{2,1,0:T(8,128)(2,1)} %get-tuple-element.8.after_ref), calls=%async_computation | async-start | bytes 131072 | tf_op jit(solution)/shard_map/all_to_all | solution.py:479
  12.6 3.7 %shard_map.132 = (bf16[256,512]{1,0:T(8,128)(2,1)S(1)}, bf16[256,2048]{1,0:T(8,128)(2,1)S(1)}) custom-call(s32[1]{0:T(128)} %bitcast.parity_ref, f32[5,512]{1,0:T(8,128)} %cw_ref.1, bf16[3,3,512,512]{3,2,1,0:T(8,128)(2,1)} %conv_ref.1, bf16[256,4096]{1,0:T(8,128)(2,1)} %weight_ref.1, bf16[16,16,128]{2,1,0:T(8,128)(2,1)} %get-tuple-element.8.after_ref), custom_call_target="tpu_custom_call" | custom-call | tf_op jit(solution)/shard_map/pallas_call | solution.py:484
  16.4 0.0 copy-start
  16.4 1.0 %copy-done = bf16[256,2048]{1,0:T(8,128)(2,1)} copy-done((bf16[256,2048]{1,0:T(8,128)(2,1)}, bf16[256,2048]{1,0:T(8,128)(2,1)S(1)}, u32[]{:S(2)}) %copy-start) | copy-done | bytes 1048600
  17.3 0.0 all-to-all-done.in_ref
  17.3 0.0 collective-permute-done.other_ref
  17.3 0.0 copy-start.1
  17.3 1.2 %copy-done.1 = bf16[256,2048]{1,0:T(8,128)(2,1)S(1)} copy-done((bf16[256,2048]{1,0:T(8,128)(2,1)S(1)}, bf16[256,2048]{1,0:T(8,128)(2,1)}, u32[]{:S(2)}) %copy-start.1) | copy-done | bytes 1048600
  18.6 2.2 %shard_map.133 = (bf16[16,2,16,128]{3,2,1,0:T(8,128)(2,1)}, bf16[3,512,512]{2,1,0:T(8,128)(2,1)S(1)}) custom-call(s32[1]{0:T(128)} %bitcast.parity_ref, bf16[16,16,128]{2,1,0:T(8,128)(2,1)S(1)} %all-to-all-done.in_ref, bf16[256,2048]{1,0:T(8,128)(2,1)S(1)} %copy-done.1, bf16[256,2048]{1,0:T(8,128)(2,1)S(1)} %collective-permute-done.other_ref, ...), custom_call_target="tpu_custom_call" | custom-call | tf_op jit(solution)/shard_map/pallas_call | solution.py:502
  20.7 5.1 %all-to-all-start.1 = ((bf16[16,2,16,128]{3,2,1,0:T(8,128)(2,1)}), bf16[16,2,16,128]{3,2,1,0:T(8,128)(2,1)S(1)}, u32[]{:S(2)}, u32[]{:S(2)}) async-start(bf16[16,2,16,128]{3,2,1,0:T(8,128)(2,1)} %get-tuple-element.11.after_ref), calls=%async_computation.1 | async-start | bytes 262144 | tf_op jit(solution)/shard_map/all_to_all | solution.py:517
  25.9 4.4 %shard_map.135 = bf16[384,512]{1,0:T(8,128)(2,1)} custom-call(s32[1]{0:T(128)} %bitcast.1.section_ref, bf16[16,16,128]{2,1,0:T(8,128)(2,1)S(1)} %all-to-all-done.in_ref, bf16[256,512]{1,0:T(8,128)(2,1)S(1)} %get-tuple-element.12.fold_ref, bf16[3,512,512]{2,1,0:T(8,128)(2,1)S(1)} %get-tuple-element.13.early_ref, bf16[3,3,512,512]{3,2,1,0:T(8,128)(2,1)} %two_any.3, ...), custom_call_target="tpu_custom_call" | custom-call | tf_op jit(solution)/shard_map/pallas_call | solution.py:522
  30.3 1.2 %all-to-all-done.1.in_ref = bf16[16,2,16,128]{3,2,1,0:T(8,128)(2,1)S(1)} async-done(((bf16[16,2,16,128]{3,2,1,0:T(8,128)(2,1)}), bf16[16,2,16,128]{3,2,1,0:T(8,128)(2,1)S(1)}, u32[]{:S(2)}, u32[]{:S(2)}) %all-to-all-start.1) | async-done | bytes 131104 | tf_op jit(solution)/shard_map/all_to_all | solution.py:517
  31.5 0.6 %shard_map.134 = bf16[2,4096]{1,0:T(2,128)(2,1)} custom-call(bf16[16,2,16,128]{3,2,1,0:T(8,128)(2,1)S(1)} %all-to-all-done.1.in_ref), custom_call_target="tpu_custom_call" | custom-call | tf_op jit(solution)/shard_map/pallas_call | solution.py:534
Async XLA Ops:
  4.6 12.7 %collective-permute-start = (bf16[256,2048]{1,0:T(8,128)(2,1)S(1)}, bf16[256,2048]{1,0:T(8,128)(2,1)S(1)}, u32[]{:S(2)}, u32[]{:S(2)}) collective-permute-start(bf16[256,2048]{1,0:T(8,128)(2,1)S(1)} %get-tuple-element.10), channel_id=1, source_target_pairs={{0,1},{1,0},{2,3},{3,2},{4,5},{5,4},{6,7},{7,6},{8,9},{9,8},{10,11... | collective-permute-start | bytes 3145736 | tf_op jit(solution)/shard_map/ppermute | solution.py:482
  5.1 12.2 %all-to-all-start = ((bf16[16,16,128]{2,1,0:T(8,128)(2,1)}), bf16[16,16,128]{2,1,0:T(8,128)(2,1)S(1)}, u32[]{:S(2)}, u32[]{:S(2)}) async-start(bf16[16,16,128]{2,1,0:T(8,128)(2,1)} %get-tuple-element.8.after_ref), calls=%async_computation | async-start | bytes 131072 | tf_op jit(solution)/shard_map/all_to_all | solution.py:479
  16.4 1.0 %copy-start = (bf16[256,2048]{1,0:T(8,128)(2,1)}, bf16[256,2048]{1,0:T(8,128)(2,1)S(1)}, u32[]{:S(2)}) copy-start(bf16[256,2048]{1,0:T(8,128)(2,1)S(1)} %get-tuple-element.9.own_ref) | copy-start | bytes 3145732
  17.3 1.2 %copy-start.1 = (bf16[256,2048]{1,0:T(8,128)(2,1)S(1)}, bf16[256,2048]{1,0:T(8,128)(2,1)}, u32[]{:S(2)}) copy-start(bf16[256,2048]{1,0:T(8,128)(2,1)} %copy-done) | copy-start | bytes 3145732
  20.7 10.8 %all-to-all-start.1 = ((bf16[16,2,16,128]{3,2,1,0:T(8,128)(2,1)}), bf16[16,2,16,128]{3,2,1,0:T(8,128)(2,1)S(1)}, u32[]{:S(2)}, u32[]{:S(2)}) async-start(bf16[16,2,16,128]{3,2,1,0:T(8,128)(2,1)} %get-tuple-element.11.after_ref), calls=%async_computation.1 | async-start | bytes 262144 | tf_op jit(solution)/shard_map/all_to_all | solution.py:517

commit v5 on v4

--- a/solution.py
+++ b/solution.py
@@ -24,7 +24,6 @@
 FOLD_ROWS = 256
 TAPS = [(dr, dc) for dc in (1, 0, 2) for dr in range(3)]
 EARLY = 3
-VMEM_LIMIT = 24 * 1024 * 1024
 
 
 def window_start(section):
@@ -403,6 +402,10 @@
     out_ref[...] = summed.astype(jnp.bfloat16)
 
 
+def limit(mebibytes):
+    return pltpu.CompilerParams(vmem_limit_bytes=mebibytes * 1024 * 1024)
+
+
 def near(array):
     return pltpu.with_memory_space_constraint(array, pltpu.VMEM)
 
@@ -436,7 +439,6 @@
     half = width // 2
     lines = 8
     groups = half // (lines * LANES)
-    params = pltpu.CompilerParams(vmem_limit_bytes=VMEM_LIMIT)
     smem = pl.BlockSpec(memory_space=pltpu.SMEM)
     vmem = pl.BlockSpec(memory_space=pltpu.VMEM)
     anywhere = pl.BlockSpec(memory_space=pl.ANY)
@@ -462,7 +464,7 @@
             pltpu.VMEM((width, LANES), jnp.bfloat16),
             pltpu.SemaphoreType.DMA((5 + 2 * rows,)),
         ],
-        compiler_params=pltpu.CompilerParams(vmem_limit_bytes=56 * 1024 * 1024),
+        compiler_params=limit(56),
     )(
         cache_lengths,
         tile_slot,
@@ -496,7 +498,7 @@
             pltpu.SemaphoreType.DMA((9,)),
             pltpu.SemaphoreType.DMA,
         ],
-        compiler_params=params,
+        compiler_params=limit(12),
     )(parity, far(code_weight), far(conv_one), far(out_weight), near(outgoing))
 
     partials, early = pl.pallas_call(
@@ -512,7 +514,7 @@
             pltpu.VMEM((groups, tiles * rows * lines, LANES), jnp.float32),
             pltpu.SemaphoreType.DMA((EARLY,)),
         ],
-        compiler_params=params,
+        compiler_params=limit(8),
     )(parity, near(incoming), near(own), near(other), far(conv_two))
     gathered = lax.all_to_all(
         partials, "rows", split_axis=0, concat_axis=0, axis_index_groups=order, tiled=True
@@ -528,7 +530,7 @@
             pltpu.VMEM((len(TAPS) - EARLY,) + conv_two.shape[2:], conv_two.dtype),
             pltpu.SemaphoreType.DMA((len(TAPS) - EARLY,)),
         ],
-        compiler_params=params,
+        compiler_params=limit(16),
     )(section.reshape(1).astype(jnp.int32), near(incoming), near(folded), near(early), far(conv_two), near(partials))
 
     mixed = pl.pallas_call(
@@ -536,7 +538,7 @@
         in_specs=[vmem],
         out_shape=jax.ShapeDtypeStruct((rows, width), jnp.bfloat16),
         scratch_shapes=[pltpu.VMEM((2 * groups, rows * lines, LANES), jnp.float32)],
-        compiler_params=params,
+        compiler_params=limit(8),
     )(near(gathered))
     return (mixed, decoded.reshape(TILE_H, IMG_W, channels))
 

time: 32.7 us -> 32.7 us (level)
  no operation moved by 1% of the time
where the time goes in v5:
time: 32.7 us; the launch traced here: 32.2 us
  Pallas kernels  14.9 us (46%)
  starting transfers between devices  13.2 us (40%)
  local copies, waits for them, and re-layouts  2.18 us (7%)
  waiting for transfers between devices  1.22 us (4%)
  between operations  0.69 us (2%)
    all_to_all x1, starting transfers between devices, on_device(): lax.all_to_all(outgoing, 'rows', split_axis=0, concat_axis=0, axis_index_...  7.52 us
    all_to_all x1, starting transfers between devices, on_device(): lax.all_to_all(partials, 'rows', split_axis=0, concat_axis=0, axis_index_...  5.13 us
    pallas_call x1, Pallas kernels, on_device(): pl.pallas_call(functools.partial(decode_kernel, feature_rows=feature_rows...  4.44 us
    pallas_call x1, Pallas kernels, on_device(): pl.pallas_call(functools.partial(attend_kernel, tiles=tiles, per=per, fea...  3.95 us
    pallas_call x1, Pallas kernels, on_device(): pl.pallas_call(fold_kernel, in_specs=[smem, vmem, anywhere, anywhere, any...  3.71 us
    pallas_call x1, Pallas kernels, on_device(): pl.pallas_call(functools.partial(project_kernel, rows=rows, per=per), in_...  2.18 us
    unnamed x4, local copies, waits for them, and re-layouts  2.18 us
    all_to_all x1, waiting for transfers between devices, on_device(): lax.all_to_all(partials, 'rows', split_axis=0, concat_axis=0, axis_index_...  1.21 us
  transfers between devices with their start and end apart: 3, of which 1 were waited for; matrix products, arithmetic and copies ran while one was open for 0% of the time, Pallas kernels for 25%

profile of v5, /device:TPU:0, one launch (start us, length us, event | category | flops | bytes accessed | tf_op | source)
XLA Modules:
  0.0 32.2 jit_solution(16024802130871428278)
XLA Ops:
  0.6 4.0 %shard_map.131 = (bf16[16,16,128]{2,1,0:T(8,128)(2,1)}, bf16[256,2048]{1,0:T(8,128)(2,1)S(1)}) custom-call(s32[2]{0:T(128)} %lengths.1, s32[2]{0:T(128)} %slots.1, s32[1]{0:T(128)} %bitcast.parity_ref, bf16[2,4096]{1,0:T(2,128)(2,1)} %q_any.1, bf16[2,4096]{1,0:T(2,128)(2,1)} %nk_any.1, bf16[2,4096]{1,0:T(2,128)(2,1)} %nv_any.1, bf16[2,64,4096]{2,1,0:T(8,128)(2,1)} %k_any.1, ...), custom_call_target="tpu_custom_call" | custom-call | tf_op jit(solution)/shard_map/pallas_call | solution.py:447
  4.6 0.5 %collective-permute-start = (bf16[256,2048]{1,0:T(8,128)(2,1)S(1)}, bf16[256,2048]{1,0:T(8,128)(2,1)S(1)}, u32[]{:S(2)}, u32[]{:S(2)}) collective-permute-start(bf16[256,2048]{1,0:T(8,128)(2,1)S(1)} %get-tuple-element.10), channel_id=1, source_target_pairs={{0,1},{1,0},{2,3},{3,2},{4,5},{5,4},{6,7},{7,6},{8,9},{9,8},{10,11... | collective-permute-start | bytes 3145736 | tf_op jit(solution)/shard_map/ppermute | solution.py:484
  5.1 7.5 %all-to-all-start = ((bf16[16,16,128]{2,1,0:T(8,128)(2,1)}), bf16[16,16,128]{2,1,0:T(8,128)(2,1)S(1)}, u32[]{:S(2)}, u32[]{:S(2)}) async-start(bf16[16,16,128]{2,1,0:T(8,128)(2,1)} %get-tuple-element.8.after_ref), calls=%async_computation | async-start | bytes 131072 | tf_op jit(solution)/shard_map/all_to_all | solution.py:481
  12.6 3.7 %shard_map.132 = (bf16[256,512]{1,0:T(8,128)(2,1)S(1)}, bf16[256,2048]{1,0:T(8,128)(2,1)S(1)}) custom-call(s32[1]{0:T(128)} %bitcast.parity_ref, f32[5,512]{1,0:T(8,128)} %cw_ref.1, bf16[3,3,512,512]{3,2,1,0:T(8,128)(2,1)} %conv_ref.1, bf16[256,4096]{1,0:T(8,128)(2,1)} %weight_ref.1, bf16[16,16,128]{2,1,0:T(8,128)(2,1)} %get-tuple-element.8.after_ref), custom_call_target="tpu_custom_call" | custom-call | tf_op jit(solution)/shard_map/pallas_call | solution.py:486
  16.4 0.0 copy-start
  16.4 1.0 %copy-done = bf16[256,2048]{1,0:T(8,128)(2,1)} copy-done((bf16[256,2048]{1,0:T(8,128)(2,1)}, bf16[256,2048]{1,0:T(8,128)(2,1)S(1)}, u32[]{:S(2)}) %copy-start) | copy-done | bytes 1048600
  17.3 0.0 all-to-all-done.in_ref
  17.3 0.0 collective-permute-done.other_ref
  17.3 0.0 copy-start.1
  17.3 1.2 %copy-done.1 = bf16[256,2048]{1,0:T(8,128)(2,1)S(1)} copy-done((bf16[256,2048]{1,0:T(8,128)(2,1)S(1)}, bf16[256,2048]{1,0:T(8,128)(2,1)}, u32[]{:S(2)}) %copy-start.1) | copy-done | bytes 1048600
  18.6 2.2 %shard_map.133 = (bf16[16,2,16,128]{3,2,1,0:T(8,128)(2,1)}, bf16[3,512,512]{2,1,0:T(8,128)(2,1)S(1)}) custom-call(s32[1]{0:T(128)} %bitcast.parity_ref, bf16[16,16,128]{2,1,0:T(8,128)(2,1)S(1)} %all-to-all-done.in_ref, bf16[256,2048]{1,0:T(8,128)(2,1)S(1)} %copy-done.1, bf16[256,2048]{1,0:T(8,128)(2,1)S(1)} %collective-permute-done.other_ref, ...), custom_call_target="tpu_custom_call" | custom-call | tf_op jit(solution)/shard_map/pallas_call | solution.py:504
  20.7 5.1 %all-to-all-start.1 = ((bf16[16,2,16,128]{3,2,1,0:T(8,128)(2,1)}), bf16[16,2,16,128]{3,2,1,0:T(8,128)(2,1)S(1)}, u32[]{:S(2)}, u32[]{:S(2)}) async-start(bf16[16,2,16,128]{3,2,1,0:T(8,128)(2,1)} %get-tuple-element.11.after_ref), calls=%async_computation.1 | async-start | bytes 262144 | tf_op jit(solution)/shard_map/all_to_all | solution.py:519
  25.9 4.4 %shard_map.135 = bf16[384,512]{1,0:T(8,128)(2,1)} custom-call(s32[1]{0:T(128)} %bitcast.1.section_ref, bf16[16,16,128]{2,1,0:T(8,128)(2,1)S(1)} %all-to-all-done.in_ref, bf16[256,512]{1,0:T(8,128)(2,1)S(1)} %get-tuple-element.12.fold_ref, bf16[3,512,512]{2,1,0:T(8,128)(2,1)S(1)} %get-tuple-element.13.early_ref, bf16[3,3,512,512]{3,2,1,0:T(8,128)(2,1)} %two_any.3, ...), custom_call_target="tpu_custom_call" | custom-call | tf_op jit(solution)/shard_map/pallas_call | solution.py:524
  30.3 1.2 %all-to-all-done.1.in_ref = bf16[16,2,16,128]{3,2,1,0:T(8,128)(2,1)S(1)} async-done(((bf16[16,2,16,128]{3,2,1,0:T(8,128)(2,1)}), bf16[16,2,16,128]{3,2,1,0:T(8,128)(2,1)S(1)}, u32[]{:S(2)}, u32[]{:S(2)}) %all-to-all-start.1) | async-done | bytes 131104 | tf_op jit(solution)/shard_map/all_to_all | solution.py:519
  31.5 0.6 %shard_map.134 = bf16[2,4096]{1,0:T(2,128)(2,1)} custom-call(bf16[16,2,16,128]{3,2,1,0:T(8,128)(2,1)S(1)} %all-to-all-done.1.in_ref), custom_call_target="tpu_custom_call" | custom-call | tf_op jit(solution)/shard_map/pallas_call | solution.py:536
Async XLA Ops:
  4.6 12.7 %collective-permute-start = (bf16[256,2048]{1,0:T(8,128)(2,1)S(1)}, bf16[256,2048]{1,0:T(8,128)(2,1)S(1)}, u32[]{:S(2)}, u32[]{:S(2)}) collective-permute-start(bf16[256,2048]{1,0:T(8,128)(2,1)S(1)} %get-tuple-element.10), channel_id=1, source_target_pairs={{0,1},{1,0},{2,3},{3,2},{4,5},{5,4},{6,7},{7,6},{8,9},{9,8},{10,11... | collective-permute-start | bytes 3145736 | tf_op jit(solution)/shard_map/ppermute | solution.py:484
  5.1 12.2 %all-to-all-start = ((bf16[16,16,128]{2,1,0:T(8,128)(2,1)}), bf16[16,16,128]{2,1,0:T(8,128)(2,1)S(1)}, u32[]{:S(2)}, u32[]{:S(2)}) async-start(bf16[16,16,128]{2,1,0:T(8,128)(2,1)} %get-tuple-element.8.after_ref), calls=%async_computation | async-start | bytes 131072 | tf_op jit(solution)/shard_map/all_to_all | solution.py:481
  16.4 1.0 %copy-start = (bf16[256,2048]{1,0:T(8,128)(2,1)}, bf16[256,2048]{1,0:T(8,128)(2,1)S(1)}, u32[]{:S(2)}) copy-start(bf16[256,2048]{1,0:T(8,128)(2,1)S(1)} %get-tuple-element.9.own_ref) | copy-start | bytes 3145732
  17.3 1.2 %copy-start.1 = (bf16[256,2048]{1,0:T(8,128)(2,1)S(1)}, bf16[256,2048]{1,0:T(8,128)(2,1)}, u32[]{:S(2)}) copy-start(bf16[256,2048]{1,0:T(8,128)(2,1)} %copy-done) | copy-start | bytes 3145732
  20.7 10.8 %all-to-all-start.1 = ((bf16[16,2,16,128]{3,2,1,0:T(8,128)(2,1)}), bf16[16,2,16,128]{3,2,1,0:T(8,128)(2,1)S(1)}, u32[]{:S(2)}, u32[]{:S(2)}) async-start(bf16[16,2,16,128]{3,2,1,0:T(8,128)(2,1)} %get-tuple-element.11.after_ref), calls=%async_computation.1 | async-start | bytes 262144 | tf_op jit(solution)/shard_map/all_to_all | solution.py:519

commit v6 on v2

--- a/solution.py
+++ b/solution.py
@@ -22,6 +22,8 @@
 CODE_ROWS = WINDOW * PIECES
 TAP_ROWS = 24
 FOLD_ROWS = 256
+TAPS = [(dr, dc) for dc in (1, 0, 2) for dr in range(3)]
+EARLY = 3
 VMEM_LIMIT = 24 * 1024 * 1024
 
 
@@ -59,9 +61,8 @@
 
 
 def attend_kernel(
-    lengths,
-    slots,
-    parity_ref,
+    lengths_any,
+    slots_any,
     q_any,
     nk_any,
     nv_any,
@@ -80,6 +81,8 @@
     msg,
     by_head,
     spread,
+    lengths,
+    slots,
     sems,
     *,
     tiles,
@@ -91,7 +94,14 @@
     small = [
         pltpu.make_async_copy(source, target, sems.at[at])
         for at, (source, target) in enumerate(
-            ((q_any, q_ref), (nk_any, nk_ref), (nv_any, nv_ref), (codes_any, codes_ref))
+            (
+                (q_any, q_ref),
+                (nk_any, nk_ref),
+                (nv_any, nv_ref),
+                (codes_any, codes_ref),
+                (lengths_any, lengths),
+                (slots_any, slots),
+            )
         )
     ]
     cached = k_any.shape[1]
@@ -102,15 +112,15 @@
             )
             for r in range(rows)
         ]
-        for source, target, base in ((k_any, k_ref, 4), (v_any, v_ref, 4 + rows))
-    )
-    begin = pl.multiple_of((1 - parity_ref[0]) * give_columns, LANES)
+        for source, target, base in ((k_any, k_ref, 6), (v_any, v_ref, 6 + rows))
+    )
+    begin = pl.multiple_of((1 - lax.axis_index("rows") % 2) * give_columns, LANES)
     give = pltpu.make_async_copy(
-        weight_any.at[:, pl.ds(begin, give_columns)], give_ref, sems.at[4 + 2 * rows]
+        weight_any.at[:, pl.ds(begin, give_columns)], give_ref, sems.at[6 + 2 * rows]
     )
     for copy in small:
         copy.start()
-    for copy in keys + values:
+    for copy in keys:
         copy.start()
 
     heads = width // HEAD_DIM
@@ -160,6 +170,8 @@
         jnp.bfloat16
     )
     new_values = jnp.concatenate([nv_ref[...].astype(jnp.float32), padding], 0).astype(jnp.bfloat16)
+    for copy in values:
+        copy.start()
     for copy in keys:
         copy.wait()
     products = jnp.dot(k_ref[...], spread[...], preferred_element_type=jnp.float32) * factor
@@ -201,7 +213,7 @@
     give.wait()
 
 
-def project_kernel(parity_ref, in_ref, own_ref, other_ref, out_ref, held, total, *, rows, per):
+def project_kernel(in_ref, own_ref, other_ref, out_ref, held, total, *, rows, per):
     tiles, depth = in_ref.shape[:2]
     held[...] = in_ref[...].astype(jnp.float32).reshape(held.shape)
     groups = total.shape[0]
@@ -212,7 +224,7 @@
         parts = [held[pl.ds(row * per + j, tiles, stride=depth), :] for j in range(per)]
         lhs.append(jnp.concatenate(parts, 1))
     lhs = jnp.concatenate(lhs, 0)
-    even = parity_ref[0] == 0
+    even = lax.axis_index("rows") % 2 == 0
     first, second = lhs[:, :share], lhs[:, share:]
     own = jnp.where(even, first, second).astype(jnp.bfloat16)
     other = jnp.where(even, second, first).astype(jnp.bfloat16)
@@ -252,7 +264,7 @@
 
 
 def fold_kernel(
-    parity_ref, cw_ref, conv_ref, weight_ref, after_ref, out_ref, near_ref, levels_w, folded, held, sems, near_sem
+    cw_ref, conv_ref, weight_ref, after_ref, out_ref, near_ref, levels_w, folded, held, sems, near_sem
 ):
     del after_ref
     taps = [(dr, dc) for dr in range(3) for dc in range(3)]
@@ -262,7 +274,7 @@
     ]
     for copy in copies:
         copy.start()
-    begin = pl.multiple_of(parity_ref[0] * near_ref.shape[1], LANES)
+    begin = pl.multiple_of(lax.axis_index("rows") % 2 * near_ref.shape[1], LANES)
     bring = pltpu.make_async_copy(
         weight_ref.at[:, pl.ds(begin, near_ref.shape[1])], near_ref, near_sem
     )
@@ -281,17 +293,17 @@
 
 
 def decode_kernel(
-    section_ref, in_ref, fold_ref, two_any, after_ref, out_ref, two_ref, sems, *, feature_rows
+    in_ref, fold_ref, two_any, after_ref, out_ref, two_ref, sems, *, feature_rows
 ):
     del after_ref
-    copies = {}
-    for dc in (1, 0, 2):
-        for dr in range(3):
-            copies[dr, dc] = pltpu.make_async_copy(
-                two_any.at[dr, dc], two_ref.at[dr, dc], sems.at[dr, dc]
-            )
-            copies[dr, dc].start()
-    section = section_ref[0]
+    copies = [
+        pltpu.make_async_copy(two_any.at[dr, dc], two_ref.at[at], sems.at[at])
+        for at, (dr, dc) in enumerate(TAPS)
+    ]
+    for copy in copies[:EARLY]:
+        copy.start()
+    tiles = lax.axis_size("rows")
+    section = (lax.axis_index("rows") + IMG_SPLIT // 2) % tiles % IMG_SPLIT
     got = jnp.sum(in_ref[...].astype(jnp.float32), 0)
     pieces = []
     for at in range(PIECES):
@@ -325,6 +337,8 @@
     placed = lax.dot_general(
         chooser, value, (((1,), (1,)), ((), ())), preferred_element_type=jnp.float32
     )
+    for copy in copies[EARLY:]:
+        copy.start()
     column = spot % IMG_W
     moved = [
         jnp.where(column == 0, 0.0, pltpu.roll(placed, 1, 0)),
@@ -347,22 +361,28 @@
 
     count = count - 2 * IMG_W
     column = lax.broadcasted_iota(jnp.int32, (count, 1), 0) % IMG_W
-    summed = None
-    for dc in (1, 0, 2):
-        part = None
-        for dr in range(3):
-            copies[dr, dc].wait()
-            term = jnp.dot(
-                activated[dr * IMG_W : dr * IMG_W + count],
-                two_ref[dr, dc],
-                preferred_element_type=jnp.float32,
-            )
-            part = term if part is None else part + term
+    summed = part = None
+    for at, (dr, dc) in enumerate(TAPS):
+        if at == 0:
+            for copy in copies[:EARLY]:
+                copy.wait()
+        if at == EARLY:
+            for copy in copies[EARLY:]:
+                copy.wait()
+        term = jnp.dot(
+            activated[dr * IMG_W : dr * IMG_W + count],
+            two_ref[at],
+            preferred_element_type=jnp.float32,
+        )
+        part = term if part is None else part + term
+        if dr < 2:
+            continue
         if dc == 0:
             part = jnp.where(column == 0, 0.0, pltpu.roll(part, 1, 0))
         if dc == 2:
             part = jnp.where(column == IMG_W - 1, 0.0, pltpu.roll(part, count - 1, 0))
         summed = part if summed is None else summed + part
+        part = None
     out_ref[...] = summed.astype(jnp.bfloat16)
 
 
@@ -389,7 +409,6 @@
     conv_two,
 ):
     tiles = lax.axis_size("rows")
-    place = lax.axis_index("rows")
     rows, width = queries.shape
     channels = code_weight.shape[1]
     share = width // tiles
@@ -400,14 +419,12 @@
     lines = 8
     groups = half // (lines * LANES)
     params = pltpu.CompilerParams(vmem_limit_bytes=VMEM_LIMIT)
-    smem = pl.BlockSpec(memory_space=pltpu.SMEM)
     vmem = pl.BlockSpec(memory_space=pltpu.VMEM)
     anywhere = pl.BlockSpec(memory_space=pl.ANY)
-    parity = (place % 2).reshape(1).astype(jnp.int32)
 
     outgoing, give = pl.pallas_call(
         functools.partial(attend_kernel, tiles=tiles, per=per, feature_rows=feature_rows),
-        in_specs=[smem] * 3 + [anywhere] * 7,
+        in_specs=[anywhere] * 9,
         out_specs=[vmem, vmem],
         out_shape=[
             pltpu.VMEM((tiles, depth, LANES), jnp.bfloat16),
@@ -423,13 +440,14 @@
             pltpu.VMEM((tiles, depth, LANES), jnp.float32),
             pltpu.VMEM((LANES, LANES), jnp.float32),
             pltpu.VMEM((width, LANES), jnp.bfloat16),
-            pltpu.SemaphoreType.DMA((5 + 2 * rows,)),
+            pltpu.SMEM(cache_lengths.shape, cache_lengths.dtype),
+            pltpu.SMEM(tile_slot.shape, tile_slot.dtype),
+            pltpu.SemaphoreType.DMA((7 + 2 * rows,)),
         ],
         compiler_params=pltpu.CompilerParams(vmem_limit_bytes=56 * 1024 * 1024),
     )(
-        cache_lengths,
-        tile_slot,
-        parity,
+        far(cache_lengths),
+        far(tile_slot),
         far(queries),
         far(new_keys),
         far(new_values),
@@ -446,7 +464,7 @@
 
     folded, own = pl.pallas_call(
         fold_kernel,
-        in_specs=[smem, vmem, anywhere, anywhere, anywhere],
+        in_specs=[vmem, anywhere, anywhere, anywhere],
         out_specs=[vmem, vmem],
         out_shape=[
             jax.ShapeDtypeStruct((FOLD_ROWS, channels), jnp.bfloat16),
@@ -460,34 +478,33 @@
             pltpu.SemaphoreType.DMA,
         ],
         compiler_params=params,
-    )(parity, far(code_weight), far(conv_one), far(out_weight), near(outgoing))
+    )(far(code_weight), far(conv_one), far(out_weight), near(outgoing))
 
     partials = pl.pallas_call(
         functools.partial(project_kernel, rows=rows, per=per),
-        in_specs=[smem, vmem, vmem, vmem],
+        in_specs=[vmem, vmem, vmem],
         out_shape=pltpu.VMEM((tiles, groups, rows * lines, LANES), jnp.bfloat16),
         scratch_shapes=[
             pltpu.VMEM((tiles * depth, LANES), jnp.float32),
             pltpu.VMEM((groups, tiles * rows * lines, LANES), jnp.float32),
         ],
         compiler_params=params,
-    )(parity, near(incoming), near(own), near(other))
+    )(near(incoming), near(own), near(other))
     gathered = lax.all_to_all(
         partials, "rows", split_axis=0, concat_axis=0, axis_index_groups=order, tiled=True
     )
 
-    section = (place + IMG_SPLIT // 2) % tiles % IMG_SPLIT
     decoded = pl.pallas_call(
         functools.partial(decode_kernel, feature_rows=feature_rows),
-        in_specs=[smem, vmem, vmem, anywhere, anywhere],
+        in_specs=[vmem, vmem, anywhere, anywhere],
         out_specs=vmem,
         out_shape=jax.ShapeDtypeStruct((TILE_H * IMG_W, channels), jnp.bfloat16),
         scratch_shapes=[
-            pltpu.VMEM(conv_two.shape, conv_two.dtype),
-            pltpu.SemaphoreType.DMA((3, 3)),
+            pltpu.VMEM((len(TAPS),) + conv_two.shape[2:], conv_two.dtype),
+            pltpu.SemaphoreType.DMA((len(TAPS),)),
         ],
         compiler_params=params,
-    )(section.reshape(1).astype(jnp.int32), near(incoming), near(folded), far(conv_two), near(partials))
+    )(near(incoming), near(folded), far(conv_two), near(partials))
 
     mixed = pl.pallas_call(
         functools.partial(total_kernel, rows=rows),

time: 30.2 us -> 28.9 us (0.957)
  Pallas kernels: 15.7 us -> 13.6 us
  waiting for transfers between devices: 0.92 us -> 1.76 us
    pallas_call x1, Pallas kernels: 6.23 us -> 4.8 us  [on_device(): pl.pallas_call(functools.partial(decode_kernel, feature_rows=feature_rows...]
    all_to_all x1, waiting for transfers between devices: 0.01 us -> 0.85 us  [on_device(): lax.all_to_all(partials, 'rows', split_axis=0, concat_axis=0, axis_index_...]
    pallas_call x1, Pallas kernels: 3.95 us -> 3.3 us  [on_device(): pl.pallas_call(functools.partial(attend_kernel, tiles=tiles, per=per, fea...]
  transfers between devices with their start and end apart: 3 -> 3, of which waited for: 1 -> 2; matrix products, arithmetic and copies ran while one was open for 0% -> 0% of each run, Pallas kernels for 33% -> 30%
where the time goes in v6:
time: 28.9 us; the launch traced here: 28.4 us
  Pallas kernels  13.6 us (47%)
  starting transfers between devices  12.4 us (43%)
  waiting for transfers between devices  1.76 us (6%)
  between operations  0.66 us (2%)
    all_to_all x1, starting transfers between devices, on_device(): lax.all_to_all(outgoing, 'rows', split_axis=0, concat_axis=0, axis_index_...  7.52 us
    pallas_call x1, Pallas kernels, on_device(): pl.pallas_call(functools.partial(decode_kernel, feature_rows=feature_rows...  4.8 us
    all_to_all x1, starting transfers between devices, on_device(): lax.all_to_all(partials, 'rows', split_axis=0, concat_axis=0, axis_index_...  4.37 us
    pallas_call x1, Pallas kernels, on_device(): pl.pallas_call(fold_kernel, in_specs=[vmem, anywhere, anywhere, anywhere]...  3.71 us
    pallas_call x1, Pallas kernels, on_device(): pl.pallas_call(functools.partial(attend_kernel, tiles=tiles, per=per, fea...  3.3 us
    pallas_call x1, Pallas kernels, on_device(): pl.pallas_call(functools.partial(project_kernel, rows=rows, per=per), in_...  1.14 us
    all_to_all x1, waiting for transfers between devices, on_device(): lax.all_to_all(outgoing, 'rows', split_axis=0, concat_axis=0, axis_index_...  0.91 us
    all_to_all x1, waiting for transfers between devices, on_device(): lax.all_to_all(partials, 'rows', split_axis=0, concat_axis=0, axis_index_...  0.85 us
  transfers between devices with their start and end apart: 3, of which 2 were waited for; matrix products, arithmetic and copies ran while one was open for 0% of the time, Pallas kernels for 30%

profile of v6, /device:TPU:0, one launch (start us, length us, event | category | flops | bytes accessed | tf_op | source)
XLA Modules:
  0.0 28.4 jit_solution(8366208301166225371)
XLA Ops:
  0.6 3.3 %shard_map.131 = (bf16[16,16,128]{2,1,0:T(8,128)(2,1)}, bf16[256,2048]{1,0:T(8,128)(2,1)S(1)}) custom-call(s32[2]{0:T(128)} %lengths_any.1, s32[2]{0:T(128)} %slots_any.1, bf16[2,4096]{1,0:T(2,128)(2,1)} %q_any.1, bf16[2,4096]{1,0:T(2,128)(2,1)} %nk_any.1, bf16[2,4096]{1,0:T(2,128)(2,1)} %nv_any.1, bf16[2,64,4096]{2,1,0:T(8,128)(2,1)} %k_any.1, ...), custom_call_target="tpu_custom_call" | custom-call | tf_op jit(solution)/shard_map/pallas_call | solution.py:425
  3.9 0.5 %collective-permute-start = (bf16[256,2048]{1,0:T(8,128)(2,1)S(1)}, bf16[256,2048]{1,0:T(8,128)(2,1)S(1)}, u32[]{:S(2)}, u32[]{:S(2)}) collective-permute-start(bf16[256,2048]{1,0:T(8,128)(2,1)S(1)} %get-tuple-element.8), channel_id=1, source_target_pairs={{0,1},{1,0},{2,3},{3,2},{4,5},{5,4},{6,7},{7,6},{8,9},{9,8},{10,11... | collective-permute-start | bytes 3145736 | tf_op jit(solution)/shard_map/ppermute | solution.py:463
  4.5 7.5 %all-to-all-start = ((bf16[16,16,128]{2,1,0:T(8,128)(2,1)}), bf16[16,16,128]{2,1,0:T(8,128)(2,1)S(1)}, u32[]{:S(2)}, u32[]{:S(2)}) async-start(bf16[16,16,128]{2,1,0:T(8,128)(2,1)} %get-tuple-element.6.after_ref), calls=%async_computation | async-start | bytes 131072 | tf_op jit(solution)/shard_map/all_to_all | solution.py:460
  12.0 3.7 %shard_map.132 = (bf16[256,512]{1,0:T(8,128)(2,1)S(1)}, bf16[256,2048]{1,0:T(8,128)(2,1)S(1)}) custom-call(f32[5,512]{1,0:T(8,128)} %cw_ref.1, bf16[3,3,512,512]{3,2,1,0:T(8,128)(2,1)} %conv_ref.1, bf16[256,4096]{1,0:T(8,128)(2,1)} %weight_ref.1, bf16[16,16,128]{2,1,0:T(8,128)(2,1)} %get-tuple-element.6.after_ref), custom_call_target="tpu_custom_call" | custom-call | tf_op jit(solution)/shard_map/pallas_call | solution.py:465
  15.7 0.9 %all-to-all-done.in_ref = bf16[16,16,128]{2,1,0:T(8,128)(2,1)S(1)} async-done(((bf16[16,16,128]{2,1,0:T(8,128)(2,1)}), bf16[16,16,128]{2,1,0:T(8,128)(2,1)S(1)}, u32[]{:S(2)}, u32[]{:S(2)}) %all-to-all-start) | async-done | bytes 65568 | tf_op jit(solution)/shard_map/all_to_all | solution.py:460
  16.6 0.0 collective-permute-done.other_ref
  16.6 1.1 %shard_map.133.after_ref = bf16[16,2,16,128]{3,2,1,0:T(8,128)(2,1)} custom-call(bf16[16,16,128]{2,1,0:T(8,128)(2,1)S(1)} %all-to-all-done.in_ref, bf16[256,2048]{1,0:T(8,128)(2,1)S(1)} %get-tuple-element.7.own_ref, bf16[256,2048]{1,0:T(8,128)(2,1)S(1)} %collective-permute-done.other_ref), custom_call_target="tpu_custom_call" | custom-call | tf_op jit(solution)/shard_map/pallas_call | solution.py:483
  17.7 4.4 %all-to-all-start.1 = ((bf16[16,2,16,128]{3,2,1,0:T(8,128)(2,1)}), bf16[16,2,16,128]{3,2,1,0:T(8,128)(2,1)S(1)}, u32[]{:S(2)}, u32[]{:S(2)}) async-start(bf16[16,2,16,128]{3,2,1,0:T(8,128)(2,1)} %shard_map.133.after_ref), calls=%async_computation.1 | async-start | bytes 262144 | tf_op jit(solution)/shard_map/all_to_all | solution.py:493
  22.1 4.8 %shard_map.135 = bf16[384,512]{1,0:T(8,128)(2,1)} custom-call(bf16[16,16,128]{2,1,0:T(8,128)(2,1)S(1)} %all-to-all-done.in_ref, bf16[256,512]{1,0:T(8,128)(2,1)S(1)} %get-tuple-element.9.fold_ref, bf16[3,3,512,512]{3,2,1,0:T(8,128)(2,1)} %two_any.1, bf16[16,2,16,128]{3,2,1,0:T(8,128)(2,1)} %shard_map.133.after_ref), custom_call_target="tpu_custom_call" | custom-call | tf_op jit(solution)/shard_map/pallas_call | solution.py:497
  26.9 0.8 %all-to-all-done.1.in_ref = bf16[16,2,16,128]{3,2,1,0:T(8,128)(2,1)S(1)} async-done(((bf16[16,2,16,128]{3,2,1,0:T(8,128)(2,1)}), bf16[16,2,16,128]{3,2,1,0:T(8,128)(2,1)S(1)}, u32[]{:S(2)}, u32[]{:S(2)}) %all-to-all-start.1) | async-done | bytes 131104 | tf_op jit(solution)/shard_map/all_to_all | solution.py:493
  27.8 0.6 %shard_map.134 = bf16[2,4096]{1,0:T(2,128)(2,1)} custom-call(bf16[16,2,16,128]{3,2,1,0:T(8,128)(2,1)S(1)} %all-to-all-done.1.in_ref), custom_call_target="tpu_custom_call" | custom-call | tf_op jit(solution)/shard_map/pallas_call | solution.py:509
Async XLA Ops:
  3.9 12.7 %collective-permute-start = (bf16[256,2048]{1,0:T(8,128)(2,1)S(1)}, bf16[256,2048]{1,0:T(8,128)(2,1)S(1)}, u32[]{:S(2)}, u32[]{:S(2)}) collective-permute-start(bf16[256,2048]{1,0:T(8,128)(2,1)S(1)} %get-tuple-element.8), channel_id=1, source_target_pairs={{0,1},{1,0},{2,3},{3,2},{4,5},{5,4},{6,7},{7,6},{8,9},{9,8},{10,11... | collective-permute-start | bytes 3145736 | tf_op jit(solution)/shard_map/ppermute | solution.py:463
  4.5 12.1 %all-to-all-start = ((bf16[16,16,128]{2,1,0:T(8,128)(2,1)}), bf16[16,16,128]{2,1,0:T(8,128)(2,1)S(1)}, u32[]{:S(2)}, u32[]{:S(2)}) async-start(bf16[16,16,128]{2,1,0:T(8,128)(2,1)} %get-tuple-element.6.after_ref), calls=%async_computation | async-start | bytes 131072 | tf_op jit(solution)/shard_map/all_to_all | solution.py:460
  17.7 10.0 %all-to-all-start.1 = ((bf16[16,2,16,128]{3,2,1,0:T(8,128)(2,1)}), bf16[16,2,16,128]{3,2,1,0:T(8,128)(2,1)S(1)}, u32[]{:S(2)}, u32[]{:S(2)}) async-start(bf16[16,2,16,128]{3,2,1,0:T(8,128)(2,1)} %shard_map.133.after_ref), calls=%async_computation.1 | async-start | bytes 262144 | tf_op jit(solution)/shard_map/all_to_all | solution.py:493

commit v7 on v6

--- a/solution.py
+++ b/solution.py
@@ -128,7 +128,34 @@
     msg[...] = jnp.zeros_like(msg)
     for copy in small:
         copy.wait()
-
+    for copy in values:
+        copy.start()
+
+    queries = q_ref[...].astype(jnp.float32)
+    by_head[...] = jnp.zeros_like(by_head)
+    for r in range(rows):
+        for head in range(heads):
+            by_head[r * heads + head : r * heads + head + 1, :] = queries[
+                r : r + 1, head * LANES : (head + 1) * LANES
+            ]
+    turned = by_head[...].T
+    column = lax.broadcasted_iota(jnp.int32, (1, LANES), 1)
+    for head in range(heads):
+        spread[head * LANES : (head + 1) * LANES, :] = jnp.where(
+            column % heads == head, turned, 0.0
+        ).astype(jnp.bfloat16)
+    padding = jnp.zeros((16 - rows, width), jnp.float32)
+    known = rows * cached
+    k_ref[known:, :] = jnp.concatenate([nk_ref[...].astype(jnp.float32), padding], 0).astype(
+        jnp.bfloat16
+    )
+    v_ref[known:, :] = jnp.concatenate([nv_ref[...].astype(jnp.float32), padding], 0).astype(
+        jnp.bfloat16
+    )
+    for copy in keys:
+        copy.wait()
+    products = jnp.dot(k_ref[...], spread[...], preferred_element_type=jnp.float32) * factor
+    give.start()
     words = codes_ref[...]
     blocks = words.shape[1] // LANES
     pieces = [encode(words & 32767), encode(words >> 15)]
@@ -151,31 +178,6 @@
                     place = feature_rows + at * WINDOW + step
                     msg[tile, place : place + 1, :] = total[:, block * LANES : (block + 1) * LANES]
 
-    queries = q_ref[...].astype(jnp.float32)
-    by_head[...] = jnp.zeros_like(by_head)
-    for r in range(rows):
-        for head in range(heads):
-            by_head[r * heads + head : r * heads + head + 1, :] = queries[
-                r : r + 1, head * LANES : (head + 1) * LANES
-            ]
-    turned = by_head[...].T
-    column = lax.broadcasted_iota(jnp.int32, (1, LANES), 1)
-    for head in range(heads):
-        spread[head * LANES : (head + 1) * LANES, :] = jnp.where(
-            column % heads == head, turned, 0.0
-        ).astype(jnp.bfloat16)
-    padding = jnp.zeros((16 - rows, width), jnp.float32)
-    known = rows * cached
-    k_ref[known:, :] = jnp.concatenate([nk_ref[...].astype(jnp.float32), padding], 0).astype(
-        jnp.bfloat16
-    )
-    new_values = jnp.concatenate([nv_ref[...].astype(jnp.float32), padding], 0).astype(jnp.bfloat16)
-    for copy in values:
-        copy.start()
-    for copy in keys:
-        copy.wait()
-    products = jnp.dot(k_ref[...], spread[...], preferred_element_type=jnp.float32) * factor
-    give.start()
     own_scores = products[known:]
     scores = products[:known]
     owner = column // heads
@@ -191,16 +193,15 @@
     cache_exp = jnp.where(live, jnp.exp(scores - highest), 0.0)
     own_exp = jnp.exp(own_score - highest)
     denom = jnp.sum(cache_exp, 0, keepdims=True) + own_exp
-    cache_weight = (cache_exp / denom).T[: rows * heads].astype(jnp.bfloat16)
+    cache_weight = (cache_exp / denom).T[: rows * heads]
     own_weight = jnp.where(own_at, own_exp / denom, 0.0)
     own_weight = jnp.concatenate(
         [own_weight, jnp.zeros((LANES - own_weight.shape[0], LANES), jnp.float32)], 0
-    ).T[: rows * heads, :16].astype(jnp.bfloat16)
+    ).T[: rows * heads, :16]
+    weight = jnp.concatenate([cache_weight, own_weight], 1).astype(jnp.bfloat16)
     for copy in values:
         copy.wait()
-    attended = jnp.dot(cache_weight, v_ref[...], preferred_element_type=jnp.float32) + jnp.dot(
-        own_weight, new_values, preferred_element_type=jnp.float32
-    )
+    attended = jnp.dot(weight, v_ref[...], preferred_element_type=jnp.float32)
     for tile in range(tiles):
         for r in range(rows):
             for step in range(per):
@@ -435,7 +436,7 @@
             pltpu.VMEM(new_keys.shape, new_keys.dtype),
             pltpu.VMEM(new_values.shape, new_values.dtype),
             pltpu.VMEM((rows * cache_keys.shape[1] + 16, width), cache_keys.dtype),
-            pltpu.VMEM((rows * cache_values.shape[1], width), cache_values.dtype),
+            pltpu.VMEM((rows * cache_values.shape[1] + 16, width), cache_values.dtype),
             pltpu.VMEM(codes.shape, codes.dtype),
             pltpu.VMEM((tiles, depth, LANES), jnp.float32),
             pltpu.VMEM((LANES, LANES), jnp.float32),

time: 28.9 us -> 28.9 us (level)
  no operation moved by 1% of the time
where the time goes in v7:
time: 28.9 us; the launch traced here: 28.4 us
  Pallas kernels  13.6 us (47%)
  starting transfers between devices  12.4 us (43%)
  waiting for transfers between devices  1.76 us (6%)
  between operations  0.66 us (2%)
    all_to_all x1, starting transfers between devices, on_device(): lax.all_to_all(outgoing, 'rows', split_axis=0, concat_axis=0, axis_index_...  7.52 us
    pallas_call x1, Pallas kernels, on_device(): pl.pallas_call(functools.partial(decode_kernel, feature_rows=feature_rows...  4.8 us
    all_to_all x1, starting transfers between devices, on_device(): lax.all_to_all(partials, 'rows', split_axis=0, concat_axis=0, axis_index_...  4.37 us
    pallas_call x1, Pallas kernels, on_device(): pl.pallas_call(fold_kernel, in_specs=[vmem, anywhere, anywhere, anywhere]...  3.71 us
    pallas_call x1, Pallas kernels, on_device(): pl.pallas_call(functools.partial(attend_kernel, tiles=tiles, per=per, fea...  3.3 us
    pallas_call x1, Pallas kernels, on_device(): pl.pallas_call(functools.partial(project_kernel, rows=rows, per=per), in_...  1.14 us
    all_to_all x1, waiting for transfers between devices, on_device(): lax.all_to_all(outgoing, 'rows', split_axis=0, concat_axis=0, axis_index_...  0.91 us
    all_to_all x1, waiting for transfers between devices, on_device(): lax.all_to_all(partials, 'rows', split_axis=0, concat_axis=0, axis_index_...  0.85 us
  transfers between devices with their start and end apart: 3, of which 2 were waited for; matrix products, arithmetic and copies ran while one was open for 0% of the time, Pallas kernels for 30%

profile of v7, /device:TPU:0, one launch (start us, length us, event | category | flops | bytes accessed | tf_op | source)
XLA Modules:
  0.0 28.4 jit_solution(9729891752213772041)
XLA Ops:
  0.6 3.3 %shard_map.131 = (bf16[16,16,128]{2,1,0:T(8,128)(2,1)}, bf16[256,2048]{1,0:T(8,128)(2,1)S(1)}) custom-call(s32[2]{0:T(128)} %lengths_any.1, s32[2]{0:T(128)} %slots_any.1, bf16[2,4096]{1,0:T(2,128)(2,1)} %q_any.1, bf16[2,4096]{1,0:T(2,128)(2,1)} %nk_any.1, bf16[2,4096]{1,0:T(2,128)(2,1)} %nv_any.1, bf16[2,64,4096]{2,1,0:T(8,128)(2,1)} %k_any.1, ...), custom_call_target="tpu_custom_call" | custom-call | tf_op jit(solution)/shard_map/pallas_call | solution.py:426
  3.9 0.5 %collective-permute-start = (bf16[256,2048]{1,0:T(8,128)(2,1)S(1)}, bf16[256,2048]{1,0:T(8,128)(2,1)S(1)}, u32[]{:S(2)}, u32[]{:S(2)}) collective-permute-start(bf16[256,2048]{1,0:T(8,128)(2,1)S(1)} %get-tuple-element.8), channel_id=1, source_target_pairs={{0,1},{1,0},{2,3},{3,2},{4,5},{5,4},{6,7},{7,6},{8,9},{9,8},{10,11... | collective-permute-start | bytes 3145736 | tf_op jit(solution)/shard_map/ppermute | solution.py:464
  4.5 7.5 %all-to-all-start = ((bf16[16,16,128]{2,1,0:T(8,128)(2,1)}), bf16[16,16,128]{2,1,0:T(8,128)(2,1)S(1)}, u32[]{:S(2)}, u32[]{:S(2)}) async-start(bf16[16,16,128]{2,1,0:T(8,128)(2,1)} %get-tuple-element.6.after_ref), calls=%async_computation | async-start | bytes 131072 | tf_op jit(solution)/shard_map/all_to_all | solution.py:461
  12.0 3.7 %shard_map.132 = (bf16[256,512]{1,0:T(8,128)(2,1)S(1)}, bf16[256,2048]{1,0:T(8,128)(2,1)S(1)}) custom-call(f32[5,512]{1,0:T(8,128)} %cw_ref.1, bf16[3,3,512,512]{3,2,1,0:T(8,128)(2,1)} %conv_ref.1, bf16[256,4096]{1,0:T(8,128)(2,1)} %weight_ref.1, bf16[16,16,128]{2,1,0:T(8,128)(2,1)} %get-tuple-element.6.after_ref), custom_call_target="tpu_custom_call" | custom-call | tf_op jit(solution)/shard_map/pallas_call | solution.py:466
  15.7 0.9 %all-to-all-done.in_ref = bf16[16,16,128]{2,1,0:T(8,128)(2,1)S(1)} async-done(((bf16[16,16,128]{2,1,0:T(8,128)(2,1)}), bf16[16,16,128]{2,1,0:T(8,128)(2,1)S(1)}, u32[]{:S(2)}, u32[]{:S(2)}) %all-to-all-start) | async-done | bytes 65568 | tf_op jit(solution)/shard_map/all_to_all | solution.py:461
  16.6 0.0 collective-permute-done.other_ref
  16.6 1.1 %shard_map.133.after_ref = bf16[16,2,16,128]{3,2,1,0:T(8,128)(2,1)} custom-call(bf16[16,16,128]{2,1,0:T(8,128)(2,1)S(1)} %all-to-all-done.in_ref, bf16[256,2048]{1,0:T(8,128)(2,1)S(1)} %get-tuple-element.7.own_ref, bf16[256,2048]{1,0:T(8,128)(2,1)S(1)} %collective-permute-done.other_ref), custom_call_target="tpu_custom_call" | custom-call | tf_op jit(solution)/shard_map/pallas_call | solution.py:484
  17.8 4.4 %all-to-all-start.1 = ((bf16[16,2,16,128]{3,2,1,0:T(8,128)(2,1)}), bf16[16,2,16,128]{3,2,1,0:T(8,128)(2,1)S(1)}, u32[]{:S(2)}, u32[]{:S(2)}) async-start(bf16[16,2,16,128]{3,2,1,0:T(8,128)(2,1)} %shard_map.133.after_ref), calls=%async_computation.1 | async-start | bytes 262144 | tf_op jit(solution)/shard_map/all_to_all | solution.py:494
  22.1 4.8 %shard_map.135 = bf16[384,512]{1,0:T(8,128)(2,1)} custom-call(bf16[16,16,128]{2,1,0:T(8,128)(2,1)S(1)} %all-to-all-done.in_ref, bf16[256,512]{1,0:T(8,128)(2,1)S(1)} %get-tuple-element.9.fold_ref, bf16[3,3,512,512]{3,2,1,0:T(8,128)(2,1)} %two_any.1, bf16[16,2,16,128]{3,2,1,0:T(8,128)(2,1)} %shard_map.133.after_ref), custom_call_target="tpu_custom_call" | custom-call | tf_op jit(solution)/shard_map/pallas_call | solution.py:498
  26.9 0.8 %all-to-all-done.1.in_ref = bf16[16,2,16,128]{3,2,1,0:T(8,128)(2,1)S(1)} async-done(((bf16[16,2,16,128]{3,2,1,0:T(8,128)(2,1)}), bf16[16,2,16,128]{3,2,1,0:T(8,128)(2,1)S(1)}, u32[]{:S(2)}, u32[]{:S(2)}) %all-to-all-start.1) | async-done | bytes 131104 | tf_op jit(solution)/shard_map/all_to_all | solution.py:494
  27.8 0.6 %shard_map.134 = bf16[2,4096]{1,0:T(2,128)(2,1)} custom-call(bf16[16,2,16,128]{3,2,1,0:T(8,128)(2,1)S(1)} %all-to-all-done.1.in_ref), custom_call_target="tpu_custom_call" | custom-call | tf_op jit(solution)/shard_map/pallas_call | solution.py:510
Async XLA Ops:
  3.9 12.7 %collective-permute-start = (bf16[256,2048]{1,0:T(8,128)(2,1)S(1)}, bf16[256,2048]{1,0:T(8,128)(2,1)S(1)}, u32[]{:S(2)}, u32[]{:S(2)}) collective-permute-start(bf16[256,2048]{1,0:T(8,128)(2,1)S(1)} %get-tuple-element.8), channel_id=1, source_target_pairs={{0,1},{1,0},{2,3},{3,2},{4,5},{5,4},{6,7},{7,6},{8,9},{9,8},{10,11... | collective-permute-start | bytes 3145736 | tf_op jit(solution)/shard_map/ppermute | solution.py:464
  4.5 12.1 %all-to-all-start = ((bf16[16,16,128]{2,1,0:T(8,128)(2,1)}), bf16[16,16,128]{2,1,0:T(8,128)(2,1)S(1)}, u32[]{:S(2)}, u32[]{:S(2)}) async-start(bf16[16,16,128]{2,1,0:T(8,128)(2,1)} %get-tuple-element.6.after_ref), calls=%async_computation | async-start | bytes 131072 | tf_op jit(solution)/shard_map/all_to_all | solution.py:461
  17.8 10.0 %all-to-all-start.1 = ((bf16[16,2,16,128]{3,2,1,0:T(8,128)(2,1)}), bf16[16,2,16,128]{3,2,1,0:T(8,128)(2,1)S(1)}, u32[]{:S(2)}, u32[]{:S(2)}) async-start(bf16[16,2,16,128]{3,2,1,0:T(8,128)(2,1)} %shard_map.133.after_ref), calls=%async_computation.1 | async-start | bytes 262144 | tf_op jit(solution)/shard_map/all_to_all | solution.py:494

commit v8 on v7

--- a/solution.py
+++ b/solution.py
@@ -118,9 +118,7 @@
     give = pltpu.make_async_copy(
         weight_any.at[:, pl.ds(begin, give_columns)], give_ref, sems.at[6 + 2 * rows]
     )
-    for copy in small:
-        copy.start()
-    for copy in keys:
+    for copy in small + keys + values:
         copy.start()
 
     heads = width // HEAD_DIM
@@ -128,8 +126,6 @@
     msg[...] = jnp.zeros_like(msg)
     for copy in small:
         copy.wait()
-    for copy in values:
-        copy.start()
 
     queries = q_ref[...].astype(jnp.float32)
     by_head[...] = jnp.zeros_like(by_head)
@@ -155,7 +151,6 @@
     for copy in keys:
         copy.wait()
     products = jnp.dot(k_ref[...], spread[...], preferred_element_type=jnp.float32) * factor
-    give.start()
     words = codes_ref[...]
     blocks = words.shape[1] // LANES
     pieces = [encode(words & 32767), encode(words >> 15)]
@@ -201,6 +196,7 @@
     weight = jnp.concatenate([cache_weight, own_weight], 1).astype(jnp.bfloat16)
     for copy in values:
         copy.wait()
+    give.start()
     attended = jnp.dot(weight, v_ref[...], preferred_element_type=jnp.float32)
     for tile in range(tiles):
         for r in range(rows):

time: 28.9 us -> 29.5 us (1.021)
  Pallas kernels: 13.6 us -> 14.1 us
    pallas_call x1, Pallas kernels: 3.3 us -> 3.83 us  [on_device(): pl.pallas_call(functools.partial(attend_kernel, tiles=tiles, per=per, fea...]
  transfers between devices with their start and end apart: 3 -> 3, of which waited for: 2 -> 2; matrix products, arithmetic and copies ran while one was open for 0% -> 0% of each run, Pallas kernels for 30% -> 29%
where the time goes in v8:
time: 29.5 us; the launch traced here: 29 us
  Pallas kernels  14.1 us (48%)
  starting transfers between devices  12.4 us (42%)
  waiting for transfers between devices  1.76 us (6%)
  between operations  0.66 us (2%)
    all_to_all x1, starting transfers between devices, on_device(): lax.all_to_all(outgoing, 'rows', split_axis=0, concat_axis=0, axis_index_...  7.52 us
    pallas_call x1, Pallas kernels, on_device(): pl.pallas_call(functools.partial(decode_kernel, feature_rows=feature_rows...  4.8 us
    all_to_all x1, starting transfers between devices, on_device(): lax.all_to_all(partials, 'rows', split_axis=0, concat_axis=0, axis_index_...  4.37 us
    pallas_call x1, Pallas kernels, on_device(): pl.pallas_call(functools.partial(attend_kernel, tiles=tiles, per=per, fea...  3.83 us
    pallas_call x1, Pallas kernels, on_device(): pl.pallas_call(fold_kernel, in_specs=[vmem, anywhere, anywhere, anywhere]...  3.71 us
    pallas_call x1, Pallas kernels, on_device(): pl.pallas_call(functools.partial(project_kernel, rows=rows, per=per), in_...  1.14 us
    all_to_all x1, waiting for transfers between devices, on_device(): lax.all_to_all(outgoing, 'rows', split_axis=0, concat_axis=0, axis_index_...  0.91 us
    all_to_all x1, waiting for transfers between devices, on_device(): lax.all_to_all(partials, 'rows', split_axis=0, concat_axis=0, axis_index_...  0.85 us
  transfers between devices with their start and end apart: 3, of which 2 were waited for; matrix products, arithmetic and copies ran while one was open for 0% of the time, Pallas kernels for 29%

profile of v8, /device:TPU:0, one launch (start us, length us, event | category | flops | bytes accessed | tf_op | source)
XLA Modules:
  0.0 29.0 jit_solution(11262297257721050476)
XLA Ops:
  0.6 3.8 %shard_map.131 = (bf16[16,16,128]{2,1,0:T(8,128)(2,1)}, bf16[256,2048]{1,0:T(8,128)(2,1)S(1)}) custom-call(s32[2]{0:T(128)} %lengths_any.1, s32[2]{0:T(128)} %slots_any.1, bf16[2,4096]{1,0:T(2,128)(2,1)} %q_any.1, bf16[2,4096]{1,0:T(2,128)(2,1)} %nk_any.1, bf16[2,4096]{1,0:T(2,128)(2,1)} %nv_any.1, bf16[2,64,4096]{2,1,0:T(8,128)(2,1)} %k_any.1, ...), custom_call_target="tpu_custom_call" | custom-call | tf_op jit(solution)/shard_map/pallas_call | solution.py:422
  4.5 0.5 %collective-permute-start = (bf16[256,2048]{1,0:T(8,128)(2,1)S(1)}, bf16[256,2048]{1,0:T(8,128)(2,1)S(1)}, u32[]{:S(2)}, u32[]{:S(2)}) collective-permute-start(bf16[256,2048]{1,0:T(8,128)(2,1)S(1)} %get-tuple-element.8), channel_id=1, source_target_pairs={{0,1},{1,0},{2,3},{3,2},{4,5},{5,4},{6,7},{7,6},{8,9},{9,8},{10,11... | collective-permute-start | bytes 3145736 | tf_op jit(solution)/shard_map/ppermute | solution.py:460
  5.0 7.5 %all-to-all-start = ((bf16[16,16,128]{2,1,0:T(8,128)(2,1)}), bf16[16,16,128]{2,1,0:T(8,128)(2,1)S(1)}, u32[]{:S(2)}, u32[]{:S(2)}) async-start(bf16[16,16,128]{2,1,0:T(8,128)(2,1)} %get-tuple-element.6.after_ref), calls=%async_computation | async-start | bytes 131072 | tf_op jit(solution)/shard_map/all_to_all | solution.py:457
  12.5 3.7 %shard_map.132 = (bf16[256,512]{1,0:T(8,128)(2,1)S(1)}, bf16[256,2048]{1,0:T(8,128)(2,1)S(1)}) custom-call(f32[5,512]{1,0:T(8,128)} %cw_ref.1, bf16[3,3,512,512]{3,2,1,0:T(8,128)(2,1)} %conv_ref.1, bf16[256,4096]{1,0:T(8,128)(2,1)} %weight_ref.1, bf16[16,16,128]{2,1,0:T(8,128)(2,1)} %get-tuple-element.6.after_ref), custom_call_target="tpu_custom_call" | custom-call | tf_op jit(solution)/shard_map/pallas_call | solution.py:462
  16.2 0.9 %all-to-all-done.in_ref = bf16[16,16,128]{2,1,0:T(8,128)(2,1)S(1)} async-done(((bf16[16,16,128]{2,1,0:T(8,128)(2,1)}), bf16[16,16,128]{2,1,0:T(8,128)(2,1)S(1)}, u32[]{:S(2)}, u32[]{:S(2)}) %all-to-all-start) | async-done | bytes 65568 | tf_op jit(solution)/shard_map/all_to_all | solution.py:457
  17.1 0.0 collective-permute-done.other_ref
  17.1 1.1 %shard_map.133.after_ref = bf16[16,2,16,128]{3,2,1,0:T(8,128)(2,1)} custom-call(bf16[16,16,128]{2,1,0:T(8,128)(2,1)S(1)} %all-to-all-done.in_ref, bf16[256,2048]{1,0:T(8,128)(2,1)S(1)} %get-tuple-element.7.own_ref, bf16[256,2048]{1,0:T(8,128)(2,1)S(1)} %collective-permute-done.other_ref), custom_call_target="tpu_custom_call" | custom-call | tf_op jit(solution)/shard_map/pallas_call | solution.py:480
  18.3 4.4 %all-to-all-start.1 = ((bf16[16,2,16,128]{3,2,1,0:T(8,128)(2,1)}), bf16[16,2,16,128]{3,2,1,0:T(8,128)(2,1)S(1)}, u32[]{:S(2)}, u32[]{:S(2)}) async-start(bf16[16,2,16,128]{3,2,1,0:T(8,128)(2,1)} %shard_map.133.after_ref), calls=%async_computation.1 | async-start | bytes 262144 | tf_op jit(solution)/shard_map/all_to_all | solution.py:490
  22.7 4.8 %shard_map.135 = bf16[384,512]{1,0:T(8,128)(2,1)} custom-call(bf16[16,16,128]{2,1,0:T(8,128)(2,1)S(1)} %all-to-all-done.in_ref, bf16[256,512]{1,0:T(8,128)(2,1)S(1)} %get-tuple-element.9.fold_ref, bf16[3,3,512,512]{3,2,1,0:T(8,128)(2,1)} %two_any.1, bf16[16,2,16,128]{3,2,1,0:T(8,128)(2,1)} %shard_map.133.after_ref), custom_call_target="tpu_custom_call" | custom-call | tf_op jit(solution)/shard_map/pallas_call | solution.py:494
  27.5 0.8 %all-to-all-done.1.in_ref = bf16[16,2,16,128]{3,2,1,0:T(8,128)(2,1)S(1)} async-done(((bf16[16,2,16,128]{3,2,1,0:T(8,128)(2,1)}), bf16[16,2,16,128]{3,2,1,0:T(8,128)(2,1)S(1)}, u32[]{:S(2)}, u32[]{:S(2)}) %all-to-all-start.1) | async-done | bytes 131104 | tf_op jit(solution)/shard_map/all_to_all | solution.py:490
  28.3 0.6 %shard_map.134 = bf16[2,4096]{1,0:T(2,128)(2,1)} custom-call(bf16[16,2,16,128]{3,2,1,0:T(8,128)(2,1)S(1)} %all-to-all-done.1.in_ref), custom_call_target="tpu_custom_call" | custom-call | tf_op jit(solution)/shard_map/pallas_call | solution.py:506
Async XLA Ops:
  4.5 12.7 %collective-permute-start = (bf16[256,2048]{1,0:T(8,128)(2,1)S(1)}, bf16[256,2048]{1,0:T(8,128)(2,1)S(1)}, u32[]{:S(2)}, u32[]{:S(2)}) collective-permute-start(bf16[256,2048]{1,0:T(8,128)(2,1)S(1)} %get-tuple-element.8), channel_id=1, source_target_pairs={{0,1},{1,0},{2,3},{3,2},{4,5},{5,4},{6,7},{7,6},{8,9},{9,8},{10,11... | collective-permute-start | bytes 3145736 | tf_op jit(solution)/shard_map/ppermute | solution.py:460
  5.0 12.1 %all-to-all-start = ((bf16[16,16,128]{2,1,0:T(8,128)(2,1)}), bf16[16,16,128]{2,1,0:T(8,128)(2,1)S(1)}, u32[]{:S(2)}, u32[]{:S(2)}) async-start(bf16[16,16,128]{2,1,0:T(8,128)(2,1)} %get-tuple-element.6.after_ref), calls=%async_computation | async-start | bytes 131072 | tf_op jit(solution)/shard_map/all_to_all | solution.py:457
  18.3 10.0 %all-to-all-start.1 = ((bf16[16,2,16,128]{3,2,1,0:T(8,128)(2,1)}), bf16[16,2,16,128]{3,2,1,0:T(8,128)(2,1)S(1)}, u32[]{:S(2)}, u32[]{:S(2)}) async-start(bf16[16,2,16,128]{3,2,1,0:T(8,128)(2,1)} %shard_map.133.after_ref), calls=%async_computation.1 | async-start | bytes 262144 | tf_op jit(solution)/shard_map/all_to_all | solution.py:490

commit v9 on v7

--- a/solution.py
+++ b/solution.py
@@ -69,9 +69,7 @@
     k_any,
     v_any,
     codes_any,
-    weight_any,
     out_ref,
-    give_ref,
     q_ref,
     nk_ref,
     nv_ref,
@@ -90,7 +88,6 @@
     feature_rows,
 ):
     rows, width = q_ref.shape
-    give_columns = give_ref.shape[1]
     small = [
         pltpu.make_async_copy(source, target, sems.at[at])
         for at, (source, target) in enumerate(
@@ -114,10 +111,6 @@
         ]
         for source, target, base in ((k_any, k_ref, 6), (v_any, v_ref, 6 + rows))
     )
-    begin = pl.multiple_of((1 - lax.axis_index("rows") % 2) * give_columns, LANES)
-    give = pltpu.make_async_copy(
-        weight_any.at[:, pl.ds(begin, give_columns)], give_ref, sems.at[6 + 2 * rows]
-    )
     for copy in small:
         copy.start()
     for copy in keys:
@@ -155,7 +148,6 @@
     for copy in keys:
         copy.wait()
     products = jnp.dot(k_ref[...], spread[...], preferred_element_type=jnp.float32) * factor
-    give.start()
     words = codes_ref[...]
     blocks = words.shape[1] // LANES
     pieces = [encode(words & 32767), encode(words >> 15)]
@@ -211,7 +203,6 @@
                     r * heads + head : r * heads + head + 1, head * LANES : (head + 1) * LANES
                 ]
     out_ref[...] = msg[...].astype(jnp.bfloat16)
-    give.wait()
 
 
 def project_kernel(in_ref, own_ref, other_ref, out_ref, held, total, *, rows, per):
@@ -265,7 +256,19 @@
 
 
 def fold_kernel(
-    cw_ref, conv_ref, weight_ref, after_ref, out_ref, near_ref, levels_w, folded, held, sems, near_sem
+    cw_ref,
+    conv_ref,
+    weight_ref,
+    other_ref,
+    after_ref,
+    out_ref,
+    near_ref,
+    near_other_ref,
+    levels_w,
+    folded,
+    held,
+    sems,
+    near_sems,
 ):
     del after_ref
     taps = [(dr, dc) for dr in range(3) for dc in range(3)]
@@ -276,10 +279,13 @@
     for copy in copies:
         copy.start()
     begin = pl.multiple_of(lax.axis_index("rows") % 2 * near_ref.shape[1], LANES)
-    bring = pltpu.make_async_copy(
-        weight_ref.at[:, pl.ds(begin, near_ref.shape[1])], near_ref, near_sem
-    )
-    bring.start()
+    columns = pl.ds(begin, near_ref.shape[1])
+    brings = [
+        pltpu.make_async_copy(source.at[:, columns], target, near_sems.at[at])
+        for at, (source, target) in enumerate(((weight_ref, near_ref), (other_ref, near_other_ref)))
+    ]
+    for bring in brings:
+        bring.start()
     levels_w[...] = jnp.zeros_like(levels_w)
     levels_w[0:FSQ_DIMS, :] = cw_ref[...]
     left = split_three(levels_w[...]).astype(jnp.bfloat16)
@@ -290,7 +296,8 @@
         total = parts[0:8] + parts[8:16] + parts[16:24]
         folded[at * TAP_ROWS : (at + 1) * TAP_ROWS, :] = split_three(total)
     out_ref[...] = folded[...].astype(jnp.bfloat16)
-    bring.wait()
+    for bring in brings:
+        bring.wait()
 
 
 def decode_kernel(
@@ -423,14 +430,11 @@
     vmem = pl.BlockSpec(memory_space=pltpu.VMEM)
     anywhere = pl.BlockSpec(memory_space=pl.ANY)
 
-    outgoing, give = pl.pallas_call(
+    outgoing = pl.pallas_call(
         functools.partial(attend_kernel, tiles=tiles, per=per, feature_rows=feature_rows),
-        in_specs=[anywhere] * 9,
-        out_specs=[vmem, vmem],
-        out_shape=[
-            pltpu.VMEM((tiles, depth, LANES), jnp.bfloat16),
-            pltpu.VMEM((share, half), out_weight.dtype),
-        ],
+        in_specs=[anywhere] * 8,
+        out_specs=vmem,
+        out_shape=jax.ShapeDtypeStruct((tiles, depth, LANES), jnp.bfloat16),
         scratch_shapes=[
             pltpu.VMEM(queries.shape, queries.dtype),
             pltpu.VMEM(new_keys.shape, new_keys.dtype),
@@ -443,7 +447,7 @@
             pltpu.VMEM((width, LANES), jnp.bfloat16),
             pltpu.SMEM(cache_lengths.shape, cache_lengths.dtype),
             pltpu.SMEM(tile_slot.shape, tile_slot.dtype),
-            pltpu.SemaphoreType.DMA((7 + 2 * rows,)),
+            pltpu.SemaphoreType.DMA((6 + 2 * rows,)),
         ],
         compiler_params=pltpu.CompilerParams(vmem_limit_bytes=56 * 1024 * 1024),
     )(
@@ -455,20 +459,20 @@
         far(cache_keys),
         far(cache_values),
         far(codes),
-        far(out_weight),
     )
     order = [[member(at, tiles) for at in range(tiles)]]
     incoming = lax.all_to_all(
         outgoing, "rows", split_axis=0, concat_axis=0, axis_index_groups=order, tiled=True
     )
-    other = lax.ppermute(give, "rows", [(i, i ^ 1) for i in range(tiles)])
-
-    folded, own = pl.pallas_call(
+    other = lax.ppermute(out_weight, "rows", [(i, i ^ 1) for i in range(tiles)])
+
+    folded, own, other = pl.pallas_call(
         fold_kernel,
-        in_specs=[vmem, anywhere, anywhere, anywhere],
-        out_specs=[vmem, vmem],
+        in_specs=[vmem] + [anywhere] * 4,
+        out_specs=[vmem] * 3,
         out_shape=[
             jax.ShapeDtypeStruct((FOLD_ROWS, channels), jnp.bfloat16),
+            pltpu.VMEM((share, half), out_weight.dtype),
             pltpu.VMEM((share, half), out_weight.dtype),
         ],
         scratch_shapes=[
@@ -476,10 +480,10 @@
             pltpu.VMEM((FOLD_ROWS, channels), jnp.float32),
             pltpu.VMEM((9,) + conv_one.shape[2:], conv_one.dtype),
             pltpu.SemaphoreType.DMA((9,)),
-            pltpu.SemaphoreType.DMA,
+            pltpu.SemaphoreType.DMA((2,)),
         ],
         compiler_params=params,
-    )(far(code_weight), far(conv_one), far(out_weight), near(outgoing))
+    )(far(code_weight), far(conv_one), far(out_weight), far(other), far(outgoing))
 
     partials = pl.pallas_call(
         functools.partial(project_kernel, rows=rows, per=per),

time: 28.9 us -> 28.7 us (level)
  transfers between devices with their start and end apart: 3 -> 3, of which waited for: 2 -> 2; matrix products, arithmetic and copies ran while one was open for 0% -> 0% of each run, Pallas kernels for 30% -> 41%
where the time goes in v9:
time: 28.7 us; the launch traced here: 28.2 us
  Pallas kernels  13.5 us (47%)
  starting transfers between devices  12.4 us (43%)
  waiting for transfers between devices  1.68 us (6%)
  between operations  0.66 us (2%)
    all_to_all x1, starting transfers between devices, on_device(): lax.all_to_all(outgoing, 'rows', split_axis=0, concat_axis=0, axis_index_...  7.53 us
    pallas_call x1, Pallas kernels, on_device(): pl.pallas_call(functools.partial(decode_kernel, feature_rows=feature_rows...  4.8 us
    all_to_all x1, starting transfers between devices, on_device(): lax.all_to_all(partials, 'rows', split_axis=0, concat_axis=0, axis_index_...  4.37 us
    pallas_call x1, Pallas kernels, on_device(): pl.pallas_call(fold_kernel, in_specs=[vmem] + [anywhere] * 4, out_specs=[...  3.78 us
    pallas_call x1, Pallas kernels, on_device(): pl.pallas_call(functools.partial(attend_kernel, tiles=tiles, per=per, fea...  3.12 us
    pallas_call x1, Pallas kernels, on_device(): pl.pallas_call(functools.partial(project_kernel, rows=rows, per=per), in_...  1.13 us
    all_to_all x1, waiting for transfers between devices, on_device(): lax.all_to_all(partials, 'rows', split_axis=0, concat_axis=0, axis_index_...  0.85 us
    all_to_all x1, waiting for transfers between devices, on_device(): lax.all_to_all(outgoing, 'rows', split_axis=0, concat_axis=0, axis_index_...  0.83 us
  transfers between devices with their start and end apart: 3, of which 2 were waited for; matrix products, arithmetic and copies ran while one was open for 0% of the time, Pallas kernels for 41%

profile of v9, /device:TPU:0, one launch (start us, length us, event | category | flops | bytes accessed | tf_op | source)
XLA Modules:
  0.0 28.2 jit_solution(2444556308062598669)
XLA Ops:
  0.6 0.5 %collective-permute-start = (bf16[256,4096]{1,0:T(8,128)(2,1)}, bf16[256,4096]{1,0:T(8,128)(2,1)}, u32[]{:S(2)}, u32[]{:S(2)}) collective-permute-start(bf16[256,4096]{1,0:T(8,128)(2,1)} %weight_ref.1), channel_id=1, source_target_pairs={{0,1},{1,0},{2,3},{3,2},{4,5},{5,4},{6,7},{7,6},{8,9},{9,8},{10,11... | collective-permute-start | bytes 6291464 | tf_op jit(solution)/shard_map/ppermute | solution.py:467
  1.2 3.1 %shard_map.131.after_ref = bf16[16,16,128]{2,1,0:T(8,128)(2,1)} custom-call(s32[2]{0:T(128)} %lengths_any.1, s32[2]{0:T(128)} %slots_any.1, bf16[2,4096]{1,0:T(2,128)(2,1)} %q_any.1, bf16[2,4096]{1,0:T(2,128)(2,1)} %nk_any.1, bf16[2,4096]{1,0:T(2,128)(2,1)} %nv_any.1, bf16[2,64,4096]{2,1,0:T(8,128)(2,1)} %k_any.1, bf16[2,64,4096]{2,1,0:T(8,128)(2,1)} %v_any.1, ...), custom_call_target="tpu_custom_call" | custom-call | tf_op jit(solution)/shard_map/pallas_call | solution.py:433
  4.3 7.5 %all-to-all-start = ((bf16[16,16,128]{2,1,0:T(8,128)(2,1)}), bf16[16,16,128]{2,1,0:T(8,128)(2,1)S(1)}, u32[]{:S(2)}, u32[]{:S(2)}) async-start(bf16[16,16,128]{2,1,0:T(8,128)(2,1)} %shard_map.131.after_ref), calls=%async_computation | async-start | bytes 131072 | tf_op jit(solution)/shard_map/all_to_all | solution.py:464
  11.8 0.0 collective-permute-done.other_ref
  11.8 3.8 %shard_map.132 = (bf16[256,512]{1,0:T(8,128)(2,1)S(1)}, bf16[256,2048]{1,0:T(8,128)(2,1)S(1)}, bf16[256,2048]{1,0:T(8,128)(2,1)S(1)}) custom-call(f32[5,512]{1,0:T(8,128)} %cw_ref.1, bf16[3,3,512,512]{3,2,1,0:T(8,128)(2,1)} %conv_ref.1, bf16[256,4096]{1,0:T(8,128)(2,1)} %weight_ref.1, bf16[256,4096]{1,0:T(8,128)(2,1)} %collective-permute-done.other_ref, ...), custom_call_target="tpu_custom_call" | custom-call | tf_op jit(solution)/shard_map/pallas_call | solution.py:469
  15.6 0.8 %all-to-all-done.in_ref = bf16[16,16,128]{2,1,0:T(8,128)(2,1)S(1)} async-done(((bf16[16,16,128]{2,1,0:T(8,128)(2,1)}), bf16[16,16,128]{2,1,0:T(8,128)(2,1)S(1)}, u32[]{:S(2)}, u32[]{:S(2)}) %all-to-all-start) | async-done | bytes 65568 | tf_op jit(solution)/shard_map/all_to_all | solution.py:464
  16.4 1.1 %shard_map.133.after_ref = bf16[16,2,16,128]{3,2,1,0:T(8,128)(2,1)} custom-call(bf16[16,16,128]{2,1,0:T(8,128)(2,1)S(1)} %all-to-all-done.in_ref, bf16[256,2048]{1,0:T(8,128)(2,1)S(1)} %get-tuple-element.5.own_ref, bf16[256,2048]{1,0:T(8,128)(2,1)S(1)} %get-tuple-element.6.other_ref), custom_call_target="tpu_custom_call" | custom-call | tf_op jit(solution)/shard_map/pallas_call | solution.py:488
  17.6 4.4 %all-to-all-start.1 = ((bf16[16,2,16,128]{3,2,1,0:T(8,128)(2,1)}), bf16[16,2,16,128]{3,2,1,0:T(8,128)(2,1)S(1)}, u32[]{:S(2)}, u32[]{:S(2)}) async-start(bf16[16,2,16,128]{3,2,1,0:T(8,128)(2,1)} %shard_map.133.after_ref), calls=%async_computation.1 | async-start | bytes 262144 | tf_op jit(solution)/shard_map/all_to_all | solution.py:498
  21.9 4.8 %shard_map.135 = bf16[384,512]{1,0:T(8,128)(2,1)} custom-call(bf16[16,16,128]{2,1,0:T(8,128)(2,1)S(1)} %all-to-all-done.in_ref, bf16[256,512]{1,0:T(8,128)(2,1)S(1)} %get-tuple-element.7.fold_ref, bf16[3,3,512,512]{3,2,1,0:T(8,128)(2,1)} %two_any.1, bf16[16,2,16,128]{3,2,1,0:T(8,128)(2,1)} %shard_map.133.after_ref), custom_call_target="tpu_custom_call" | custom-call | tf_op jit(solution)/shard_map/pallas_call | solution.py:502
  26.7 0.8 %all-to-all-done.1.in_ref = bf16[16,2,16,128]{3,2,1,0:T(8,128)(2,1)S(1)} async-done(((bf16[16,2,16,128]{3,2,1,0:T(8,128)(2,1)}), bf16[16,2,16,128]{3,2,1,0:T(8,128)(2,1)S(1)}, u32[]{:S(2)}, u32[]{:S(2)}) %all-to-all-start.1) | async-done | bytes 131104 | tf_op jit(solution)/shard_map/all_to_all | solution.py:498
  27.6 0.6 %shard_map.134 = bf16[2,4096]{1,0:T(2,128)(2,1)} custom-call(bf16[16,2,16,128]{3,2,1,0:T(8,128)(2,1)S(1)} %all-to-all-done.1.in_ref), custom_call_target="tpu_custom_call" | custom-call | tf_op jit(solution)/shard_map/pallas_call | solution.py:514
Async XLA Ops:
  0.6 11.2 %collective-permute-start = (bf16[256,4096]{1,0:T(8,128)(2,1)}, bf16[256,4096]{1,0:T(8,128)(2,1)}, u32[]{:S(2)}, u32[]{:S(2)}) collective-permute-start(bf16[256,4096]{1,0:T(8,128)(2,1)} %weight_ref.1), channel_id=1, source_target_pairs={{0,1},{1,0},{2,3},{3,2},{4,5},{5,4},{6,7},{7,6},{8,9},{9,8},{10,11... | collective-permute-start | bytes 6291464 | tf_op jit(solution)/shard_map/ppermute | solution.py:467
  4.3 12.2 %all-to-all-start = ((bf16[16,16,128]{2,1,0:T(8,128)(2,1)}), bf16[16,16,128]{2,1,0:T(8,128)(2,1)S(1)}, u32[]{:S(2)}, u32[]{:S(2)}) async-start(bf16[16,16,128]{2,1,0:T(8,128)(2,1)} %shard_map.131.after_ref), calls=%async_computation | async-start | bytes 131072 | tf_op jit(solution)/shard_map/all_to_all | solution.py:464
  17.6 10.0 %all-to-all-start.1 = ((bf16[16,2,16,128]{3,2,1,0:T(8,128)(2,1)}), bf16[16,2,16,128]{3,2,1,0:T(8,128)(2,1)S(1)}, u32[]{:S(2)}, u32[]{:S(2)}) async-start(bf16[16,2,16,128]{3,2,1,0:T(8,128)(2,1)} %shard_map.133.after_ref), calls=%async_computation.1 | async-start | bytes 262144 | tf_op jit(solution)/shard_map/all_to_all | solution.py:498

commit v10 on v9

--- a/solution.py
+++ b/solution.py
@@ -111,9 +111,7 @@
         ]
         for source, target, base in ((k_any, k_ref, 6), (v_any, v_ref, 6 + rows))
     )
-    for copy in small:
-        copy.start()
-    for copy in keys:
+    for copy in small + keys + values:
         copy.start()
 
     heads = width // HEAD_DIM
@@ -121,8 +119,6 @@
     msg[...] = jnp.zeros_like(msg)
     for copy in small:
         copy.wait()
-    for copy in values:
-        copy.start()
 
     queries = q_ref[...].astype(jnp.float32)
     by_head[...] = jnp.zeros_like(by_head)

time: 28.7 us -> 28.5 us (level)
  no operation moved by 1% of the time
where the time goes in v10:
time: 28.5 us; the launch traced here: 28 us
  Pallas kernels  13.3 us (47%)
  starting transfers between devices  12.4 us (44%)
  waiting for transfers between devices  1.68 us (6%)
  between operations  0.66 us (2%)
    all_to_all x1, starting transfers between devices, on_device(): lax.all_to_all(outgoing, 'rows', split_axis=0, concat_axis=0, axis_index_...  7.53 us
    pallas_call x1, Pallas kernels, on_device(): pl.pallas_call(functools.partial(decode_kernel, feature_rows=feature_rows...  4.8 us
    all_to_all x1, starting transfers between devices, on_device(): lax.all_to_all(partials, 'rows', split_axis=0, concat_axis=0, axis_index_...  4.37 us
    pallas_call x1, Pallas kernels, on_device(): pl.pallas_call(fold_kernel, in_specs=[vmem] + [anywhere] * 4, out_specs=[...  3.78 us
    pallas_call x1, Pallas kernels, on_device(): pl.pallas_call(functools.partial(attend_kernel, tiles=tiles, per=per, fea...  2.92 us
    pallas_call x1, Pallas kernels, on_device(): pl.pallas_call(functools.partial(project_kernel, rows=rows, per=per), in_...  1.13 us
    all_to_all x1, waiting for transfers between devices, on_device(): lax.all_to_all(partials, 'rows', split_axis=0, concat_axis=0, axis_index_...  0.84 us
    all_to_all x1, waiting for transfers between devices, on_device(): lax.all_to_all(outgoing, 'rows', split_axis=0, concat_axis=0, axis_index_...  0.83 us
  transfers between devices with their start and end apart: 3, of which 2 were waited for; matrix products, arithmetic and copies ran while one was open for 0% of the time, Pallas kernels for 41%

profile of v10, /device:TPU:0, one launch (start us, length us, event | category | flops | bytes accessed | tf_op | source)
XLA Modules:
  0.0 28.0 jit_solution(5989841028365861436)
XLA Ops:
  0.6 0.5 %collective-permute-start = (bf16[256,4096]{1,0:T(8,128)(2,1)}, bf16[256,4096]{1,0:T(8,128)(2,1)}, u32[]{:S(2)}, u32[]{:S(2)}) collective-permute-start(bf16[256,4096]{1,0:T(8,128)(2,1)} %weight_ref.1), channel_id=1, source_target_pairs={{0,1},{1,0},{2,3},{3,2},{4,5},{5,4},{6,7},{7,6},{8,9},{9,8},{10,11... | collective-permute-start | bytes 6291464 | tf_op jit(solution)/shard_map/ppermute | solution.py:463
  1.2 2.9 %shard_map.131.after_ref = bf16[16,16,128]{2,1,0:T(8,128)(2,1)} custom-call(s32[2]{0:T(128)} %lengths_any.1, s32[2]{0:T(128)} %slots_any.1, bf16[2,4096]{1,0:T(2,128)(2,1)} %q_any.1, bf16[2,4096]{1,0:T(2,128)(2,1)} %nk_any.1, bf16[2,4096]{1,0:T(2,128)(2,1)} %nv_any.1, bf16[2,64,4096]{2,1,0:T(8,128)(2,1)} %k_any.1, bf16[2,64,4096]{2,1,0:T(8,128)(2,1)} %v_any.1, ...), custom_call_target="tpu_custom_call" | custom-call | tf_op jit(solution)/shard_map/pallas_call | solution.py:429
  4.1 7.5 %all-to-all-start = ((bf16[16,16,128]{2,1,0:T(8,128)(2,1)}), bf16[16,16,128]{2,1,0:T(8,128)(2,1)S(1)}, u32[]{:S(2)}, u32[]{:S(2)}) async-start(bf16[16,16,128]{2,1,0:T(8,128)(2,1)} %shard_map.131.after_ref), calls=%async_computation | async-start | bytes 131072 | tf_op jit(solution)/shard_map/all_to_all | solution.py:460
  11.6 0.0 collective-permute-done.other_ref
  11.6 3.8 %shard_map.132 = (bf16[256,512]{1,0:T(8,128)(2,1)S(1)}, bf16[256,2048]{1,0:T(8,128)(2,1)S(1)}, bf16[256,2048]{1,0:T(8,128)(2,1)S(1)}) custom-call(f32[5,512]{1,0:T(8,128)} %cw_ref.1, bf16[3,3,512,512]{3,2,1,0:T(8,128)(2,1)} %conv_ref.1, bf16[256,4096]{1,0:T(8,128)(2,1)} %weight_ref.1, bf16[256,4096]{1,0:T(8,128)(2,1)} %collective-permute-done.other_ref, ...), custom_call_target="tpu_custom_call" | custom-call | tf_op jit(solution)/shard_map/pallas_call | solution.py:465
  15.4 0.8 %all-to-all-done.in_ref = bf16[16,16,128]{2,1,0:T(8,128)(2,1)S(1)} async-done(((bf16[16,16,128]{2,1,0:T(8,128)(2,1)}), bf16[16,16,128]{2,1,0:T(8,128)(2,1)S(1)}, u32[]{:S(2)}, u32[]{:S(2)}) %all-to-all-start) | async-done | bytes 65568 | tf_op jit(solution)/shard_map/all_to_all | solution.py:460
  16.2 1.1 %shard_map.133.after_ref = bf16[16,2,16,128]{3,2,1,0:T(8,128)(2,1)} custom-call(bf16[16,16,128]{2,1,0:T(8,128)(2,1)S(1)} %all-to-all-done.in_ref, bf16[256,2048]{1,0:T(8,128)(2,1)S(1)} %get-tuple-element.5.own_ref, bf16[256,2048]{1,0:T(8,128)(2,1)S(1)} %get-tuple-element.6.other_ref), custom_call_target="tpu_custom_call" | custom-call | tf_op jit(solution)/shard_map/pallas_call | solution.py:484
  17.4 4.4 %all-to-all-start.1 = ((bf16[16,2,16,128]{3,2,1,0:T(8,128)(2,1)}), bf16[16,2,16,128]{3,2,1,0:T(8,128)(2,1)S(1)}, u32[]{:S(2)}, u32[]{:S(2)}) async-start(bf16[16,2,16,128]{3,2,1,0:T(8,128)(2,1)} %shard_map.133.after_ref), calls=%async_computation.1 | async-start | bytes 262144 | tf_op jit(solution)/shard_map/all_to_all | solution.py:494
  21.7 4.8 %shard_map.135 = bf16[384,512]{1,0:T(8,128)(2,1)} custom-call(bf16[16,16,128]{2,1,0:T(8,128)(2,1)S(1)} %all-to-all-done.in_ref, bf16[256,512]{1,0:T(8,128)(2,1)S(1)} %get-tuple-element.7.fold_ref, bf16[3,3,512,512]{3,2,1,0:T(8,128)(2,1)} %two_any.1, bf16[16,2,16,128]{3,2,1,0:T(8,128)(2,1)} %shard_map.133.after_ref), custom_call_target="tpu_custom_call" | custom-call | tf_op jit(solution)/shard_map/pallas_call | solution.py:498
  26.6 0.8 %all-to-all-done.1.in_ref = bf16[16,2,16,128]{3,2,1,0:T(8,128)(2,1)S(1)} async-done(((bf16[16,2,16,128]{3,2,1,0:T(8,128)(2,1)}), bf16[16,2,16,128]{3,2,1,0:T(8,128)(2,1)S(1)}, u32[]{:S(2)}, u32[]{:S(2)}) %all-to-all-start.1) | async-done | bytes 131104 | tf_op jit(solution)/shard_map/all_to_all | solution.py:494
  27.4 0.6 %shard_map.134 = bf16[2,4096]{1,0:T(2,128)(2,1)} custom-call(bf16[16,2,16,128]{3,2,1,0:T(8,128)(2,1)S(1)} %all-to-all-done.1.in_ref), custom_call_target="tpu_custom_call" | custom-call | tf_op jit(solution)/shard_map/pallas_call | solution.py:510
Async XLA Ops:
  0.6 11.0 %collective-permute-start = (bf16[256,4096]{1,0:T(8,128)(2,1)}, bf16[256,4096]{1,0:T(8,128)(2,1)}, u32[]{:S(2)}, u32[]{:S(2)}) collective-permute-start(bf16[256,4096]{1,0:T(8,128)(2,1)} %weight_ref.1), channel_id=1, source_target_pairs={{0,1},{1,0},{2,3},{3,2},{4,5},{5,4},{6,7},{7,6},{8,9},{9,8},{10,11... | collective-permute-start | bytes 6291464 | tf_op jit(solution)/shard_map/ppermute | solution.py:463
  4.1 12.2 %all-to-all-start = ((bf16[16,16,128]{2,1,0:T(8,128)(2,1)}), bf16[16,16,128]{2,1,0:T(8,128)(2,1)S(1)}, u32[]{:S(2)}, u32[]{:S(2)}) async-start(bf16[16,16,128]{2,1,0:T(8,128)(2,1)} %shard_map.131.after_ref), calls=%async_computation | async-start | bytes 131072 | tf_op jit(solution)/shard_map/all_to_all | solution.py:460
  17.4 10.0 %all-to-all-start.1 = ((bf16[16,2,16,128]{3,2,1,0:T(8,128)(2,1)}), bf16[16,2,16,128]{3,2,1,0:T(8,128)(2,1)S(1)}, u32[]{:S(2)}, u32[]{:S(2)}) async-start(bf16[16,2,16,128]{3,2,1,0:T(8,128)(2,1)} %shard_map.133.after_ref), calls=%async_computation.1 | async-start | bytes 262144 | tf_op jit(solution)/shard_map/all_to_all | solution.py:494

commit v11 on v10

--- a/solution.py
+++ b/solution.py
@@ -201,11 +201,11 @@
     out_ref[...] = msg[...].astype(jnp.bfloat16)
 
 
-def project_kernel(in_ref, own_ref, other_ref, out_ref, held, total, *, rows, per):
+def project_kernel(in_ref, own_ref, other_ref, out_any, held, total, out_ref, sems, *, rows, per):
     tiles, depth = in_ref.shape[:2]
     held[...] = in_ref[...].astype(jnp.float32).reshape(held.shape)
     groups = total.shape[0]
-    lines = out_ref.shape[2] // rows
+    lines = out_any.shape[2] // rows
     share = own_ref.shape[0]
     lhs = []
     for row in range(rows):
@@ -216,20 +216,23 @@
     first, second = lhs[:, :share], lhs[:, share:]
     own = jnp.where(even, first, second).astype(jnp.bfloat16)
     other = jnp.where(even, second, first).astype(jnp.bfloat16)
-    product = jnp.dot(own, own_ref[...], preferred_element_type=jnp.float32) + jnp.dot(
-        other, other_ref[...], preferred_element_type=jnp.float32
-    )
-    for row in range(rows):
-        for group in range(groups):
+    reach = lines * LANES
+    copies = []
+    for group in range(groups):
+        columns = slice(group * reach, (group + 1) * reach)
+        product = jnp.dot(own, own_ref[:, columns], preferred_element_type=jnp.float32) + jnp.dot(
+            other, other_ref[:, columns], preferred_element_type=jnp.float32
+        )
+        for row in range(rows):
             for line in range(lines):
-                begin = (group * lines + line) * LANES
                 total[group, pl.ds(row * lines + line, tiles, stride=rows * lines), :] = product[
-                    row * tiles : (row + 1) * tiles, begin : begin + LANES
+                    row * tiles : (row + 1) * tiles, line * LANES : (line + 1) * LANES
                 ]
-    for group in range(groups):
-        out_ref[:, group] = (
-            total[group].astype(jnp.bfloat16).reshape(tiles, rows * lines, LANES)
-        )
+        out_ref[group] = total[group].astype(jnp.bfloat16).reshape(tiles, rows * lines, LANES)
+        copies.append(pltpu.make_async_copy(out_ref.at[group], out_any.at[:, group], sems.at[group]))
+        copies[-1].start()
+    for copy in copies:
+        copy.wait()
 
 
 def total_kernel(in_ref, out_ref, held, *, rows):
@@ -484,10 +487,13 @@
     partials = pl.pallas_call(
         functools.partial(project_kernel, rows=rows, per=per),
         in_specs=[vmem, vmem, vmem],
-        out_shape=pltpu.VMEM((tiles, groups, rows * lines, LANES), jnp.bfloat16),
+        out_specs=anywhere,
+        out_shape=jax.ShapeDtypeStruct((tiles, groups, rows * lines, LANES), jnp.bfloat16),
         scratch_shapes=[
             pltpu.VMEM((tiles * depth, LANES), jnp.float32),
             pltpu.VMEM((groups, tiles * rows * lines, LANES), jnp.float32),
+            pltpu.VMEM((groups, tiles, rows * lines, LANES), jnp.bfloat16),
+            pltpu.SemaphoreType.DMA((groups,)),
         ],
         compiler_params=params,
     )(near(incoming), near(own), near(other))
@@ -505,7 +511,7 @@
             pltpu.SemaphoreType.DMA((len(TAPS),)),
         ],
         compiler_params=params,
-    )(near(incoming), near(folded), far(conv_two), near(partials))
+    )(near(incoming), near(folded), far(conv_two), far(partials))
 
     mixed = pl.pallas_call(
         functools.partial(total_kernel, rows=rows),

time: 28.5 us -> 28.5 us (level)
  no operation moved by 1% of the time
where the time goes in v11:
time: 28.5 us; the launch traced here: 28.1 us
  Pallas kernels  13.3 us (47%)
  starting transfers between devices  12.4 us (44%)
  waiting for transfers between devices  1.68 us (6%)
  between operations  0.67 us (2%)
    all_to_all x1, starting transfers between devices, on_device(): lax.all_to_all(outgoing, 'rows', split_axis=0, concat_axis=0, axis_index_...  7.53 us
    pallas_call x1, Pallas kernels, on_device(): pl.pallas_call(functools.partial(decode_kernel, feature_rows=feature_rows...  4.8 us
    all_to_all x1, starting transfers between devices, on_device(): lax.all_to_all(partials, 'rows', split_axis=0, concat_axis=0, axis_index_...  4.38 us
    pallas_call x1, Pallas kernels, on_device(): pl.pallas_call(fold_kernel, in_specs=[vmem] + [anywhere] * 4, out_specs=[...  3.78 us
    pallas_call x1, Pallas kernels, on_device(): pl.pallas_call(functools.partial(attend_kernel, tiles=tiles, per=per, fea...  2.92 us
    pallas_call x1, Pallas kernels, on_device(): pl.pallas_call(functools.partial(project_kernel, rows=rows, per=per), in_...  1.14 us
    all_to_all x1, waiting for transfers between devices, on_device(): lax.all_to_all(partials, 'rows', split_axis=0, concat_axis=0, axis_index_...  0.85 us
    all_to_all x1, waiting for transfers between devices, on_device(): lax.all_to_all(outgoing, 'rows', split_axis=0, concat_axis=0, axis_index_...  0.83 us
  transfers between devices with their start and end apart: 3, of which 2 were waited for; matrix products, arithmetic and copies ran while one was open for 0% of the time, Pallas kernels for 41%

profile of v11, /device:TPU:0, one launch (start us, length us, event | category | flops | bytes accessed | tf_op | source)
XLA Modules:
  0.0 28.1 jit_solution(2545770272759097266)
XLA Ops:
  0.6 0.5 %collective-permute-start = (bf16[256,4096]{1,0:T(8,128)(2,1)}, bf16[256,4096]{1,0:T(8,128)(2,1)}, u32[]{:S(2)}, u32[]{:S(2)}) collective-permute-start(bf16[256,4096]{1,0:T(8,128)(2,1)} %weight_ref.1), channel_id=1, source_target_pairs={{0,1},{1,0},{2,3},{3,2},{4,5},{5,4},{6,7},{7,6},{8,9},{9,8},{10,11... | collective-permute-start | bytes 6291464 | tf_op jit(solution)/shard_map/ppermute | solution.py:466
  1.2 2.9 %shard_map.131.after_ref = bf16[16,16,128]{2,1,0:T(8,128)(2,1)} custom-call(s32[2]{0:T(128)} %lengths_any.1, s32[2]{0:T(128)} %slots_any.1, bf16[2,4096]{1,0:T(2,128)(2,1)} %q_any.1, bf16[2,4096]{1,0:T(2,128)(2,1)} %nk_any.1, bf16[2,4096]{1,0:T(2,128)(2,1)} %nv_any.1, bf16[2,64,4096]{2,1,0:T(8,128)(2,1)} %k_any.1, bf16[2,64,4096]{2,1,0:T(8,128)(2,1)} %v_any.1, ...), custom_call_target="tpu_custom_call" | custom-call | tf_op jit(solution)/shard_map/pallas_call | solution.py:432
  4.1 7.5 %all-to-all-start = ((bf16[16,16,128]{2,1,0:T(8,128)(2,1)}), bf16[16,16,128]{2,1,0:T(8,128)(2,1)S(1)}, u32[]{:S(2)}, u32[]{:S(2)}) async-start(bf16[16,16,128]{2,1,0:T(8,128)(2,1)} %shard_map.131.after_ref), calls=%async_computation | async-start | bytes 131072 | tf_op jit(solution)/shard_map/all_to_all | solution.py:463
  11.6 0.0 collective-permute-done.other_ref
  11.6 3.8 %shard_map.132 = (bf16[256,512]{1,0:T(8,128)(2,1)S(1)}, bf16[256,2048]{1,0:T(8,128)(2,1)S(1)}, bf16[256,2048]{1,0:T(8,128)(2,1)S(1)}) custom-call(f32[5,512]{1,0:T(8,128)} %cw_ref.1, bf16[3,3,512,512]{3,2,1,0:T(8,128)(2,1)} %conv_ref.1, bf16[256,4096]{1,0:T(8,128)(2,1)} %weight_ref.1, bf16[256,4096]{1,0:T(8,128)(2,1)} %collective-permute-done.other_ref, ...), custom_call_target="tpu_custom_call" | custom-call | tf_op jit(solution)/shard_map/pallas_call | solution.py:468
  15.4 0.8 %all-to-all-done.in_ref = bf16[16,16,128]{2,1,0:T(8,128)(2,1)S(1)} async-done(((bf16[16,16,128]{2,1,0:T(8,128)(2,1)}), bf16[16,16,128]{2,1,0:T(8,128)(2,1)S(1)}, u32[]{:S(2)}, u32[]{:S(2)}) %all-to-all-start) | async-done | bytes 65568 | tf_op jit(solution)/shard_map/all_to_all | solution.py:463
  16.2 1.1 %shard_map.133.after_ref = bf16[16,2,16,128]{3,2,1,0:T(8,128)(2,1)} custom-call(bf16[16,16,128]{2,1,0:T(8,128)(2,1)S(1)} %all-to-all-done.in_ref, bf16[256,2048]{1,0:T(8,128)(2,1)S(1)} %get-tuple-element.5.own_ref, bf16[256,2048]{1,0:T(8,128)(2,1)S(1)} %get-tuple-element.6.other_ref), custom_call_target="tpu_custom_call" | custom-call | tf_op jit(solution)/shard_map/pallas_call | solution.py:487
  17.4 4.4 %all-to-all-start.1 = ((bf16[16,2,16,128]{3,2,1,0:T(8,128)(2,1)}), bf16[16,2,16,128]{3,2,1,0:T(8,128)(2,1)S(1)}, u32[]{:S(2)}, u32[]{:S(2)}) async-start(bf16[16,2,16,128]{3,2,1,0:T(8,128)(2,1)} %shard_map.133.after_ref), calls=%async_computation.1 | async-start | bytes 262144 | tf_op jit(solution)/shard_map/all_to_all | solution.py:500
  21.8 4.8 %shard_map.135 = bf16[384,512]{1,0:T(8,128)(2,1)} custom-call(bf16[16,16,128]{2,1,0:T(8,128)(2,1)S(1)} %all-to-all-done.in_ref, bf16[256,512]{1,0:T(8,128)(2,1)S(1)} %get-tuple-element.7.fold_ref, bf16[3,3,512,512]{3,2,1,0:T(8,128)(2,1)} %two_any.1, bf16[16,2,16,128]{3,2,1,0:T(8,128)(2,1)} %shard_map.133.after_ref), custom_call_target="tpu_custom_call" | custom-call | tf_op jit(solution)/shard_map/pallas_call | solution.py:504
  26.6 0.8 %all-to-all-done.1.in_ref = bf16[16,2,16,128]{3,2,1,0:T(8,128)(2,1)S(1)} async-done(((bf16[16,2,16,128]{3,2,1,0:T(8,128)(2,1)}), bf16[16,2,16,128]{3,2,1,0:T(8,128)(2,1)S(1)}, u32[]{:S(2)}, u32[]{:S(2)}) %all-to-all-start.1) | async-done | bytes 131104 | tf_op jit(solution)/shard_map/all_to_all | solution.py:500
  27.4 0.6 %shard_map.134 = bf16[2,4096]{1,0:T(2,128)(2,1)} custom-call(bf16[16,2,16,128]{3,2,1,0:T(8,128)(2,1)S(1)} %all-to-all-done.1.in_ref), custom_call_target="tpu_custom_call" | custom-call | tf_op jit(solution)/shard_map/pallas_call | solution.py:516
Async XLA Ops:
  0.6 11.0 %collective-permute-start = (bf16[256,4096]{1,0:T(8,128)(2,1)}, bf16[256,4096]{1,0:T(8,128)(2,1)}, u32[]{:S(2)}, u32[]{:S(2)}) collective-permute-start(bf16[256,4096]{1,0:T(8,128)(2,1)} %weight_ref.1), channel_id=1, source_target_pairs={{0,1},{1,0},{2,3},{3,2},{4,5},{5,4},{6,7},{7,6},{8,9},{9,8},{10,11... | collective-permute-start | bytes 6291464 | tf_op jit(solution)/shard_map/ppermute | solution.py:466
  4.1 12.2 %all-to-all-start = ((bf16[16,16,128]{2,1,0:T(8,128)(2,1)}), bf16[16,16,128]{2,1,0:T(8,128)(2,1)S(1)}, u32[]{:S(2)}, u32[]{:S(2)}) async-start(bf16[16,16,128]{2,1,0:T(8,128)(2,1)} %shard_map.131.after_ref), calls=%async_computation | async-start | bytes 131072 | tf_op jit(solution)/shard_map/all_to_all | solution.py:463
  17.4 10.0 %all-to-all-start.1 = ((bf16[16,2,16,128]{3,2,1,0:T(8,128)(2,1)}), bf16[16,2,16,128]{3,2,1,0:T(8,128)(2,1)S(1)}, u32[]{:S(2)}, u32[]{:S(2)}) async-start(bf16[16,2,16,128]{3,2,1,0:T(8,128)(2,1)} %shard_map.133.after_ref), calls=%async_computation.1 | async-start | bytes 262144 | tf_op jit(solution)/shard_map/all_to_all | solution.py:500

commit v12 on v11

--- a/solution.py
+++ b/solution.py
@@ -141,9 +141,6 @@
     v_ref[known:, :] = jnp.concatenate([nv_ref[...].astype(jnp.float32), padding], 0).astype(
         jnp.bfloat16
     )
-    for copy in keys:
-        copy.wait()
-    products = jnp.dot(k_ref[...], spread[...], preferred_element_type=jnp.float32) * factor
     words = codes_ref[...]
     blocks = words.shape[1] // LANES
     pieces = [encode(words & 32767), encode(words >> 15)]
@@ -166,6 +163,9 @@
                     place = feature_rows + at * WINDOW + step
                     msg[tile, place : place + 1, :] = total[:, block * LANES : (block + 1) * LANES]
 
+    for copy in keys:
+        copy.wait()
+    products = jnp.dot(k_ref[...], spread[...], preferred_element_type=jnp.float32) * factor
     own_scores = products[known:]
     scores = products[:known]
     owner = column // heads

time: 28.5 us -> 28.5 us (level)
  no operation moved by 1% of the time
where the time goes in v12:
time: 28.5 us; the launch traced here: 28 us
  Pallas kernels  13.3 us (47%)
  starting transfers between devices  12.4 us (44%)
  waiting for transfers between devices  1.68 us (6%)
  between operations  0.67 us (2%)
    all_to_all x1, starting transfers between devices, on_device(): lax.all_to_all(outgoing, 'rows', split_axis=0, concat_axis=0, axis_index_...  7.53 us
    pallas_call x1, Pallas kernels, on_device(): pl.pallas_call(functools.partial(decode_kernel, feature_rows=feature_rows...  4.79 us
    all_to_all x1, starting transfers between devices, on_device(): lax.all_to_all(partials, 'rows', split_axis=0, concat_axis=0, axis_index_...  4.38 us
    pallas_call x1, Pallas kernels, on_device(): pl.pallas_call(fold_kernel, in_specs=[vmem] + [anywhere] * 4, out_specs=[...  3.78 us
    pallas_call x1, Pallas kernels, on_device(): pl.pallas_call(functools.partial(attend_kernel, tiles=tiles, per=per, fea...  2.9 us
    pallas_call x1, Pallas kernels, on_device(): pl.pallas_call(functools.partial(project_kernel, rows=rows, per=per), in_...  1.14 us
    all_to_all x1, waiting for transfers between devices, on_device(): lax.all_to_all(partials, 'rows', split_axis=0, concat_axis=0, axis_index_...  0.85 us
    all_to_all x1, waiting for transfers between devices, on_device(): lax.all_to_all(outgoing, 'rows', split_axis=0, concat_axis=0, axis_index_...  0.83 us
  transfers between devices with their start and end apart: 3, of which 2 were waited for; matrix products, arithmetic and copies ran while one was open for 0% of the time, Pallas kernels for 41%

profile of v12, /device:TPU:0, one launch (start us, length us, event | category | flops | bytes accessed | tf_op | source)
XLA Modules:
  0.0 28.0 jit_solution(17676108672827476332)
XLA Ops:
  0.6 0.5 %collective-permute-start = (bf16[256,4096]{1,0:T(8,128)(2,1)}, bf16[256,4096]{1,0:T(8,128)(2,1)}, u32[]{:S(2)}, u32[]{:S(2)}) collective-permute-start(bf16[256,4096]{1,0:T(8,128)(2,1)} %weight_ref.1), channel_id=1, source_target_pairs={{0,1},{1,0},{2,3},{3,2},{4,5},{5,4},{6,7},{7,6},{8,9},{9,8},{10,11... | collective-permute-start | bytes 6291464 | tf_op jit(solution)/shard_map/ppermute | solution.py:466
  1.2 2.9 %shard_map.131.after_ref = bf16[16,16,128]{2,1,0:T(8,128)(2,1)} custom-call(s32[2]{0:T(128)} %lengths_any.1, s32[2]{0:T(128)} %slots_any.1, bf16[2,4096]{1,0:T(2,128)(2,1)} %q_any.1, bf16[2,4096]{1,0:T(2,128)(2,1)} %nk_any.1, bf16[2,4096]{1,0:T(2,128)(2,1)} %nv_any.1, bf16[2,64,4096]{2,1,0:T(8,128)(2,1)} %k_any.1, bf16[2,64,4096]{2,1,0:T(8,128)(2,1)} %v_any.1, ...), custom_call_target="tpu_custom_call" | custom-call | tf_op jit(solution)/shard_map/pallas_call | solution.py:432
  4.1 7.5 %all-to-all-start = ((bf16[16,16,128]{2,1,0:T(8,128)(2,1)}), bf16[16,16,128]{2,1,0:T(8,128)(2,1)S(1)}, u32[]{:S(2)}, u32[]{:S(2)}) async-start(bf16[16,16,128]{2,1,0:T(8,128)(2,1)} %shard_map.131.after_ref), calls=%async_computation | async-start | bytes 131072 | tf_op jit(solution)/shard_map/all_to_all | solution.py:463
  11.6 0.0 collective-permute-done.other_ref
  11.6 3.8 %shard_map.132 = (bf16[256,512]{1,0:T(8,128)(2,1)S(1)}, bf16[256,2048]{1,0:T(8,128)(2,1)S(1)}, bf16[256,2048]{1,0:T(8,128)(2,1)S(1)}) custom-call(f32[5,512]{1,0:T(8,128)} %cw_ref.1, bf16[3,3,512,512]{3,2,1,0:T(8,128)(2,1)} %conv_ref.1, bf16[256,4096]{1,0:T(8,128)(2,1)} %weight_ref.1, bf16[256,4096]{1,0:T(8,128)(2,1)} %collective-permute-done.other_ref, ...), custom_call_target="tpu_custom_call" | custom-call | tf_op jit(solution)/shard_map/pallas_call | solution.py:468
  15.4 0.8 %all-to-all-done.in_ref = bf16[16,16,128]{2,1,0:T(8,128)(2,1)S(1)} async-done(((bf16[16,16,128]{2,1,0:T(8,128)(2,1)}), bf16[16,16,128]{2,1,0:T(8,128)(2,1)S(1)}, u32[]{:S(2)}, u32[]{:S(2)}) %all-to-all-start) | async-done | bytes 65568 | tf_op jit(solution)/shard_map/all_to_all | solution.py:463
  16.2 1.1 %shard_map.133.after_ref = bf16[16,2,16,128]{3,2,1,0:T(8,128)(2,1)} custom-call(bf16[16,16,128]{2,1,0:T(8,128)(2,1)S(1)} %all-to-all-done.in_ref, bf16[256,2048]{1,0:T(8,128)(2,1)S(1)} %get-tuple-element.5.own_ref, bf16[256,2048]{1,0:T(8,128)(2,1)S(1)} %get-tuple-element.6.other_ref), custom_call_target="tpu_custom_call" | custom-call | tf_op jit(solution)/shard_map/pallas_call | solution.py:487
  17.4 4.4 %all-to-all-start.1 = ((bf16[16,2,16,128]{3,2,1,0:T(8,128)(2,1)}), bf16[16,2,16,128]{3,2,1,0:T(8,128)(2,1)S(1)}, u32[]{:S(2)}, u32[]{:S(2)}) async-start(bf16[16,2,16,128]{3,2,1,0:T(8,128)(2,1)} %shard_map.133.after_ref), calls=%async_computation.1 | async-start | bytes 262144 | tf_op jit(solution)/shard_map/all_to_all | solution.py:500
  21.7 4.8 %shard_map.135 = bf16[384,512]{1,0:T(8,128)(2,1)} custom-call(bf16[16,16,128]{2,1,0:T(8,128)(2,1)S(1)} %all-to-all-done.in_ref, bf16[256,512]{1,0:T(8,128)(2,1)S(1)} %get-tuple-element.7.fold_ref, bf16[3,3,512,512]{3,2,1,0:T(8,128)(2,1)} %two_any.1, bf16[16,2,16,128]{3,2,1,0:T(8,128)(2,1)} %shard_map.133.after_ref), custom_call_target="tpu_custom_call" | custom-call | tf_op jit(solution)/shard_map/pallas_call | solution.py:504
  26.5 0.9 %all-to-all-done.1.in_ref = bf16[16,2,16,128]{3,2,1,0:T(8,128)(2,1)S(1)} async-done(((bf16[16,2,16,128]{3,2,1,0:T(8,128)(2,1)}), bf16[16,2,16,128]{3,2,1,0:T(8,128)(2,1)S(1)}, u32[]{:S(2)}, u32[]{:S(2)}) %all-to-all-start.1) | async-done | bytes 131104 | tf_op jit(solution)/shard_map/all_to_all | solution.py:500
  27.4 0.6 %shard_map.134 = bf16[2,4096]{1,0:T(2,128)(2,1)} custom-call(bf16[16,2,16,128]{3,2,1,0:T(8,128)(2,1)S(1)} %all-to-all-done.1.in_ref), custom_call_target="tpu_custom_call" | custom-call | tf_op jit(solution)/shard_map/pallas_call | solution.py:516
Async XLA Ops:
  0.6 11.0 %collective-permute-start = (bf16[256,4096]{1,0:T(8,128)(2,1)}, bf16[256,4096]{1,0:T(8,128)(2,1)}, u32[]{:S(2)}, u32[]{:S(2)}) collective-permute-start(bf16[256,4096]{1,0:T(8,128)(2,1)} %weight_ref.1), channel_id=1, source_target_pairs={{0,1},{1,0},{2,3},{3,2},{4,5},{5,4},{6,7},{7,6},{8,9},{9,8},{10,11... | collective-permute-start | bytes 6291464 | tf_op jit(solution)/shard_map/ppermute | solution.py:466
  4.1 12.2 %all-to-all-start = ((bf16[16,16,128]{2,1,0:T(8,128)(2,1)}), bf16[16,16,128]{2,1,0:T(8,128)(2,1)S(1)}, u32[]{:S(2)}, u32[]{:S(2)}) async-start(bf16[16,16,128]{2,1,0:T(8,128)(2,1)} %shard_map.131.after_ref), calls=%async_computation | async-start | bytes 131072 | tf_op jit(solution)/shard_map/all_to_all | solution.py:463
  17.4 10.0 %all-to-all-start.1 = ((bf16[16,2,16,128]{3,2,1,0:T(8,128)(2,1)}), bf16[16,2,16,128]{3,2,1,0:T(8,128)(2,1)S(1)}, u32[]{:S(2)}, u32[]{:S(2)}) async-start(bf16[16,2,16,128]{3,2,1,0:T(8,128)(2,1)} %shard_map.133.after_ref), calls=%async_computation.1 | async-start | bytes 262144 | tf_op jit(solution)/shard_map/all_to_all | solution.py:500

commit v13 on v11

--- a/solution.py
+++ b/solution.py
@@ -32,7 +32,7 @@
 
 
 def member(at, tiles):
-    return (at + tiles // 4 * 2) % tiles
+    return (at + tiles // 4 * 2 + 2) % tiles
 
 
 def message_rows(features):

time: 28.5 us -> 28.1 us (0.986)
  waiting for transfers between devices: 1.68 us -> 0.01 us
  starting transfers between devices: 12.4 us -> 13.7 us
    all_to_all x1, starting transfers between devices: 4.38 us -> 5.28 us  [on_device(): lax.all_to_all(partials, 'rows', split_axis=0, concat_axis=0, axis_index_...]
    all_to_all x1, waiting for transfers between devices: 0.85 us -> 0.01 us  [on_device(): lax.all_to_all(partials, 'rows', split_axis=0, concat_axis=0, axis_index_...]
    all_to_all x1, waiting for transfers between devices: 0.83 us -> 0.01 us  [on_device(): lax.all_to_all(outgoing, 'rows', split_axis=0, concat_axis=0, axis_index_...]
    all_to_all x1, starting transfers between devices: 7.53 us -> 7.89 us  [on_device(): lax.all_to_all(outgoing, 'rows', split_axis=0, concat_axis=0, axis_index_...]
  transfers between devices with their start and end apart: 3 -> 3, of which waited for: 2 -> 0; matrix products, arithmetic and copies ran while one was open for 0% -> 0% of each run, Pallas kernels for 41% -> 42%
where the time goes in v13:
time: 28.1 us; the launch traced here: 27.7 us
  starting transfers between devices  13.7 us (49%)
  Pallas kernels  13.3 us (47%)
  between operations  0.68 us (2%)
    all_to_all x1, starting transfers between devices, on_device(): lax.all_to_all(outgoing, 'rows', split_axis=0, concat_axis=0, axis_index_...  7.89 us
    all_to_all x1, starting transfers between devices, on_device(): lax.all_to_all(partials, 'rows', split_axis=0, concat_axis=0, axis_index_...  5.28 us
    pallas_call x1, Pallas kernels, on_device(): pl.pallas_call(functools.partial(decode_kernel, feature_rows=feature_rows...  4.8 us
    pallas_call x1, Pallas kernels, on_device(): pl.pallas_call(fold_kernel, in_specs=[vmem] + [anywhere] * 4, out_specs=[...  3.78 us
    pallas_call x1, Pallas kernels, on_device(): pl.pallas_call(functools.partial(attend_kernel, tiles=tiles, per=per, fea...  2.92 us
    pallas_call x1, Pallas kernels, on_device(): pl.pallas_call(functools.partial(project_kernel, rows=rows, per=per), in_...  1.14 us
    pallas_call x1, Pallas kernels, on_device(): pl.pallas_call(functools.partial(total_kernel, rows=rows), in_specs=[vmem...  0.64 us
  transfers between devices with their start and end apart: 3, of which 0 were waited for; matrix products, arithmetic and copies ran while one was open for 0% of the time, Pallas kernels for 42%

profile of v13, /device:TPU:0, one launch (start us, length us, event | category | flops | bytes accessed | tf_op | source)
XLA Modules:
  0.0 27.7 jit_solution(14434425671756674512)
XLA Ops:
  0.6 0.5 %collective-permute-start = (bf16[256,4096]{1,0:T(8,128)(2,1)}, bf16[256,4096]{1,0:T(8,128)(2,1)}, u32[]{:S(2)}, u32[]{:S(2)}) collective-permute-start(bf16[256,4096]{1,0:T(8,128)(2,1)} %weight_ref.1), channel_id=1, source_target_pairs={{0,1},{1,0},{2,3},{3,2},{4,5},{5,4},{6,7},{7,6},{8,9},{9,8},{10,11... | collective-permute-start | bytes 6291464 | tf_op jit(solution)/shard_map/ppermute | solution.py:466
  1.2 2.9 %shard_map.131.after_ref = bf16[16,16,128]{2,1,0:T(8,128)(2,1)} custom-call(s32[2]{0:T(128)} %lengths_any.1, s32[2]{0:T(128)} %slots_any.1, bf16[2,4096]{1,0:T(2,128)(2,1)} %q_any.1, bf16[2,4096]{1,0:T(2,128)(2,1)} %nk_any.1, bf16[2,4096]{1,0:T(2,128)(2,1)} %nv_any.1, bf16[2,64,4096]{2,1,0:T(8,128)(2,1)} %k_any.1, bf16[2,64,4096]{2,1,0:T(8,128)(2,1)} %v_any.1, ...), custom_call_target="tpu_custom_call" | custom-call | tf_op jit(solution)/shard_map/pallas_call | solution.py:432
  4.1 7.9 %all-to-all-start = ((bf16[16,16,128]{2,1,0:T(8,128)(2,1)}), bf16[16,16,128]{2,1,0:T(8,128)(2,1)S(1)}, u32[]{:S(2)}, u32[]{:S(2)}) async-start(bf16[16,16,128]{2,1,0:T(8,128)(2,1)} %shard_map.131.after_ref), calls=%async_computation | async-start | bytes 131072 | tf_op jit(solution)/shard_map/all_to_all | solution.py:463
  12.0 0.0 collective-permute-done.other_ref
  12.0 3.8 %shard_map.132 = (bf16[256,512]{1,0:T(8,128)(2,1)S(1)}, bf16[256,2048]{1,0:T(8,128)(2,1)S(1)}, bf16[256,2048]{1,0:T(8,128)(2,1)S(1)}) custom-call(f32[5,512]{1,0:T(8,128)} %cw_ref.1, bf16[3,3,512,512]{3,2,1,0:T(8,128)(2,1)} %conv_ref.1, bf16[256,4096]{1,0:T(8,128)(2,1)} %weight_ref.1, bf16[256,4096]{1,0:T(8,128)(2,1)} %collective-permute-done.other_ref, ...), custom_call_target="tpu_custom_call" | custom-call | tf_op jit(solution)/shard_map/pallas_call | solution.py:468
  15.8 0.0 all-to-all-done.in_ref
  15.8 1.1 %shard_map.133.after_ref = bf16[16,2,16,128]{3,2,1,0:T(8,128)(2,1)} custom-call(bf16[16,16,128]{2,1,0:T(8,128)(2,1)S(1)} %all-to-all-done.in_ref, bf16[256,2048]{1,0:T(8,128)(2,1)S(1)} %get-tuple-element.5.own_ref, bf16[256,2048]{1,0:T(8,128)(2,1)S(1)} %get-tuple-element.6.other_ref), custom_call_target="tpu_custom_call" | custom-call | tf_op jit(solution)/shard_map/pallas_call | solution.py:487
  16.9 5.3 %all-to-all-start.1 = ((bf16[16,2,16,128]{3,2,1,0:T(8,128)(2,1)}), bf16[16,2,16,128]{3,2,1,0:T(8,128)(2,1)S(1)}, u32[]{:S(2)}, u32[]{:S(2)}) async-start(bf16[16,2,16,128]{3,2,1,0:T(8,128)(2,1)} %shard_map.133.after_ref), calls=%async_computation.1 | async-start | bytes 262144 | tf_op jit(solution)/shard_map/all_to_all | solution.py:500
  22.2 4.8 %shard_map.135 = bf16[384,512]{1,0:T(8,128)(2,1)} custom-call(bf16[16,16,128]{2,1,0:T(8,128)(2,1)S(1)} %all-to-all-done.in_ref, bf16[256,512]{1,0:T(8,128)(2,1)S(1)} %get-tuple-element.7.fold_ref, bf16[3,3,512,512]{3,2,1,0:T(8,128)(2,1)} %two_any.1, bf16[16,2,16,128]{3,2,1,0:T(8,128)(2,1)} %shard_map.133.after_ref), custom_call_target="tpu_custom_call" | custom-call | tf_op jit(solution)/shard_map/pallas_call | solution.py:504
  27.0 0.0 all-to-all-done.1.in_ref
  27.0 0.6 %shard_map.134 = bf16[2,4096]{1,0:T(2,128)(2,1)} custom-call(bf16[16,2,16,128]{3,2,1,0:T(8,128)(2,1)S(1)} %all-to-all-done.1.in_ref), custom_call_target="tpu_custom_call" | custom-call | tf_op jit(solution)/shard_map/pallas_call | solution.py:516
Async XLA Ops:
  0.6 11.3 %collective-permute-start = (bf16[256,4096]{1,0:T(8,128)(2,1)}, bf16[256,4096]{1,0:T(8,128)(2,1)}, u32[]{:S(2)}, u32[]{:S(2)}) collective-permute-start(bf16[256,4096]{1,0:T(8,128)(2,1)} %weight_ref.1), channel_id=1, source_target_pairs={{0,1},{1,0},{2,3},{3,2},{4,5},{5,4},{6,7},{7,6},{8,9},{9,8},{10,11... | collective-permute-start | bytes 6291464 | tf_op jit(solution)/shard_map/ppermute | solution.py:466
  4.1 11.7 %all-to-all-start = ((bf16[16,16,128]{2,1,0:T(8,128)(2,1)}), bf16[16,16,128]{2,1,0:T(8,128)(2,1)S(1)}, u32[]{:S(2)}, u32[]{:S(2)}) async-start(bf16[16,16,128]{2,1,0:T(8,128)(2,1)} %shard_map.131.after_ref), calls=%async_computation | async-start | bytes 131072 | tf_op jit(solution)/shard_map/all_to_all | solution.py:463
  16.9 10.1 %all-to-all-start.1 = ((bf16[16,2,16,128]{3,2,1,0:T(8,128)(2,1)}), bf16[16,2,16,128]{3,2,1,0:T(8,128)(2,1)S(1)}, u32[]{:S(2)}, u32[]{:S(2)}) async-start(bf16[16,2,16,128]{3,2,1,0:T(8,128)(2,1)} %shard_map.133.after_ref), calls=%async_computation.1 | async-start | bytes 262144 | tf_op jit(solution)/shard_map/all_to_all | solution.py:500
